TPU v7x, 32 devices: a whole 2x2x4 slice. The times are simulated.
32 devices in a mesh: blk: 8 (over z, y), shard: 4 (over x, core).
Axes of the slice: x: 2, y: 2, z: 4, core: 2. Of those that a mesh axis runs over, the one named last changes fastest.
Arguments:
- weights: bfloat16 [8, 8192, 2048], P('blk', 'shard'), may hold values from -90 to 90
- warm_factor: float32 [8, 32, 2048], P('blk'), may hold values from -6 to 6
Outputs:
- new_weights: bfloat16 [8, 8192, 2048], P('blk', 'shard')
- new_factor: float32 [8, 32, 2048], P('blk', None, 'shard')
All inputs are finite; a program needn't handle non-finite values.
Results may differ from a plain program's by a relative error of at most 0.012.
Values may be sent and summed in bfloat16 or wider, within the bound.
No kernel may reach another device: no remote copies, remote signals or barrier semaphores. Data moves between devices by JAX's collectives and lax.ppermute only.
A program may use at most 64 MiB of HBM per device.

v0:
```python
import jax
import jax.numpy as jnp
from jax import lax
from jax.sharding import PartitionSpec as P

POWER = 4


MIXING = 1.0 / 3.0


def passed_along(value, axis, by):
    peers = lax.axis_size(axis)
    return lax.ppermute(value, axis, [(i, (i + by) % peers) for i in range(peers)])


def lower_solve(lower_factor, right_hand):
    return jax.scipy.linalg.solve_triangular(lower_factor, right_hand, lower=True)


def on_device(weights, warm_factor):
    local_weight = weights[0]
    own_factor = warm_factor[0]
    own_rounded = own_factor.astype(jnp.bfloat16)
    prior_rounded = passed_along(own_rounded, "blk", 1)
    rounded = jnp.stack([own_rounded, prior_rounded])
    width_piece = local_weight.shape[1] // lax.axis_size("shard")
    own_piece = jnp.stack([own_factor, own_factor])[:, :, :width_piece]
    left_rows = jnp.zeros((2, own_factor.shape[0], local_weight.shape[0]), jnp.bfloat16)
    for iteration in range(POWER):
        products = jnp.einsum(
            "ekc,rc->ekr", rounded, local_weight, preferred_element_type=jnp.float32
        )
        from_next = passed_along(products[1], "blk", -1)
        from_prior = passed_along(products[0], "blk", 1)
        raw_factor = jnp.stack([products[0] - from_next, from_prior - products[1]])
        gram = jnp.einsum("ekr,elr->ekl", raw_factor, raw_factor, precision=lax.Precision.HIGHEST)
        gram = lax.psum(gram, "shard")
        lower_factor = jnp.linalg.cholesky(gram)
        basis = jax.vmap(lower_solve)(lower_factor, raw_factor)
        left_rows = basis.astype(jnp.bfloat16)
        partials = jnp.einsum(
            "ekr,rc->ekc", left_rows, local_weight, preferred_element_type=jnp.float32
        )
        next_part = passed_along(partials[1], "blk", -1)
        prior_part = passed_along(partials[0], "blk", 1)
        factors = lax.psum(jnp.stack([partials[0] - next_part, prior_part - partials[1]]), "shard")
        own_piece = lax.dynamic_slice_in_dim(
            factors, lax.axis_index("shard") * width_piece, width_piece, 2
        )
        rounded = factors.astype(jnp.bfloat16)
    signed = jnp.concatenate([left_rows[1], -left_rows[0]], axis=0)
    factor_pair = jnp.concatenate([rounded[1], rounded[0]], axis=0)
    delta = jnp.einsum("jr,jc->rc", signed, factor_pair, preferred_element_type=jnp.float32)
    new_weight = (local_weight.astype(jnp.float32) + MIXING * delta).astype(jnp.bfloat16)
    return (new_weight[None], own_piece[0][None])


def solution(mesh):
    placed = (P("blk", "shard", None), P("blk", None, None))
    return jax.shard_map(
        on_device,
        mesh=mesh,
        in_specs=placed,
        out_specs=(P("blk", "shard", None), P("blk", None, "shard")),
        check_vma=False,
    )
```

profile of v0, /device:TPU:0, one launch (start us, length us, event | category | flops | bytes accessed | tf_op | source)
XLA Modules:
  0.0 363.7 jit_solution(13797275258302766750)
XLA Ops:
  12.2 5.6 %collective-permute-done = bf16[32,2048]{1,0:T(8,128)(2,1)S(1)} collective-permute-done((bf16[32,2048]{1,0:T(8,128)(2,1)S(1)}, bf16[32,2048]{1,0:T(8,128)(2,1)S(1)}, u32[]{:S(2)}, u32[]{:S(2)}) %collective-permute-start) | collective-permute-done | bytes 131104 | tf_op jit(solution)/shard_map/ppermute | solution.py:14
  17.7 6.0 %fusion.14 = f32[2,32,2048]{2,1,0:T(8,128)S(1)} fusion(bf16[1,2048,2048]{2,1,0:T(8,128)(2,1)} %param.5, bf16[1,32,2048]{2,1,0:T(8,128)(2,1)S(1)} %bitcast.173, bf16[1,32,2048]{2,1,0:T(8,128)(2,1)S(1)} %convert_element_type.38), kind=kOutput, calls=%fused_computation.15 | convolution fusion | flops 537001984 | bytes 9175040 | tf_op jit(solution)/shard_map/ekc,rc->ekr/dot_general | solution.py:31
  25.9 11.1 %collective-permute-done.1 = f32[32,2048]{1,0:T(8,128)S(1)} collective-permute-done((f32[32,2048]{1,0:T(8,128)S(1)}, f32[32,2048]{1,0:T(8,128)S(1)}, u32[]{:S(2)}, u32[]{:S(2)}) %collective-permute-start.1) | collective-permute-done | bytes 262176 | tf_op jit(solution)/shard_map/ppermute | solution.py:14
  37.6 10.3 %psum.56 = f32[2,32,32]{1,2,0:T(8,128)S(1)} all-reduce(f32[2,32,32]{1,2,0:T(8,128)S(1)} %fusion.20), channel_id=1, replica_groups=mesh['blk'=8,'shard'=4] {'shard'}, use_global_device_ids=true, to_apply=%region_0.0 | all-reduce | flops 2048 | bytes 16384 | tf_op jit(solution)/shard_map/psum | solution.py:38
  48.0 5.9 %custom-call.12 = f32[2,32,32]{2,1,0:T(8,128)S(1)} custom-call(f32[2,32,32]{2,1,0:T(8,128)S(1)} %fusion.41), custom_call_target="Cholesky" | custom-call | tf_op jit(solution)/shard_map/jit(cholesky)/cholesky | solution.py:39
  59.6 5.0 %fusion.12 = f32[2,32,2048]{2,1,0:T(8,128)S(1)} fusion(bf16[2,32,2048]{2,1,0:T(8,128)(2,1)S(1)} %convolution_convert_fusion.3, bf16[1,2048,2048]{2,1,0:T(8,128)(2,1)} %param.5), kind=kOutput, calls=%fused_computation.13 | convolution fusion | flops 536870912 | bytes 9175040 | tf_op jit(solution)/shard_map/ekr,rc->ekc/dot_general | solution.py:42
  67.2 11.4 %collective-permute-done.3 = f32[32,2048]{1,0:T(8,128)S(1)} collective-permute-done((f32[32,2048]{1,0:T(8,128)S(1)}, f32[32,2048]{1,0:T(8,128)S(1)}, u32[]{:S(2)}, u32[]{:S(2)}) %collective-permute-start.3) | collective-permute-done | bytes 262176 | tf_op jit(solution)/shard_map/ppermute | solution.py:14
  78.8 16.0 %all-reduce.6 = bf16[2,32,2048]{2,1,0:T(8,128)(2,1)S(1)} all-reduce(f32[2,32,2048]{2,1,0:T(8,128)S(1)} %pad_maximum_fusion.1), channel_id=1, replica_groups=mesh['blk'=8,'shard'=4] {'shard'}, use_global_device_ids=true, to_apply=%region_3.0 | all-reduce | flops 131072 | bytes 786432 | tf_op jit(solution)/shard_map/psum | solution.py:47
  94.7 6.0 %fusion.10 = f32[2,32,2048]{2,1,0:T(8,128)S(1)} fusion(bf16[1,2048,2048]{2,1,0:T(8,128)(2,1)} %param.5, bf16[2,32,2048]{2,1,0:T(8,128)(2,1)S(1)} %all-reduce.6), kind=kOutput, calls=%fused_computation.11 | convolution fusion | flops 536870912 | bytes 9175040 | tf_op jit(solution)/shard_map/ekc,rc->ekr/dot_general | solution.py:31
  103.6 5.8 %collective-permute-done.5 = f32[32,2048]{1,0:T(8,128)S(1)} collective-permute-done((f32[32,2048]{1,0:T(8,128)S(1)}, f32[32,2048]{1,0:T(8,128)S(1)}, u32[]{:S(2)}, u32[]{:S(2)}) %collective-permute-start.5) | collective-permute-done | bytes 262176 | tf_op jit(solution)/shard_map/ppermute | solution.py:14
  114.9 10.3 %psum.58 = f32[2,32,32]{1,2,0:T(8,128)S(1)} all-reduce(f32[2,32,32]{1,2,0:T(8,128)S(1)} %fusion.19), channel_id=1, replica_groups=mesh['blk'=8,'shard'=4] {'shard'}, use_global_device_ids=true, to_apply=%region_4.0 | all-reduce | flops 2048 | bytes 16384 | tf_op jit(solution)/shard_map/psum | solution.py:38
  125.3 5.9 %custom-call.14 = f32[2,32,32]{2,1,0:T(8,128)S(1)} custom-call(f32[2,32,32]{2,1,0:T(8,128)S(1)} %fusion.39), custom_call_target="Cholesky" | custom-call | tf_op jit(solution)/shard_map/jit(cholesky)/cholesky | solution.py:39
  131.4 4.9 %custom-call.15 = f32[2,1,32,32]{2,3,1,0:T(8,128)S(1)} custom-call(f32[2,1,32,32]{3,2,1,0:T(8,128)S(1)} %select_bitcast_fusion.2), custom_call_target="InvertDiagBlocksLowerTriangular" | custom-call | tf_op jit(solution)/shard_map/vmap(jit(_solve_triangular))/triangular_solve | solution.py:18
  136.9 5.0 %fusion.8 = f32[2,32,2048]{2,1,0:T(8,128)S(1)} fusion(bf16[2,32,2048]{2,1,0:T(8,128)(2,1)S(1)} %convolution_convert_fusion.2, bf16[1,2048,2048]{2,1,0:T(8,128)(2,1)} %param.5), kind=kOutput, calls=%fused_computation.9 | convolution fusion | flops 536870912 | bytes 9175040 | tf_op jit(solution)/shard_map/ekr,rc->ekc/dot_general | solution.py:42
  145.5 10.6 %collective-permute-done.7 = f32[32,2048]{1,0:T(8,128)S(1)} collective-permute-done((f32[32,2048]{1,0:T(8,128)S(1)}, f32[32,2048]{1,0:T(8,128)S(1)}, u32[]{:S(2)}, u32[]{:S(2)}) %collective-permute-start.7) | collective-permute-done | bytes 262176 | tf_op jit(solution)/shard_map/ppermute | solution.py:14
  156.3 16.8 %all-reduce.7 = bf16[2,32,2048]{2,1,0:T(8,128)(2,1)S(1)} all-reduce(f32[2,32,2048]{2,1,0:T(8,128)S(1)} %pad_maximum_fusion.3), channel_id=1, replica_groups=mesh['blk'=8,'shard'=4] {'shard'}, use_global_device_ids=true, to_apply=%region_5.0 | all-reduce | flops 131072 | bytes 786432 | tf_op jit(solution)/shard_map/psum | solution.py:47
  173.1 6.0 %fusion.6 = f32[2,32,2048]{2,1,0:T(8,128)S(1)} fusion(bf16[1,2048,2048]{2,1,0:T(8,128)(2,1)} %param.5, bf16[2,32,2048]{2,1,0:T(8,128)(2,1)S(1)} %all-reduce.7), kind=kOutput, calls=%fused_computation.7 | convolution fusion | flops 536870912 | bytes 9175040 | tf_op jit(solution)/shard_map/ekc,rc->ekr/dot_general | solution.py:31
  181.8 11.8 %collective-permute-done.9 = f32[32,2048]{1,0:T(8,128)S(1)} collective-permute-done((f32[32,2048]{1,0:T(8,128)S(1)}, f32[32,2048]{1,0:T(8,128)S(1)}, u32[]{:S(2)}, u32[]{:S(2)}) %collective-permute-start.9) | collective-permute-done | bytes 262176 | tf_op jit(solution)/shard_map/ppermute | solution.py:14
  194.2 10.5 %psum.60 = f32[2,32,32]{1,2,0:T(8,128)S(1)} all-reduce(f32[2,32,32]{1,2,0:T(8,128)S(1)} %fusion.18), channel_id=1, replica_groups=mesh['blk'=8,'shard'=4] {'shard'}, use_global_device_ids=true, to_apply=%region_6.0 | all-reduce | flops 2048 | bytes 16384 | tf_op jit(solution)/shard_map/psum | solution.py:38
  204.8 5.9 %custom-call.16 = f32[2,32,32]{2,1,0:T(8,128)S(1)} custom-call(f32[2,32,32]{2,1,0:T(8,128)S(1)} %fusion.37), custom_call_target="Cholesky" | custom-call | tf_op jit(solution)/shard_map/jit(cholesky)/cholesky | solution.py:39
  210.9 4.9 %custom-call.17 = f32[2,1,32,32]{2,3,1,0:T(8,128)S(1)} custom-call(f32[2,1,32,32]{3,2,1,0:T(8,128)S(1)} %select_bitcast_fusion.1), custom_call_target="InvertDiagBlocksLowerTriangular" | custom-call | tf_op jit(solution)/shard_map/vmap(jit(_solve_triangular))/triangular_solve | solution.py:18
  216.5 5.0 %fusion.4 = f32[2,32,2048]{2,1,0:T(8,128)S(1)} fusion(bf16[2,32,2048]{2,1,0:T(8,128)(2,1)S(1)} %convolution_convert_fusion.1, bf16[1,2048,2048]{2,1,0:T(8,128)(2,1)} %param.5), kind=kOutput, calls=%fused_computation.5 | convolution fusion | flops 536870912 | bytes 9175040 | tf_op jit(solution)/shard_map/ekr,rc->ekc/dot_general | solution.py:42
  223.6 11.3 %collective-permute-done.11 = f32[32,2048]{1,0:T(8,128)S(1)} collective-permute-done((f32[32,2048]{1,0:T(8,128)S(1)}, f32[32,2048]{1,0:T(8,128)S(1)}, u32[]{:S(2)}, u32[]{:S(2)}) %collective-permute-start.11) | collective-permute-done | bytes 262176 | tf_op jit(solution)/shard_map/ppermute | solution.py:14
  235.0 15.9 %all-reduce.8 = bf16[2,32,2048]{2,1,0:T(8,128)(2,1)S(1)} all-reduce(f32[2,32,2048]{2,1,0:T(8,128)S(1)} %pad_maximum_fusion.5), channel_id=1, replica_groups=mesh['blk'=8,'shard'=4] {'shard'}, use_global_device_ids=true, to_apply=%region_7.0 | all-reduce | flops 131072 | bytes 786432 | tf_op jit(solution)/shard_map/psum | solution.py:47
  250.9 6.0 %fusion.2 = f32[2,32,2048]{2,1,0:T(8,128)S(1)} fusion(bf16[1,2048,2048]{2,1,0:T(8,128)(2,1)} %param.5, bf16[2,32,2048]{2,1,0:T(8,128)(2,1)S(1)} %all-reduce.8), kind=kOutput, calls=%fused_computation.3 | convolution fusion | flops 536870912 | bytes 9175040 | tf_op jit(solution)/shard_map/ekc,rc->ekr/dot_general | solution.py:31
  260.0 11.2 %collective-permute-done.13 = f32[32,2048]{1,0:T(8,128)S(1)} collective-permute-done((f32[32,2048]{1,0:T(8,128)S(1)}, f32[32,2048]{1,0:T(8,128)S(1)}, u32[]{:S(2)}, u32[]{:S(2)}) %collective-permute-start.13) | collective-permute-done | bytes 262176 | tf_op jit(solution)/shard_map/ppermute | solution.py:14
  271.8 10.8 %psum.62 = f32[2,32,32]{1,2,0:T(8,128)S(1)} all-reduce(f32[2,32,32]{1,2,0:T(8,128)S(1)} %fusion.17), channel_id=1, replica_groups=mesh['blk'=8,'shard'=4] {'shard'}, use_global_device_ids=true, to_apply=%region_8.11 | all-reduce | flops 2048 | bytes 16384 | tf_op jit(solution)/shard_map/psum | solution.py:38
  282.7 5.9 %custom-call.18 = f32[2,32,32]{2,1,0:T(8,128)S(1)} custom-call(f32[2,32,32]{2,1,0:T(8,128)S(1)} %fusion.35), custom_call_target="Cholesky" | custom-call | tf_op jit(solution)/shard_map/jit(cholesky)/cholesky | solution.py:39
  294.4 4.9 %fusion = f32[2,32,2048]{2,1,0:T(8,128)S(1)} fusion(bf16[2,32,2048]{2,1,0:T(8,128)(2,1)S(1)} %convolution_convert_fusion, bf16[1,2048,2048]{2,1,0:T(8,128)(2,1)} %param.5), kind=kOutput, calls=%fused_computation.1 | convolution fusion | flops 536870912 | bytes 9175040 | tf_op jit(solution)/shard_map/ekr,rc->ekc/dot_general | solution.py:42
  302.9 10.7 %collective-permute-done.15 = f32[32,2048]{1,0:T(8,128)S(1)} collective-permute-done((f32[32,2048]{1,0:T(8,128)S(1)}, f32[32,2048]{1,0:T(8,128)S(1)}, u32[]{:S(2)}, u32[]{:S(2)}) %collective-permute-start.15) | collective-permute-done | bytes 262176 | tf_op jit(solution)/shard_map/ppermute | solution.py:14
  314.6 32.8 %all-reduce.5.cloned.1.call-done = f32[2,32,2048]{2,1,0:T(8,128)} async-done(((f32[2,32,2048]{2,1,0:T(8,128)}), f32[2,32,2048]{2,1,0:T(8,128)}) %all-reduce.5.cloned.1.call-update) | async-done | bytes 524304 | tf_op jit(solution)/shard_map/psum | solution.py:47
  348.5 6.9 %fusion.16 = bf16[1,2048,2048]{2,1,0:T(8,128)(2,1)} fusion(bf16[1,2048,2048]{2,1,0:T(8,128)(2,1)} %param.5, bf16[32,2048]{1,0:T(8,128)(2,1)S(1)} %get-tuple-element.39, bf16[32,2048]{1,0:T(8,128)(2,1)S(1)} %get-tuple-element.38, bf16[32,2048]{1,0:T(8,128)(2,1)S(1)} %get-tuple-element.37, bf16[32,2048]{1,0:T(8,128)(2,1)S(1)} %get-tuple-element.36), kind=kOutput, calls=%fused_computation.17 | convolution fusion | flops 554696704 | bytes 17301504 | tf_op jit(solution)/shard_map/jr,jc->rc/dot_general | solution.py:54
  (85 shorter events, 52.6 us)
Async XLA Ops:
  7.2 340.2 %all-reduce.5.cloned.1.call-start = ((), (), s32[]{:S(2)}) async-start(), calls=%async_computation | async-start | bytes 1048576 | tf_op jit(solution)/shard_map/psum | solution.py:47
  8.2 9.6 %collective-permute-start = (bf16[32,2048]{1,0:T(8,128)(2,1)S(1)}, bf16[32,2048]{1,0:T(8,128)(2,1)S(1)}, u32[]{:S(2)}, u32[]{:S(2)}) collective-permute-start(bf16[32,2048]{1,0:T(8,128)(2,1)S(1)} %convert_bitcast_fusion), channel_id=1, source_target_pairs={{0,4},{4,8},{8,12},{12,16},{16,20},{20,24},{24,28},{28,0},{1,5},{5... | collective-permute-start | bytes 393224 | tf_op jit(solution)/shard_map/ppermute | solution.py:14
  23.8 13.2 %collective-permute-start.1 = (f32[32,2048]{1,0:T(8,128)S(1)}, f32[32,2048]{1,0:T(8,128)S(1)}, u32[]{:S(2)}, u32[]{:S(2)}) collective-permute-start(f32[32,2048]{1,0:T(8,128)S(1)} %get-tuple-element.34), channel_id=1, source_target_pairs={{0,28},{4,0},{8,4},{12,8},{16,12},{20,16},{24,20},{28,24},{1,29},{... | collective-permute-start | bytes 786440 | tf_op jit(solution)/shard_map/ppermute | solution.py:14
  25.6 11.4 %collective-permute-start.2 = (f32[32,2048]{1,0:T(8,128)S(1)}, f32[32,2048]{1,0:T(8,128)S(1)}, u32[]{:S(2)}, u32[]{:S(2)}) collective-permute-start(f32[32,2048]{1,0:T(8,128)S(1)} %get-tuple-element.35), channel_id=1, source_target_pairs={{0,4},{4,8},{8,12},{12,16},{16,20},{20,24},{24,28},{28,0},{1,5},{5... | collective-permute-start | bytes 786440 | tf_op jit(solution)/shard_map/ppermute | solution.py:14
  64.6 14.0 %collective-permute-start.3 = (f32[32,2048]{1,0:T(8,128)S(1)}, f32[32,2048]{1,0:T(8,128)S(1)}, u32[]{:S(2)}, u32[]{:S(2)}) collective-permute-start(f32[32,2048]{1,0:T(8,128)S(1)} %get-tuple-element.30), channel_id=1, source_target_pairs={{0,28},{4,0},{8,4},{12,8},{16,12},{20,16},{24,20},{28,24},{1,29},{... | collective-permute-start | bytes 786440 | tf_op jit(solution)/shard_map/ppermute | solution.py:14
  67.2 11.4 %collective-permute-start.4 = (f32[32,2048]{1,0:T(8,128)S(1)}, f32[32,2048]{1,0:T(8,128)S(1)}, u32[]{:S(2)}, u32[]{:S(2)}) collective-permute-start(f32[32,2048]{1,0:T(8,128)S(1)} %get-tuple-element.31), channel_id=1, source_target_pairs={{0,4},{4,8},{8,12},{12,16},{16,20},{20,24},{24,28},{28,0},{1,5},{5... | collective-permute-start | bytes 786440 | tf_op jit(solution)/shard_map/ppermute | solution.py:14
  100.8 8.6 %collective-permute-start.5 = (f32[32,2048]{1,0:T(8,128)S(1)}, f32[32,2048]{1,0:T(8,128)S(1)}, u32[]{:S(2)}, u32[]{:S(2)}) collective-permute-start(f32[32,2048]{1,0:T(8,128)S(1)} %get-tuple-element.26), channel_id=1, source_target_pairs={{0,28},{4,0},{8,4},{12,8},{16,12},{20,16},{24,20},{28,24},{1,29},{... | collective-permute-start | bytes 786440 | tf_op jit(solution)/shard_map/ppermute | solution.py:14
  103.6 10.7 %collective-permute-start.6 = (f32[32,2048]{1,0:T(8,128)S(1)}, f32[32,2048]{1,0:T(8,128)S(1)}, u32[]{:S(2)}, u32[]{:S(2)}) collective-permute-start(f32[32,2048]{1,0:T(8,128)S(1)} %get-tuple-element.27), channel_id=1, source_target_pairs={{0,4},{4,8},{8,12},{12,16},{16,20},{20,24},{24,28},{28,0},{1,5},{5... | collective-permute-start | bytes 786440 | tf_op jit(solution)/shard_map/ppermute | solution.py:14
  142.0 14.1 %collective-permute-start.7 = (f32[32,2048]{1,0:T(8,128)S(1)}, f32[32,2048]{1,0:T(8,128)S(1)}, u32[]{:S(2)}, u32[]{:S(2)}) collective-permute-start(f32[32,2048]{1,0:T(8,128)S(1)} %get-tuple-element.22), channel_id=1, source_target_pairs={{0,28},{4,0},{8,4},{12,8},{16,12},{20,16},{24,20},{28,24},{1,29},{... | collective-permute-start | bytes 786440 | tf_op jit(solution)/shard_map/ppermute | solution.py:14
  145.5 10.7 %collective-permute-start.8 = (f32[32,2048]{1,0:T(8,128)S(1)}, f32[32,2048]{1,0:T(8,128)S(1)}, u32[]{:S(2)}, u32[]{:S(2)}) collective-permute-start(f32[32,2048]{1,0:T(8,128)S(1)} %get-tuple-element.23), channel_id=1, source_target_pairs={{0,4},{4,8},{8,12},{12,16},{16,20},{20,24},{24,28},{28,0},{1,5},{5... | collective-permute-start | bytes 786440 | tf_op jit(solution)/shard_map/ppermute | solution.py:14
  179.2 14.4 %collective-permute-start.9 = (f32[32,2048]{1,0:T(8,128)S(1)}, f32[32,2048]{1,0:T(8,128)S(1)}, u32[]{:S(2)}, u32[]{:S(2)}) collective-permute-start(f32[32,2048]{1,0:T(8,128)S(1)} %get-tuple-element.18), channel_id=1, source_target_pairs={{0,28},{4,0},{8,4},{12,8},{16,12},{20,16},{24,20},{28,24},{1,29},{... | collective-permute-start | bytes 786440 | tf_op jit(solution)/shard_map/ppermute | solution.py:14
  181.7 11.9 %collective-permute-start.10 = (f32[32,2048]{1,0:T(8,128)S(1)}, f32[32,2048]{1,0:T(8,128)S(1)}, u32[]{:S(2)}, u32[]{:S(2)}) collective-permute-start(f32[32,2048]{1,0:T(8,128)S(1)} %get-tuple-element.19), channel_id=1, source_target_pairs={{0,4},{4,8},{8,12},{12,16},{16,20},{20,24},{24,28},{28,0},{1,5},{5... | collective-permute-start | bytes 786440 | tf_op jit(solution)/shard_map/ppermute | solution.py:14
  221.5 13.4 %collective-permute-start.11 = (f32[32,2048]{1,0:T(8,128)S(1)}, f32[32,2048]{1,0:T(8,128)S(1)}, u32[]{:S(2)}, u32[]{:S(2)}) collective-permute-start(f32[32,2048]{1,0:T(8,128)S(1)} %get-tuple-element.14), channel_id=1, source_target_pairs={{0,28},{4,0},{8,4},{12,8},{16,12},{20,16},{24,20},{28,24},{1,29},{... | collective-permute-start | bytes 786440 | tf_op jit(solution)/shard_map/ppermute | solution.py:14
  223.2 11.7 %collective-permute-start.12 = (f32[32,2048]{1,0:T(8,128)S(1)}, f32[32,2048]{1,0:T(8,128)S(1)}, u32[]{:S(2)}, u32[]{:S(2)}) collective-permute-start(f32[32,2048]{1,0:T(8,128)S(1)} %get-tuple-element.15), channel_id=1, source_target_pairs={{0,4},{4,8},{8,12},{12,16},{16,20},{20,24},{24,28},{28,0},{1,5},{5... | collective-permute-start | bytes 786440 | tf_op jit(solution)/shard_map/ppermute | solution.py:14
  257.0 14.2 %collective-permute-start.13 = (f32[32,2048]{1,0:T(8,128)S(1)}, f32[32,2048]{1,0:T(8,128)S(1)}, u32[]{:S(2)}, u32[]{:S(2)}) collective-permute-start(f32[32,2048]{1,0:T(8,128)S(1)} %get-tuple-element.10), channel_id=1, source_target_pairs={{0,28},{4,0},{8,4},{12,8},{16,12},{20,16},{24,20},{28,24},{1,29},{... | collective-permute-start | bytes 786440 | tf_op jit(solution)/shard_map/ppermute | solution.py:14
  260.0 11.2 %collective-permute-start.14 = (f32[32,2048]{1,0:T(8,128)S(1)}, f32[32,2048]{1,0:T(8,128)S(1)}, u32[]{:S(2)}, u32[]{:S(2)}) collective-permute-start(f32[32,2048]{1,0:T(8,128)S(1)} %get-tuple-element.11), channel_id=1, source_target_pairs={{0,4},{4,8},{8,12},{12,16},{16,20},{20,24},{24,28},{28,0},{1,5},{5... | collective-permute-start | bytes 786440 | tf_op jit(solution)/shard_map/ppermute | solution.py:14
  299.4 14.1 %collective-permute-start.15 = (f32[32,2048]{1,0:T(8,128)S(1)}, f32[32,2048]{1,0:T(8,128)S(1)}, u32[]{:S(2)}, u32[]{:S(2)}) collective-permute-start(f32[32,2048]{1,0:T(8,128)S(1)} %get-tuple-element.6), channel_id=1, source_target_pairs={{0,28},{4,0},{8,4},{12,8},{16,12},{20,16},{24,20},{28,24},{1,29},{... | collective-permute-start | bytes 786440 | tf_op jit(solution)/shard_map/ppermute | solution.py:14
  302.9 10.8 %collective-permute-start.16 = (f32[32,2048]{1,0:T(8,128)S(1)}, f32[32,2048]{1,0:T(8,128)S(1)}, u32[]{:S(2)}, u32[]{:S(2)}) collective-permute-start(f32[32,2048]{1,0:T(8,128)S(1)} %get-tuple-element.7), channel_id=1, source_target_pairs={{0,4},{4,8},{8,12},{12,16},{16,20},{20,24},{24,28},{28,0},{1,5},{5... | collective-permute-start | bytes 786440 | tf_op jit(solution)/shard_map/ppermute | solution.py:14
Sparse Core Ops, SparseCore 0:
  314.7 32.6 all-reduce.4
where the time goes:
time: 364 us
  waiting for transfers between devices  127 us (35%)
  blocking collectives  90.5 us (25%)
  matrix products  55.7 us (15%)
  other arithmetic  48.5 us (13%)
  starting transfers between devices  25.1 us (7%)
  between operations  14.3 us (4%)
    ppermute x17, waiting for transfers between devices, passed_along(): lax.ppermute(value, axis, [(i, (i + by) % peers) for i in range(peers)])  94.6 us
    psum x3, blocking collectives, on_device(): lax.psum(jnp.stack([partials[0] - next_part, prior_part - partials[1]]),...  48.7 us
    psum x4, blocking collectives, on_device(): gram = lax.psum(gram, 'shard')  41.9 us
    psum x1, waiting for transfers between devices, on_device(): lax.psum(jnp.stack([partials[0] - next_part, prior_part - partials[1]]),...  32.8 us
    ppermute x17, starting transfers between devices, passed_along(): lax.ppermute(value, axis, [(i, (i + by) % peers) for i in range(peers)])  25.1 us
    dot_general x4, matrix products, on_device(): jnp.einsum('ekc,rc->ekr', rounded, local_weight, preferred_element_type=j...  24.1 us
    another operation x13, other arithmetic, on_device(): lower_factor = jnp.linalg.cholesky(gram)  24.1 us
    another operation x9, other arithmetic, lower_solve(): jax.scipy.linalg.solve_triangular(lower_factor, right_hand, lower=True)  20 us
  transfers between devices with their start and end apart: 18, of which 13 were waited for; matrix products, arithmetic and copies ran while one was open for 0% of the time, Pallas kernels for 0%

commit v1 on v0

v1 whole, which is shorter than its diff:
```python
import functools

import jax
import jax.numpy as jnp
from jax import lax
from jax.experimental import pallas as pl
from jax.experimental.pallas import tpu as pltpu
from jax.sharding import PartitionSpec as P

POWER = 4
MIXING = 1.0 / 3.0
LANES = 128
F32 = jnp.float32
BF16 = jnp.bfloat16
HIGHEST = lax.Precision.HIGHEST
VMEM = pl.BlockSpec(memory_space=pltpu.VMEM)
SMEM = pl.BlockSpec(memory_space=pltpu.SMEM)
HBM = pl.BlockSpec(memory_space=pl.ANY)


def kernel_call(body, outs, name, *operands, scratch=(), mib=8, flops=0, moved=0):
    specs = []
    for operand in operands:
        specs.append(SMEM if operand.dtype == jnp.int32 else VMEM)
    return pl.pallas_call(
        body,
        out_shape=outs,
        in_specs=specs,
        out_specs=jax.tree.map(lambda _: VMEM, outs),
        scratch_shapes=list(scratch),
        compiler_params=pltpu.CompilerParams(vmem_limit_bytes=mib * 1024 * 1024),
        cost_estimate=pl.CostEstimate(flops=flops, bytes_accessed=moved, transcendentals=0),
        name=name,
    )(*operands)


def out(shape, dtype):
    return jax.ShapeDtypeStruct(shape, dtype)


def hold_kernel(source, held, sem):
    copy = pltpu.make_async_copy(source, held, sem)
    copy.start()
    copy.wait()


def hold(weight):
    return pl.pallas_call(
        hold_kernel,
        out_shape=pltpu.VMEM(weight.shape, weight.dtype),
        in_specs=[HBM],
        out_specs=VMEM,
        scratch_shapes=[pltpu.SemaphoreType.DMA],
        compiler_params=pltpu.CompilerParams(vmem_limit_bytes=1024 * 1024),
        name="hold",
    )(weight)


def project(factor, weight, even, odd):
    rank = even.shape[0]
    product = lax.dot_general(
        factor, weight[...], (((1,), (1,)), ((), ())), preferred_element_type=F32
    )
    even[...] = product[:rank]
    odd[...] = product[rank:]


def first_kernel(place, own, prior, weight, even, odd, factor):
    rank = own.shape[0]
    parity = place[1]
    factor[pl.ds(pl.multiple_of(parity * rank, rank), rank), :] = own[...]
    factor[pl.ds(pl.multiple_of((1 - parity) * rank, rank), rank), :] = prior[...]
    project(factor[...], weight, even, odd)


def gathered(place, pieces, factor):
    width = pieces[0].shape[1]
    for offset, piece in enumerate(pieces):
        start = pl.multiple_of(jnp.bitwise_xor(place[0], offset) * width, width)
        factor[:, pl.ds(start, width)] = piece[...]


def next_kernel(place, *refs):
    *pieces, weight, even, odd, factor = refs
    gathered(place, pieces, factor)
    project(factor[...], weight, even, odd)


def back_kernel(slices, place, even, odd, even_other, odd_other, weight, keep, send, raw, total):
    rank, rows = even.shape
    width = weight.shape[1] // slices
    raw[:rank, :] = even[...] - even_other[...]
    raw[rank:, :] = odd[...] - odd_other[...]
    value = raw[...]
    high = value.astype(BF16)
    low = (value - high.astype(F32)).astype(BF16)
    both = jnp.dot(jnp.concatenate([high, low], axis=0), weight[...], preferred_element_type=F32)
    total[...] = both[: 2 * rank] + both[2 * rank :]
    mine = jnp.bitwise_and(place[0], 1)
    half = slices // 2
    for i in range(half):
        kept = pl.multiple_of((2 * i + mine) * width, width)
        sent = pl.multiple_of((2 * i + 1 - mine) * width, width)
        keep[:, i * width : (i + 1) * width] = total[:, pl.ds(kept, width)]
        send[:, i * width : (i + 1) * width] = total[:, pl.ds(sent, width)]
    product = lax.dot_general(
        value, value, (((1,), (1,)), ((), ())), precision=HIGHEST, preferred_element_type=F32
    )
    gram = jnp.concatenate([product[:rank, :rank], product[rank:, rank:]], axis=0)
    gram = jnp.concatenate([gram, jnp.zeros((2 * rank, LANES - rank), F32)], axis=1)
    keep[:, half * width :] = gram
    send[:, half * width :] = gram


def merge_kernel(bit, slices, place, held, came, keep, send):
    width = (held.shape[1] - LANES) // slices
    mine = jnp.bitwise_and(lax.div(place[0], jnp.int32(bit)), 1)
    for i in range(slices // 2):
        kept = pl.ds(pl.multiple_of((2 * i + mine) * width, width), width)
        sent = pl.ds(pl.multiple_of((2 * i + 1 - mine) * width, width), width)
        keep[:, i * width : (i + 1) * width] = held[:, kept] + came[:, kept]
        send[:, i * width : (i + 1) * width] = held[:, sent] + came[:, sent]
    last = slices // 2 * width
    gram = held[:, slices * width :] + came[:, slices * width :]
    keep[:, last:] = gram
    send[:, last:] = gram


def split_kernel(held, came, even, odd, gram):
    rank, width = even.shape
    even[...] = held[:rank, :width] + came[:rank, :width]
    odd[...] = held[rank:, :width] + came[rank:, :width]
    gram[...] = held[:, width:] + came[:, width:]


def inverse_kernel(gram, inverse):
    rank = gram.shape[0] // 2
    shape = (2, rank, LANES)
    lane = lax.broadcasted_iota(jnp.int32, shape, 2)
    row = lax.broadcasted_iota(jnp.int32, shape, 1)
    work = gram[...].reshape(shape)
    work = jnp.where(lane < rank, work, jnp.where(lane - rank == row, 1.0, 0.0))
    for k in range(rank):
        pivot = work[:, k : k + 1, :]
        scaled = pivot / pivot[:, :, k : k + 1]
        column = jnp.where(row[:, :, :1] > k, work[:, :, k : k + 1], 0.0)
        work = work - column * scaled
    diagonal = jnp.sum(jnp.where(lane == row, work, 0.0), axis=2, keepdims=True)
    work = work / jnp.sqrt(diagonal)
    inverse[...] = work.reshape(2 * rank, LANES)[:, rank : 2 * rank]


def normalised(inverse, even, odd):
    rank = even.shape[0]
    return jnp.concatenate(
        [
            jnp.dot(inverse[:rank, :], even, precision=HIGHEST, preferred_element_type=F32),
            jnp.dot(inverse[rank:, :], odd, precision=HIGHEST, preferred_element_type=F32),
        ],
        axis=0,
    )


def round_kernel(inverse, even, odd, even_other, odd_other, rounded):
    value = normalised(inverse[...], even[...] + even_other[...], odd[...] + odd_other[...])
    rounded[...] = value.astype(BF16)


def final_kernel(place, inverse, even, odd, even_other, odd_other, rounded, own, value):
    rank = even.shape[0]
    value[...] = normalised(inverse[...], even[...] + even_other[...], odd[...] + odd_other[...])
    rounded[...] = value[...].astype(BF16)
    own[...] = value[pl.ds(pl.multiple_of(place[1] * rank, rank), rank), :]


def basis_kernel(inverse, even, odd, even_other, odd_other, columns):
    basis = normalised(inverse[...], even[...] - even_other[...], odd[...] - odd_other[...])
    columns[...] = basis.T.astype(BF16)


def update_kernel(place, columns, *refs):
    *pieces, weight, result, factor = refs

    @pl.when(pl.program_id(0) == 0)
    def _():
        gathered(place, pieces, factor)

    tile = result.shape[0]
    rows = pl.ds(pl.multiple_of(pl.program_id(0) * tile, tile), tile)
    delta = jnp.dot(columns[rows, :], factor[...], preferred_element_type=F32)
    result[...] = (weight[rows, :].astype(F32) - MIXING * delta).astype(BF16)


def swapped(value, axis, pairs):
    return lax.ppermute(value, axis, pairs)


def on_device(weights, warm_factor):
    peers = lax.axis_size("blk")
    shards = lax.axis_size("shard")
    shard = lax.axis_index("shard")
    parity = lax.rem(lax.axis_index("blk"), 2)
    place = jnp.stack([shard, parity]).astype(jnp.int32)
    even_pairs = [(i, i + 1 if i % 2 == 0 else i - 1) for i in range(peers)]
    odd_pairs = [(i, (i + 1) % peers if i % 2 else (i - 1) % peers) for i in range(peers)]
    bits = [1 << i for i in range(shards.bit_length() - 1)]
    across = {bit: [(i, i ^ bit) for i in range(shards)] for bit in bits}

    own = warm_factor[0].astype(BF16)
    rank, wid = own.shape
    prior = lax.ppermute(own, "blk", [(i, (i + 1) % peers) for i in range(peers)])
    weight = hold(weights[0])
    rows = weight.shape[0]
    width = wid // shards
    factor_scratch = [pltpu.VMEM((2 * rank, wid), BF16)]
    product_outs = (out((rank, rows), F32), out((rank, rows), F32))
    full_cost = dict(flops=4 * rank * rows * wid, moved=rows * wid * 2)

    products = kernel_call(
        first_kernel, product_outs, "first", place, own, prior, weight,
        scratch=factor_scratch, mib=16, **full_cost,
    )
    for iteration in range(POWER):
        even, odd = products
        even_other = swapped(even, "blk", even_pairs)
        odd_other = swapped(odd, "blk", odd_pairs)
        slices = shards
        part = (2 * rank, slices // 2 * width + LANES)
        keep, send = kernel_call(
            functools.partial(back_kernel, slices),
            (out(part, F32), out(part, F32)), "back",
            place, even, odd, even_other, odd_other, weight,
            scratch=[pltpu.VMEM((2 * rank, rows), F32), pltpu.VMEM((2 * rank, wid), F32)],
            mib=20, flops=8 * rank * rows * wid, moved=rows * wid * 2,
        )
        for bit in bits:
            came = swapped(send, "shard", across[bit])
            slices //= 2
            if slices == 1:
                break
            part = (2 * rank, slices // 2 * width + LANES)
            keep, send = kernel_call(
                functools.partial(merge_kernel, 2 * bit, slices),
                (out(part, F32), out(part, F32)), "merge", place, keep, came,
            )
        piece = (rank, width)
        even_sum, odd_sum, gram = kernel_call(
            split_kernel, (out(piece, F32), out(piece, F32), out((2 * rank, LANES), F32)),
            "split", keep, came,
        )
        even_sum_other = swapped(even_sum, "blk", even_pairs)
        odd_sum_other = swapped(odd_sum, "blk", odd_pairs)
        inverse = kernel_call(
            inverse_kernel, out((2 * rank, rank), F32), "inverse", gram, flops=1000000, moved=8 * 1024 * 1024,
        )
        sums = (even_sum, odd_sum, even_sum_other, odd_sum_other)
        rounded_out = out((2 * rank, width), BF16)
        if iteration < POWER - 1:
            rounded = kernel_call(round_kernel, rounded_out, "round", inverse, *sums)
        else:
            columns = kernel_call(
                basis_kernel, out((rows, 2 * rank), BF16), "basis",
                inverse, even, odd, even_other, odd_other, mib=16,
                flops=8 * rank * rank * rows, moved=8 * 1024 * 1024,
            )
            rounded, new_factor = kernel_call(
                final_kernel, (rounded_out, out(piece, F32)), "final", place, inverse, *sums,
                scratch=[pltpu.VMEM((2 * rank, width), F32)],
            )
        pieces = {0: rounded}
        for bit in reversed(bits):
            for offset in list(pieces):
                pieces[offset ^ bit] = swapped(pieces[offset], "shard", across[bit])
        pieces = [pieces[offset] for offset in range(shards)]
        if iteration < POWER - 1:
            products = kernel_call(
                next_kernel, product_outs, "next", place, *pieces, weight,
                scratch=factor_scratch, mib=16, **full_cost,
            )
    tile = min(256, rows)
    new_weight = pl.pallas_call(
        update_kernel,
        grid=(rows // tile,),
        out_shape=out((rows, wid), BF16),
        in_specs=[SMEM] + [VMEM] * (len(pieces) + 2),
        out_specs=pl.BlockSpec((tile, wid), lambda i: (i, 0)),
        scratch_shapes=factor_scratch,
        compiler_params=pltpu.CompilerParams(vmem_limit_bytes=20 * 1024 * 1024),
        name="update",
    )(place, columns, *pieces, weight)
    return (new_weight[None], new_factor[None])


def solution(mesh):
    placed = (P("blk", "shard", None), P("blk", None, None))
    return jax.shard_map(
        on_device,
        mesh=mesh,
        in_specs=placed,
        out_specs=(P("blk", "shard", None), P("blk", None, "shard")),
        check_vma=False,
    )
```

time: 364 us -> 184 us (0.51)
  blocking collectives: 90.5 us -> 0 us
  matrix products: 55.7 us -> 0 us
  other arithmetic: 48.5 us -> 1.04 us
  Pallas kernels: 0 us -> 46.1 us
  waiting for transfers between devices: 127 us -> 95.2 us
  between operations: 14.3 us -> 0.83 us
  starting transfers between devices: 25.1 us -> 37 us
    psum x7 -> x0, blocking collectives: 90.5 us -> none  [the longest x3 48.7 us: on_device(): lax.psum(jnp.stack([partials[0] - next_part, prior_part - partials[1]]),...]
    dot_general x13 -> x0, matrix products: 53.1 us -> none  [the longest x4 24.1 us: on_device(): jnp.einsum('ekc,rc->ekr', rounded, local_weight, preferred_element_type=j...]
    pallas_call x0 -> x27, Pallas kernels: none -> 46.1 us  [the longest x25 38.9 us: kernel_call(): pl.pallas_call(body, out_shape=outs, in_specs=specs, out_specs=jax.tree.m...]
    another operation x34 -> x1, other arithmetic: 45.5 us -> 0.08 us  [on_device(): place = jnp.stack([shard, parity]).astype(jnp.int32)]
    psum x1 -> x0, waiting for transfers between devices: 32.8 us -> none  [on_device(): lax.psum(jnp.stack([partials[0] - next_part, prior_part - partials[1]]),...]
    ppermute x17 -> x37, starting transfers between devices: 25.1 us -> 37 us  [the longest x36 33.9 us: swapped(): return lax.ppermute(value, axis, pairs)]
    ppermute x17 -> x37, waiting for transfers between devices: 94.6 us -> 95.2 us  [the longest x36 92.7 us: swapped(): return lax.ppermute(value, axis, pairs)]
  transfers between devices with their start and end apart: 18 -> 37, of which waited for: 13 -> 25; matrix products, arithmetic and copies ran while one was open for 0% -> 0% of each run, Pallas kernels for 0% -> 7%
where the time goes in v1:
time: 184 us; the launch traced here: 183 us
  waiting for transfers between devices  95.2 us (52%)
  Pallas kernels  46.1 us (25%)
  starting transfers between devices  37 us (20%)
  local copies, waits for them, and re-layouts  3.38 us (2%)
    ppermute x36, waiting for transfers between devices, swapped(): return lax.ppermute(value, axis, pairs)  92.7 us
    pallas_call x25, Pallas kernels, kernel_call(): pl.pallas_call(body, out_shape=outs, in_specs=specs, out_specs=jax.tree.m...  38.9 us
    ppermute x36, starting transfers between devices, swapped(): return lax.ppermute(value, axis, pairs)  33.9 us
    pallas_call x1, Pallas kernels, on_device(): pl.pallas_call(update_kernel, grid=(rows // tile,), out_shape=out((rows,...  6.59 us
  transfers between devices with their start and end apart: 37, of which 25 were waited for; matrix products, arithmetic and copies ran while one was open for 0% of the time, Pallas kernels for 7%

profile of v1, /device:TPU:0, one launch (start us, length us, event | category | flops | bytes accessed | tf_op | source)
XLA Modules:
  0.0 183.4 jit_solution(1593364212974880174)
XLA Ops:
  1.6 3.0 %collective-permute-start = (bf16[32,2048]{1,0:T(8,128)(2,1)S(1)}, bf16[32,2048]{1,0:T(8,128)(2,1)S(1)}, u32[]{:S(2)}, u32[]{:S(2)}) collective-permute-start(bf16[32,2048]{1,0:T(8,128)(2,1)S(1)} %convert_bitcast_fusion.own), channel_id=1, source_target_pairs={{0,4},{4,8},{8,12},{12,16},{16,20},{20,24},{24,28},{28,0},{1,5},{5... | collective-permute-start | bytes 393224 | tf_op jit(solution)/shard_map/ppermute | solution.py:211
  4.6 3.4 %copy-done = bf16[1,2048,2048]{2,1,0:T(8,128)(2,1)S(1)} copy-done((bf16[1,2048,2048]{2,1,0:T(8,128)(2,1)S(1)}, bf16[1,2048,2048]{2,1,0:T(8,128)(2,1)}, u32[]{:S(2)}) %copy-start) | copy-done | bytes 8388632
  11.2 3.2 %first.1 = (f32[32,2048]{1,0:T(8,128)S(1)}, f32[32,2048]{1,0:T(8,128)S(1)}) custom-call(s32[2]{0:T(128)S(1)} %pad_add_fusion.place, bf16[32,2048]{1,0:T(8,128)(2,1)S(1)} %convert_bitcast_fusion.own, bf16[32,2048]{1,0:T(8,128)(2,1)S(1)} %collective-permute-done.prior, bf16[2048,2048]{1,0:T(8,128)(2,1)S(1)} %hold.1.weight.refs_4_), custom_call_target="tpu_custom_call" | custom-call | flops 536870912 | bytes 8388608 | tf_op jit(solution)/shard_map/first/pallas_call | solution.py:25
  14.4 3.1 %collective-permute-start.2 = (f32[32,2048]{1,0:T(8,128)S(1)}, f32[32,2048]{1,0:T(8,128)S(1)}, u32[]{:S(2)}, u32[]{:S(2)}) collective-permute-start(f32[32,2048]{1,0:T(8,128)S(1)} %get-tuple-element.41.odd), channel_id=1, source_target_pairs={{0,28},{4,8},{8,4},{12,16},{16,12},{20,24},{24,20},{28,0},{1,29},{... | collective-permute-start | bytes 786440 | tf_op jit(solution)/shard_map/ppermute | solution.py:195
  17.6 10.0 %collective-permute-done.1.even_other = f32[32,2048]{1,0:T(8,128)S(1)} collective-permute-done((f32[32,2048]{1,0:T(8,128)S(1)}, f32[32,2048]{1,0:T(8,128)S(1)}, u32[]{:S(2)}, u32[]{:S(2)}) %collective-permute-start.1) | collective-permute-done | bytes 262176 | tf_op jit(solution)/shard_map/ppermute | solution.py:195
  33.5 4.9 %collective-permute-done.4.came = f32[64,640]{1,0:T(8,128)S(1)} collective-permute-done((f32[64,640]{1,0:T(8,128)S(1)}, f32[64,640]{1,0:T(8,128)S(1)}, u32[]{:S(2)}, u32[]{:S(2)}) %collective-permute-start.4) | collective-permute-done | bytes 163872 | tf_op jit(solution)/shard_map/ppermute | solution.py:195
  38.8 2.6 %collective-permute-start.6 = (f32[32,512]{1,0:T(8,128)S(1)}, f32[32,512]{1,0:T(8,128)S(1)}, u32[]{:S(2)}, u32[]{:S(2)}) collective-permute-start(f32[32,512]{1,0:T(8,128)S(1)} %get-tuple-element.48.odd), channel_id=1, source_target_pairs={{0,28},{4,8},{8,4},{12,16},{16,12},{20,24},{24,20},{28,0},{1,29},{... | collective-permute-start | bytes 196616 | tf_op jit(solution)/shard_map/ppermute | solution.py:195
  41.4 2.8 %inverse.4 = f32[64,32]{1,0:T(8,128)S(1)} custom-call(f32[64,128]{1,0:T(8,128)S(1)} %get-tuple-element.46.gram), custom_call_target="tpu_custom_call" | custom-call | flops 1000000 | bytes 8388608 | tf_op jit(solution)/shard_map/inverse/pallas_call | solution.py:25
  47.4 3.0 %collective-permute-done.8.refs_2_ = bf16[64,512]{1,0:T(8,128)(2,1)S(1)} collective-permute-done((bf16[64,512]{1,0:T(8,128)(2,1)S(1)}, bf16[64,512]{1,0:T(8,128)(2,1)S(1)}, u32[]{:S(2)}, u32[]{:S(2)}) %collective-permute-start.8) | collective-permute-done | bytes 65568 | tf_op jit(solution)/shard_map/ppermute | solution.py:195
  51.6 3.2 %next.3 = (f32[32,2048]{1,0:T(8,128)S(1)}, f32[32,2048]{1,0:T(8,128)S(1)}) custom-call(s32[2]{0:T(128)S(1)} %pad_add_fusion.place, bf16[64,512]{1,0:T(8,128)(2,1)S(1)} %round.3.refs_0_, bf16[64,512]{1,0:T(8,128)(2,1)S(1)} %collective-permute-done.7.refs_1_, bf16[64,512]{1,0:T(8,128)(2,1)S(1)} %collective-permute-done.8.refs_2_, ...), custom_call_target="tpu_custom_call" | custom-call | flops 536870912 | bytes 8388608 | tf_op jit(solution)/shard_map/next/pallas_call | solution.py:25
  54.9 2.6 %collective-permute-start.11 = (f32[32,2048]{1,0:T(8,128)S(1)}, f32[32,2048]{1,0:T(8,128)S(1)}, u32[]{:S(2)}, u32[]{:S(2)}) collective-permute-start(f32[32,2048]{1,0:T(8,128)S(1)} %get-tuple-element.50.odd), channel_id=1, source_target_pairs={{0,28},{4,8},{8,4},{12,16},{16,12},{20,24},{24,20},{28,0},{1,29},{... | collective-permute-start | bytes 786440 | tf_op jit(solution)/shard_map/ppermute | solution.py:195
  57.5 11.4 %collective-permute-done.10.even_other = f32[32,2048]{1,0:T(8,128)S(1)} collective-permute-done((f32[32,2048]{1,0:T(8,128)S(1)}, f32[32,2048]{1,0:T(8,128)S(1)}, u32[]{:S(2)}, u32[]{:S(2)}) %collective-permute-start.10) | collective-permute-done | bytes 262176 | tf_op jit(solution)/shard_map/ppermute | solution.py:195
  74.8 4.9 %collective-permute-done.13.came = f32[64,640]{1,0:T(8,128)S(1)} collective-permute-done((f32[64,640]{1,0:T(8,128)S(1)}, f32[64,640]{1,0:T(8,128)S(1)}, u32[]{:S(2)}, u32[]{:S(2)}) %collective-permute-start.13) | collective-permute-done | bytes 163872 | tf_op jit(solution)/shard_map/ppermute | solution.py:195
  80.1 2.6 %collective-permute-start.15 = (f32[32,512]{1,0:T(8,128)S(1)}, f32[32,512]{1,0:T(8,128)S(1)}, u32[]{:S(2)}, u32[]{:S(2)}) collective-permute-start(f32[32,512]{1,0:T(8,128)S(1)} %get-tuple-element.57.odd), channel_id=1, source_target_pairs={{0,28},{4,8},{8,4},{12,16},{16,12},{20,24},{24,20},{28,0},{1,29},{... | collective-permute-start | bytes 196616 | tf_op jit(solution)/shard_map/ppermute | solution.py:195
  82.7 2.8 %inverse.5 = f32[64,32]{1,0:T(8,128)S(1)} custom-call(f32[64,128]{1,0:T(8,128)S(1)} %get-tuple-element.55.gram), custom_call_target="tpu_custom_call" | custom-call | flops 1000000 | bytes 8388608 | tf_op jit(solution)/shard_map/inverse/pallas_call | solution.py:25
  88.7 3.0 %collective-permute-done.17.refs_2_ = bf16[64,512]{1,0:T(8,128)(2,1)S(1)} collective-permute-done((bf16[64,512]{1,0:T(8,128)(2,1)S(1)}, bf16[64,512]{1,0:T(8,128)(2,1)S(1)}, u32[]{:S(2)}, u32[]{:S(2)}) %collective-permute-start.17) | collective-permute-done | bytes 65568 | tf_op jit(solution)/shard_map/ppermute | solution.py:195
  92.9 3.2 %next.4 = (f32[32,2048]{1,0:T(8,128)S(1)}, f32[32,2048]{1,0:T(8,128)S(1)}) custom-call(s32[2]{0:T(128)S(1)} %pad_add_fusion.place, bf16[64,512]{1,0:T(8,128)(2,1)S(1)} %round.4.refs_0_, bf16[64,512]{1,0:T(8,128)(2,1)S(1)} %collective-permute-done.16.refs_1_, bf16[64,512]{1,0:T(8,128)(2,1)S(1)} %collective-permute-done.17.refs_2_, ...), custom_call_target="tpu_custom_call" | custom-call | flops 536870912 | bytes 8388608 | tf_op jit(solution)/shard_map/next/pallas_call | solution.py:25
  96.2 2.6 %collective-permute-start.20 = (f32[32,2048]{1,0:T(8,128)S(1)}, f32[32,2048]{1,0:T(8,128)S(1)}, u32[]{:S(2)}, u32[]{:S(2)}) collective-permute-start(f32[32,2048]{1,0:T(8,128)S(1)} %get-tuple-element.59.odd), channel_id=1, source_target_pairs={{0,28},{4,8},{8,4},{12,16},{16,12},{20,24},{24,20},{28,0},{1,29},{... | collective-permute-start | bytes 786440 | tf_op jit(solution)/shard_map/ppermute | solution.py:195
  98.8 11.4 %collective-permute-done.19.even_other = f32[32,2048]{1,0:T(8,128)S(1)} collective-permute-done((f32[32,2048]{1,0:T(8,128)S(1)}, f32[32,2048]{1,0:T(8,128)S(1)}, u32[]{:S(2)}, u32[]{:S(2)}) %collective-permute-start.19) | collective-permute-done | bytes 262176 | tf_op jit(solution)/shard_map/ppermute | solution.py:195
  110.1 2.6 %back.6 = (f32[64,1152]{1,0:T(8,128)S(1)}, f32[64,1152]{1,0:T(8,128)S(1)}) custom-call(s32[2]{0:T(128)S(1)} %pad_add_fusion.place, f32[32,2048]{1,0:T(8,128)S(1)} %get-tuple-element.58.even, f32[32,2048]{1,0:T(8,128)S(1)} %get-tuple-element.59.odd, f32[32,2048]{1,0:T(8,128)S(1)} %collective-permute-done.19.even_other, ...), custom_call_target="tpu_custom_call" | custom-call | flops 1073741824 | bytes 8388608 | tf_op jit(solution)/shard_map/back/pallas_call | solution.py:25
  116.3 4.9 %collective-permute-done.22.came = f32[64,640]{1,0:T(8,128)S(1)} collective-permute-done((f32[64,640]{1,0:T(8,128)S(1)}, f32[64,640]{1,0:T(8,128)S(1)}, u32[]{:S(2)}, u32[]{:S(2)}) %collective-permute-start.22) | collective-permute-done | bytes 163872 | tf_op jit(solution)/shard_map/ppermute | solution.py:195
  121.6 2.6 %collective-permute-start.24 = (f32[32,512]{1,0:T(8,128)S(1)}, f32[32,512]{1,0:T(8,128)S(1)}, u32[]{:S(2)}, u32[]{:S(2)}) collective-permute-start(f32[32,512]{1,0:T(8,128)S(1)} %get-tuple-element.66.odd), channel_id=1, source_target_pairs={{0,28},{4,8},{8,4},{12,16},{16,12},{20,24},{24,20},{28,0},{1,29},{... | collective-permute-start | bytes 196616 | tf_op jit(solution)/shard_map/ppermute | solution.py:195
  124.2 2.8 %inverse.6 = f32[64,32]{1,0:T(8,128)S(1)} custom-call(f32[64,128]{1,0:T(8,128)S(1)} %get-tuple-element.64.gram), custom_call_target="tpu_custom_call" | custom-call | flops 1000000 | bytes 8388608 | tf_op jit(solution)/shard_map/inverse/pallas_call | solution.py:25
  130.2 3.0 %collective-permute-done.26.refs_2_ = bf16[64,512]{1,0:T(8,128)(2,1)S(1)} collective-permute-done((bf16[64,512]{1,0:T(8,128)(2,1)S(1)}, bf16[64,512]{1,0:T(8,128)(2,1)S(1)}, u32[]{:S(2)}, u32[]{:S(2)}) %collective-permute-start.26) | collective-permute-done | bytes 65568 | tf_op jit(solution)/shard_map/ppermute | solution.py:195
  134.4 3.2 %next.5 = (f32[32,2048]{1,0:T(8,128)S(1)}, f32[32,2048]{1,0:T(8,128)S(1)}) custom-call(s32[2]{0:T(128)S(1)} %pad_add_fusion.place, bf16[64,512]{1,0:T(8,128)(2,1)S(1)} %round.5.refs_0_, bf16[64,512]{1,0:T(8,128)(2,1)S(1)} %collective-permute-done.25.refs_1_, bf16[64,512]{1,0:T(8,128)(2,1)S(1)} %collective-permute-done.26.refs_2_, ...), custom_call_target="tpu_custom_call" | custom-call | flops 536870912 | bytes 8388608 | tf_op jit(solution)/shard_map/next/pallas_call | solution.py:25
  137.6 2.6 %collective-permute-start.29 = (f32[32,2048]{1,0:T(8,128)S(1)}, f32[32,2048]{1,0:T(8,128)S(1)}, u32[]{:S(2)}, u32[]{:S(2)}) collective-permute-start(f32[32,2048]{1,0:T(8,128)S(1)} %get-tuple-element.68.odd), channel_id=1, source_target_pairs={{0,28},{4,8},{8,4},{12,16},{16,12},{20,24},{24,20},{28,0},{1,29},{... | collective-permute-start | bytes 786440 | tf_op jit(solution)/shard_map/ppermute | solution.py:195
  140.3 11.4 %collective-permute-done.28.even_other = f32[32,2048]{1,0:T(8,128)S(1)} collective-permute-done((f32[32,2048]{1,0:T(8,128)S(1)}, f32[32,2048]{1,0:T(8,128)S(1)}, u32[]{:S(2)}, u32[]{:S(2)}) %collective-permute-start.28) | collective-permute-done | bytes 262176 | tf_op jit(solution)/shard_map/ppermute | solution.py:195
  157.6 4.9 %collective-permute-done.31.came = f32[64,640]{1,0:T(8,128)S(1)} collective-permute-done((f32[64,640]{1,0:T(8,128)S(1)}, f32[64,640]{1,0:T(8,128)S(1)}, u32[]{:S(2)}, u32[]{:S(2)}) %collective-permute-start.31) | collective-permute-done | bytes 163872 | tf_op jit(solution)/shard_map/ppermute | solution.py:195
  162.9 2.6 %collective-permute-start.33 = (f32[32,512]{1,0:T(8,128)S(1)}, f32[32,512]{1,0:T(8,128)S(1)}, u32[]{:S(2)}, u32[]{:S(2)}) collective-permute-start(f32[32,512]{1,0:T(8,128)S(1)} %get-tuple-element.75.odd), channel_id=1, source_target_pairs={{0,28},{4,8},{8,4},{12,16},{16,12},{20,24},{24,20},{28,0},{1,29},{... | collective-permute-start | bytes 196616 | tf_op jit(solution)/shard_map/ppermute | solution.py:195
  165.5 2.8 %inverse.7 = f32[64,32]{1,0:T(8,128)S(1)} custom-call(f32[64,128]{1,0:T(8,128)S(1)} %get-tuple-element.73.gram), custom_call_target="tpu_custom_call" | custom-call | flops 1000000 | bytes 8388608 | tf_op jit(solution)/shard_map/inverse/pallas_call | solution.py:25
  172.6 3.0 %collective-permute-done.35.refs_2_ = bf16[64,512]{1,0:T(8,128)(2,1)S(1)} collective-permute-done((bf16[64,512]{1,0:T(8,128)(2,1)S(1)}, bf16[64,512]{1,0:T(8,128)(2,1)S(1)}, u32[]{:S(2)}, u32[]{:S(2)}) %collective-permute-start.35) | collective-permute-done | bytes 65568 | tf_op jit(solution)/shard_map/ppermute | solution.py:195
  176.8 6.6 %update.1 = bf16[2048,2048]{1,0:T(8,128)(2,1)} custom-call(s32[2]{0:T(128)S(1)} %pad_add_fusion.place, bf16[2048,64]{1,0:T(8,128)(2,1)S(1)} %basis.1.columns, bf16[64,512]{1,0:T(8,128)(2,1)S(1)} %get-tuple-element.76.refs_0_, bf16[64,512]{1,0:T(8,128)(2,1)S(1)} %collective-permute-done.34.refs_1_, bf16[64,512]{1,0:T(8,128)(2,1)S(1)} %collective-permute-done.35.refs_2_, ...), custom_call_target="tpu_custom_call" | custom-call | tf_op jit(solution)/shard_map/update/pallas_call | solution.py:281
  (73 shorter events, 46.4 us)
Async XLA Ops:
  1.6 9.6 %collective-permute-start = (bf16[32,2048]{1,0:T(8,128)(2,1)S(1)}, bf16[32,2048]{1,0:T(8,128)(2,1)S(1)}, u32[]{:S(2)}, u32[]{:S(2)}) collective-permute-start(bf16[32,2048]{1,0:T(8,128)(2,1)S(1)} %convert_bitcast_fusion.own), channel_id=1, source_target_pairs={{0,4},{4,8},{8,12},{12,16},{16,20},{20,24},{24,28},{28,0},{1,5},{5... | collective-permute-start | bytes 393224 | tf_op jit(solution)/shard_map/ppermute | solution.py:211
  14.3 13.2 %collective-permute-start.1 = (f32[32,2048]{1,0:T(8,128)S(1)}, f32[32,2048]{1,0:T(8,128)S(1)}, u32[]{:S(2)}, u32[]{:S(2)}) collective-permute-start(f32[32,2048]{1,0:T(8,128)S(1)} %get-tuple-element.40.even), channel_id=1, source_target_pairs={{0,4},{4,0},{8,12},{12,8},{16,20},{20,16},{24,28},{28,24},{1,5},{5... | collective-permute-start | bytes 786440 | tf_op jit(solution)/shard_map/ppermute | solution.py:195
  14.4 13.1 %collective-permute-start.2 = (f32[32,2048]{1,0:T(8,128)S(1)}, f32[32,2048]{1,0:T(8,128)S(1)}, u32[]{:S(2)}, u32[]{:S(2)}) collective-permute-start(f32[32,2048]{1,0:T(8,128)S(1)} %get-tuple-element.41.odd), channel_id=1, source_target_pairs={{0,28},{4,8},{8,4},{12,16},{16,12},{20,24},{24,20},{28,0},{1,29},{... | collective-permute-start | bytes 786440 | tf_op jit(solution)/shard_map/ppermute | solution.py:195
  29.9 1.6 collective-permute-start.3
  32.1 6.3 %collective-permute-start.4 = (f32[64,640]{1,0:T(8,128)S(1)}, f32[64,640]{1,0:T(8,128)S(1)}, u32[]{:S(2)}, u32[]{:S(2)}) collective-permute-start(f32[64,640]{1,0:T(8,128)S(1)} %get-tuple-element.45), channel_id=1, source_target_pairs={{0,2},{1,3},{2,0},{3,1},{4,6},{5,7},{6,4},{7,5},{8,10},{9,11},{10,... | collective-permute-start | bytes 491528 | tf_op jit(solution)/shard_map/ppermute | solution.py:195
  38.5 5.7 %collective-permute-start.5 = (f32[32,512]{1,0:T(8,128)S(1)}, f32[32,512]{1,0:T(8,128)S(1)}, u32[]{:S(2)}, u32[]{:S(2)}) collective-permute-start(f32[32,512]{1,0:T(8,128)S(1)} %get-tuple-element.47.even), channel_id=1, source_target_pairs={{0,4},{4,0},{8,12},{12,8},{16,20},{20,16},{24,28},{28,24},{1,5},{5... | collective-permute-start | bytes 196616 | tf_op jit(solution)/shard_map/ppermute | solution.py:195
  38.8 7.0 %collective-permute-start.6 = (f32[32,512]{1,0:T(8,128)S(1)}, f32[32,512]{1,0:T(8,128)S(1)}, u32[]{:S(2)}, u32[]{:S(2)}) collective-permute-start(f32[32,512]{1,0:T(8,128)S(1)} %get-tuple-element.48.odd), channel_id=1, source_target_pairs={{0,28},{4,8},{8,4},{12,16},{16,12},{20,24},{24,20},{28,0},{1,29},{... | collective-permute-start | bytes 196616 | tf_op jit(solution)/shard_map/ppermute | solution.py:195
  46.0 4.3 %collective-permute-start.8 = (bf16[64,512]{1,0:T(8,128)(2,1)S(1)}, bf16[64,512]{1,0:T(8,128)(2,1)S(1)}, u32[]{:S(2)}, u32[]{:S(2)}) collective-permute-start(bf16[64,512]{1,0:T(8,128)(2,1)S(1)} %round.3.refs_0_), channel_id=1, source_target_pairs={{0,2},{1,3},{2,0},{3,1},{4,6},{5,7},{6,4},{7,5},{8,10},{9,11},{10,... | collective-permute-start | bytes 196616 | tf_op jit(solution)/shard_map/ppermute | solution.py:195
  47.4 3.0 %collective-permute-start.7 = (bf16[64,512]{1,0:T(8,128)(2,1)S(1)}, bf16[64,512]{1,0:T(8,128)(2,1)S(1)}, u32[]{:S(2)}, u32[]{:S(2)}) collective-permute-start(bf16[64,512]{1,0:T(8,128)(2,1)S(1)} %round.3.refs_0_), channel_id=1, source_target_pairs={{0,1},{1,0},{2,3},{3,2},{4,5},{5,4},{6,7},{7,6},{8,9},{9,8},{10,11... | collective-permute-start | bytes 196616 | tf_op jit(solution)/shard_map/ppermute | solution.py:195
  54.8 14.1 %collective-permute-start.10 = (f32[32,2048]{1,0:T(8,128)S(1)}, f32[32,2048]{1,0:T(8,128)S(1)}, u32[]{:S(2)}, u32[]{:S(2)}) collective-permute-start(f32[32,2048]{1,0:T(8,128)S(1)} %get-tuple-element.49.even), channel_id=1, source_target_pairs={{0,4},{4,0},{8,12},{12,8},{16,20},{20,16},{24,28},{28,24},{1,5},{5... | collective-permute-start | bytes 786440 | tf_op jit(solution)/shard_map/ppermute | solution.py:195
  54.9 14.0 %collective-permute-start.11 = (f32[32,2048]{1,0:T(8,128)S(1)}, f32[32,2048]{1,0:T(8,128)S(1)}, u32[]{:S(2)}, u32[]{:S(2)}) collective-permute-start(f32[32,2048]{1,0:T(8,128)S(1)} %get-tuple-element.50.odd), channel_id=1, source_target_pairs={{0,28},{4,8},{8,4},{12,16},{16,12},{20,24},{24,20},{28,0},{1,29},{... | collective-permute-start | bytes 786440 | tf_op jit(solution)/shard_map/ppermute | solution.py:195
  71.3 1.6 collective-permute-start.12
  73.5 6.3 %collective-permute-start.13 = (f32[64,640]{1,0:T(8,128)S(1)}, f32[64,640]{1,0:T(8,128)S(1)}, u32[]{:S(2)}, u32[]{:S(2)}) collective-permute-start(f32[64,640]{1,0:T(8,128)S(1)} %get-tuple-element.54), channel_id=1, source_target_pairs={{0,2},{1,3},{2,0},{3,1},{4,6},{5,7},{6,4},{7,5},{8,10},{9,11},{10,... | collective-permute-start | bytes 491528 | tf_op jit(solution)/shard_map/ppermute | solution.py:195
  79.8 5.7 %collective-permute-start.14 = (f32[32,512]{1,0:T(8,128)S(1)}, f32[32,512]{1,0:T(8,128)S(1)}, u32[]{:S(2)}, u32[]{:S(2)}) collective-permute-start(f32[32,512]{1,0:T(8,128)S(1)} %get-tuple-element.56.even), channel_id=1, source_target_pairs={{0,4},{4,0},{8,12},{12,8},{16,20},{20,16},{24,28},{28,24},{1,5},{5... | collective-permute-start | bytes 196616 | tf_op jit(solution)/shard_map/ppermute | solution.py:195
  80.1 7.0 %collective-permute-start.15 = (f32[32,512]{1,0:T(8,128)S(1)}, f32[32,512]{1,0:T(8,128)S(1)}, u32[]{:S(2)}, u32[]{:S(2)}) collective-permute-start(f32[32,512]{1,0:T(8,128)S(1)} %get-tuple-element.57.odd), channel_id=1, source_target_pairs={{0,28},{4,8},{8,4},{12,16},{16,12},{20,24},{24,20},{28,0},{1,29},{... | collective-permute-start | bytes 196616 | tf_op jit(solution)/shard_map/ppermute | solution.py:195
  87.3 4.3 %collective-permute-start.17 = (bf16[64,512]{1,0:T(8,128)(2,1)S(1)}, bf16[64,512]{1,0:T(8,128)(2,1)S(1)}, u32[]{:S(2)}, u32[]{:S(2)}) collective-permute-start(bf16[64,512]{1,0:T(8,128)(2,1)S(1)} %round.4.refs_0_), channel_id=1, source_target_pairs={{0,2},{1,3},{2,0},{3,1},{4,6},{5,7},{6,4},{7,5},{8,10},{9,11},{10,... | collective-permute-start | bytes 196616 | tf_op jit(solution)/shard_map/ppermute | solution.py:195
  88.7 3.0 %collective-permute-start.16 = (bf16[64,512]{1,0:T(8,128)(2,1)S(1)}, bf16[64,512]{1,0:T(8,128)(2,1)S(1)}, u32[]{:S(2)}, u32[]{:S(2)}) collective-permute-start(bf16[64,512]{1,0:T(8,128)(2,1)S(1)} %round.4.refs_0_), channel_id=1, source_target_pairs={{0,1},{1,0},{2,3},{3,2},{4,5},{5,4},{6,7},{7,6},{8,9},{9,8},{10,11... | collective-permute-start | bytes 196616 | tf_op jit(solution)/shard_map/ppermute | solution.py:195
  96.1 14.1 %collective-permute-start.19 = (f32[32,2048]{1,0:T(8,128)S(1)}, f32[32,2048]{1,0:T(8,128)S(1)}, u32[]{:S(2)}, u32[]{:S(2)}) collective-permute-start(f32[32,2048]{1,0:T(8,128)S(1)} %get-tuple-element.58.even), channel_id=1, source_target_pairs={{0,4},{4,0},{8,12},{12,8},{16,20},{20,16},{24,28},{28,24},{1,5},{5... | collective-permute-start | bytes 786440 | tf_op jit(solution)/shard_map/ppermute | solution.py:195
  96.2 14.0 %collective-permute-start.20 = (f32[32,2048]{1,0:T(8,128)S(1)}, f32[32,2048]{1,0:T(8,128)S(1)}, u32[]{:S(2)}, u32[]{:S(2)}) collective-permute-start(f32[32,2048]{1,0:T(8,128)S(1)} %get-tuple-element.59.odd), channel_id=1, source_target_pairs={{0,28},{4,8},{8,4},{12,16},{16,12},{20,24},{24,20},{28,0},{1,29},{... | collective-permute-start | bytes 786440 | tf_op jit(solution)/shard_map/ppermute | solution.py:195
  112.8 1.6 collective-permute-start.21
  114.9 6.3 %collective-permute-start.22 = (f32[64,640]{1,0:T(8,128)S(1)}, f32[64,640]{1,0:T(8,128)S(1)}, u32[]{:S(2)}, u32[]{:S(2)}) collective-permute-start(f32[64,640]{1,0:T(8,128)S(1)} %get-tuple-element.63), channel_id=1, source_target_pairs={{0,2},{1,3},{2,0},{3,1},{4,6},{5,7},{6,4},{7,5},{8,10},{9,11},{10,... | collective-permute-start | bytes 491528 | tf_op jit(solution)/shard_map/ppermute | solution.py:195
  121.3 5.7 %collective-permute-start.23 = (f32[32,512]{1,0:T(8,128)S(1)}, f32[32,512]{1,0:T(8,128)S(1)}, u32[]{:S(2)}, u32[]{:S(2)}) collective-permute-start(f32[32,512]{1,0:T(8,128)S(1)} %get-tuple-element.65.even), channel_id=1, source_target_pairs={{0,4},{4,0},{8,12},{12,8},{16,20},{20,16},{24,28},{28,24},{1,5},{5... | collective-permute-start | bytes 196616 | tf_op jit(solution)/shard_map/ppermute | solution.py:195
  121.6 7.0 %collective-permute-start.24 = (f32[32,512]{1,0:T(8,128)S(1)}, f32[32,512]{1,0:T(8,128)S(1)}, u32[]{:S(2)}, u32[]{:S(2)}) collective-permute-start(f32[32,512]{1,0:T(8,128)S(1)} %get-tuple-element.66.odd), channel_id=1, source_target_pairs={{0,28},{4,8},{8,4},{12,16},{16,12},{20,24},{24,20},{28,0},{1,29},{... | collective-permute-start | bytes 196616 | tf_op jit(solution)/shard_map/ppermute | solution.py:195
  128.8 4.3 %collective-permute-start.26 = (bf16[64,512]{1,0:T(8,128)(2,1)S(1)}, bf16[64,512]{1,0:T(8,128)(2,1)S(1)}, u32[]{:S(2)}, u32[]{:S(2)}) collective-permute-start(bf16[64,512]{1,0:T(8,128)(2,1)S(1)} %round.5.refs_0_), channel_id=1, source_target_pairs={{0,2},{1,3},{2,0},{3,1},{4,6},{5,7},{6,4},{7,5},{8,10},{9,11},{10,... | collective-permute-start | bytes 196616 | tf_op jit(solution)/shard_map/ppermute | solution.py:195
  130.2 3.0 %collective-permute-start.25 = (bf16[64,512]{1,0:T(8,128)(2,1)S(1)}, bf16[64,512]{1,0:T(8,128)(2,1)S(1)}, u32[]{:S(2)}, u32[]{:S(2)}) collective-permute-start(bf16[64,512]{1,0:T(8,128)(2,1)S(1)} %round.5.refs_0_), channel_id=1, source_target_pairs={{0,1},{1,0},{2,3},{3,2},{4,5},{5,4},{6,7},{7,6},{8,9},{9,8},{10,11... | collective-permute-start | bytes 196616 | tf_op jit(solution)/shard_map/ppermute | solution.py:195
  137.6 14.1 %collective-permute-start.28 = (f32[32,2048]{1,0:T(8,128)S(1)}, f32[32,2048]{1,0:T(8,128)S(1)}, u32[]{:S(2)}, u32[]{:S(2)}) collective-permute-start(f32[32,2048]{1,0:T(8,128)S(1)} %get-tuple-element.67.even), channel_id=1, source_target_pairs={{0,4},{4,0},{8,12},{12,8},{16,20},{20,16},{24,28},{28,24},{1,5},{5... | collective-permute-start | bytes 786440 | tf_op jit(solution)/shard_map/ppermute | solution.py:195
  137.6 14.0 %collective-permute-start.29 = (f32[32,2048]{1,0:T(8,128)S(1)}, f32[32,2048]{1,0:T(8,128)S(1)}, u32[]{:S(2)}, u32[]{:S(2)}) collective-permute-start(f32[32,2048]{1,0:T(8,128)S(1)} %get-tuple-element.68.odd), channel_id=1, source_target_pairs={{0,28},{4,8},{8,4},{12,16},{16,12},{20,24},{24,20},{28,0},{1,29},{... | collective-permute-start | bytes 786440 | tf_op jit(solution)/shard_map/ppermute | solution.py:195
  156.3 6.3 %collective-permute-start.31 = (f32[64,640]{1,0:T(8,128)S(1)}, f32[64,640]{1,0:T(8,128)S(1)}, u32[]{:S(2)}, u32[]{:S(2)}) collective-permute-start(f32[64,640]{1,0:T(8,128)S(1)} %get-tuple-element.72), channel_id=1, source_target_pairs={{0,2},{1,3},{2,0},{3,1},{4,6},{5,7},{6,4},{7,5},{8,10},{9,11},{10,... | collective-permute-start | bytes 491528 | tf_op jit(solution)/shard_map/ppermute | solution.py:195
  162.6 5.7 %collective-permute-start.32 = (f32[32,512]{1,0:T(8,128)S(1)}, f32[32,512]{1,0:T(8,128)S(1)}, u32[]{:S(2)}, u32[]{:S(2)}) collective-permute-start(f32[32,512]{1,0:T(8,128)S(1)} %get-tuple-element.74.even), channel_id=1, source_target_pairs={{0,4},{4,0},{8,12},{12,8},{16,20},{20,16},{24,28},{28,24},{1,5},{5... | collective-permute-start | bytes 196616 | tf_op jit(solution)/shard_map/ppermute | solution.py:195
  162.9 7.0 %collective-permute-start.33 = (f32[32,512]{1,0:T(8,128)S(1)}, f32[32,512]{1,0:T(8,128)S(1)}, u32[]{:S(2)}, u32[]{:S(2)}) collective-permute-start(f32[32,512]{1,0:T(8,128)S(1)} %get-tuple-element.75.odd), channel_id=1, source_target_pairs={{0,28},{4,8},{8,4},{12,16},{16,12},{20,24},{24,20},{28,0},{1,29},{... | collective-permute-start | bytes 196616 | tf_op jit(solution)/shard_map/ppermute | solution.py:195
  171.3 4.3 %collective-permute-start.35 = (bf16[64,512]{1,0:T(8,128)(2,1)S(1)}, bf16[64,512]{1,0:T(8,128)(2,1)S(1)}, u32[]{:S(2)}, u32[]{:S(2)}) collective-permute-start(bf16[64,512]{1,0:T(8,128)(2,1)S(1)} %get-tuple-element.76.refs_0_), channel_id=1, source_target_pairs={{0,2},{1,3},{2,0},{3,1},{4,6},{5,7},{6,4},{7,5},{8,10},{9,11},{10,... | collective-permute-start | bytes 196616 | tf_op jit(solution)/shard_map/ppermute | solution.py:195
  172.6 3.6 %collective-permute-start.34 = (bf16[64,512]{1,0:T(8,128)(2,1)S(1)}, bf16[64,512]{1,0:T(8,128)(2,1)S(1)}, u32[]{:S(2)}, u32[]{:S(2)}) collective-permute-start(bf16[64,512]{1,0:T(8,128)(2,1)S(1)} %get-tuple-element.76.refs_0_), channel_id=1, source_target_pairs={{0,1},{1,0},{2,3},{3,2},{4,5},{5,4},{6,7},{7,6},{8,9},{9,8},{10,11... | collective-permute-start | bytes 196616 | tf_op jit(solution)/shard_map/ppermute | solution.py:195
  (6 other events, 10.0 us)

commit v2 on v1

v2 whole, which is shorter than its diff:
```python
import functools

import jax
import jax.numpy as jnp
from jax import lax
from jax.experimental import pallas as pl
from jax.experimental.pallas import tpu as pltpu
from jax.sharding import PartitionSpec as P

POWER = 4
MIXING = 1.0 / 3.0
LANES = 128
MIB = 1024 * 1024
F32 = jnp.float32
BF16 = jnp.bfloat16
HIGHEST = lax.Precision.HIGHEST
VMEM = pl.BlockSpec(memory_space=pltpu.VMEM)
SMEM = pl.BlockSpec(memory_space=pltpu.SMEM)
HBM = pl.BlockSpec(memory_space=pl.ANY)


def kernel_call(body, outs, name, *operands, scratch=(), mib=8, flops=0, moved=0):
    specs = []
    for operand in operands:
        specs.append(SMEM if operand.dtype == jnp.int32 else VMEM)
    return pl.pallas_call(
        body,
        out_shape=outs,
        in_specs=specs,
        out_specs=jax.tree.map(lambda _: VMEM, outs),
        scratch_shapes=list(scratch),
        compiler_params=pltpu.CompilerParams(vmem_limit_bytes=mib * MIB),
        cost_estimate=pl.CostEstimate(flops=flops, bytes_accessed=moved, transcendentals=0),
        name=name,
    )(*operands)


def out(shape, dtype):
    return jax.ShapeDtypeStruct(shape, dtype)


def hold_kernel(source, held, turned, sems):
    tile = source.shape[0] // sems.shape[0]
    spans = [slice(i * tile, (i + 1) * tile) for i in range(sems.shape[0])]
    copies = [
        pltpu.make_async_copy(source.at[span, :], held.at[span, :], sems.at[i])
        for i, span in enumerate(spans)
    ]
    for copy in copies:
        copy.start()
    for copy, span in zip(copies, spans):
        copy.wait()
        turned[:, span] = held[span, :].T


def hold(weight):
    rows, wid = weight.shape
    return pl.pallas_call(
        hold_kernel,
        out_shape=(pltpu.VMEM((rows, wid), weight.dtype), pltpu.VMEM((wid, rows), weight.dtype)),
        in_specs=[HBM],
        out_specs=(VMEM, VMEM),
        scratch_shapes=[pltpu.SemaphoreType.DMA((max(1, rows // 256),))],
        compiler_params=pltpu.CompilerParams(vmem_limit_bytes=32 * MIB),
        cost_estimate=pl.CostEstimate(flops=0, bytes_accessed=2 * rows * wid, transcendentals=0),
        name="hold",
    )(weight)


def project(factor, turned, even, odd):
    rank = even.shape[0]
    product = jnp.dot(factor, turned[...], preferred_element_type=F32)
    even[...] = product[:rank]
    odd[...] = product[rank:]


def first_kernel(place, own, prior, turned, even, odd, factor):
    rank = own.shape[0]
    parity = place[1]
    factor[pl.ds(pl.multiple_of(parity * rank, rank), rank), :] = own[...]
    factor[pl.ds(pl.multiple_of((1 - parity) * rank, rank), rank), :] = prior[...]
    project(factor[...], turned, even, odd)


def gathered(place, pieces, factor):
    width = pieces[0].shape[1]
    for offset, piece in enumerate(pieces):
        start = pl.multiple_of(jnp.bitwise_xor(place[0], offset) * width, width)
        factor[:, pl.ds(start, width)] = piece[...]


def next_kernel(place, *refs):
    *pieces, turned, even, odd, factor = refs
    gathered(place, pieces, factor)
    project(factor[...], turned, even, odd)


def half_product(wanted, slices, both, weight, result):
    rank2 = both.shape[0] // 2
    width = weight.shape[1] // slices
    for i in range(slices // 2):
        start = pl.multiple_of((2 * i + wanted) * width, width)
        product = jnp.dot(both[...], weight[:, pl.ds(start, width)], preferred_element_type=F32)
        result[:, i * width : (i + 1) * width] = product[:rank2] + product[rank2:]


def back_send_kernel(slices, place, even, odd, even_other, odd_other, weight, both, send):
    rank = even.shape[0]
    for slot, (mine, theirs) in enumerate(((even, even_other), (odd, odd_other))):
        raw = mine[...] - theirs[...]
        high = raw.astype(BF16)
        both[slot * rank : (slot + 1) * rank, :] = high
        both[(2 + slot) * rank : (3 + slot) * rank, :] = (raw - high.astype(F32)).astype(BF16)
    half_product(1 - jnp.bitwise_and(place[0], 1), slices, both, weight, send)
    parts = lax.dot_general(
        both[...], both[...], (((1,), (1,)), ((), ())), preferred_element_type=F32
    )
    parts = parts[: 2 * rank] + parts[2 * rank :]
    parts = parts[:, : 2 * rank] + parts[:, 2 * rank :]
    gram = jnp.concatenate([parts[:rank, :rank], parts[rank:, rank:]], axis=0)
    send[:, -LANES:] = jnp.concatenate([gram, jnp.zeros((2 * rank, LANES - rank), F32)], axis=1)


def back_keep_kernel(slices, place, both, weight, keep):
    half_product(jnp.bitwise_and(place[0], 1), slices, both, weight, keep)


def chosen(place, bit):
    return jnp.bitwise_and(lax.div(place[0], jnp.int32(bit)), 1)


def merge_kernel(bit, slices, place, held, held_gram, came, keep, gram, send):
    width = held.shape[1] // slices
    mine = chosen(place, bit)
    for i in range(slices // 2):
        kept = pl.ds(pl.multiple_of((2 * i + mine) * width, width), width)
        sent = pl.ds(pl.multiple_of((2 * i + 1 - mine) * width, width), width)
        keep[:, i * width : (i + 1) * width] = held[:, kept] + came[:, kept]
        send[:, i * width : (i + 1) * width] = held[:, sent] + came[:, sent]
    total = held_gram[:, -LANES:] + came[:, -LANES:]
    gram[...] = total
    send[:, -LANES:] = total


def part_kernel(bit, place, held, held_gram, came, even, odd, even_sent, odd_sent, gram, send):
    rank, width = even.shape
    mine = chosen(place, bit)
    kept = pl.ds(pl.multiple_of(mine * width, width), width)
    sent = pl.ds(pl.multiple_of((1 - mine) * width, width), width)
    even[...] = held[:rank, kept] + came[:rank, kept]
    odd[...] = held[rank:, kept] + came[rank:, kept]
    leaving = held[:, sent] + came[:, sent]
    even_sent[...] = leaving[:rank]
    odd_sent[...] = leaving[rank:]
    send[:, :width] = leaving
    total = held_gram[:, -LANES:] + came[:, -LANES:]
    gram[...] = total
    send[:, width:] = total


def inverse_kernel(gram, came, inverse):
    rank = gram.shape[0] // 2
    shape = (2, rank, LANES)
    lane = lax.broadcasted_iota(jnp.int32, shape, 2)
    row = lax.broadcasted_iota(jnp.int32, shape, 1)
    work = (gram[...] + came[:, -LANES:]).reshape(shape)
    work = jnp.where(lane < rank, work, jnp.where(lane - rank == row, 1.0, 0.0))
    for k in range(rank):
        pivot = work[:, k : k + 1, :]
        scaled = pivot / pivot[:, :, k : k + 1]
        column = jnp.where(row[:, :, :1] > k, work[:, :, k : k + 1], 0.0)
        work = work - column * scaled
    diagonal = jnp.sum(jnp.where(lane == row, work, 0.0), axis=2, keepdims=True)
    work = work / jnp.sqrt(diagonal)
    inverse[...] = work.reshape(2 * rank, LANES)[:, rank : 2 * rank]


def normalised(inverse, even, odd):
    rank = even.shape[0]
    return jnp.concatenate(
        [
            jnp.dot(inverse[:rank, :], even, precision=HIGHEST, preferred_element_type=F32),
            jnp.dot(inverse[rank:, :], odd, precision=HIGHEST, preferred_element_type=F32),
        ],
        axis=0,
    )


def summed(inverse, came, even, odd, even_pair, odd_pair, even_far, odd_far):
    rank, width = even.shape
    even_sum = (even[...] + came[:rank, :width]) + (even_pair[...] + even_far[...])
    odd_sum = (odd[...] + came[rank:, :width]) + (odd_pair[...] + odd_far[...])
    return normalised(inverse[...], even_sum, odd_sum)


def round_kernel(*refs):
    *sums, rounded = refs
    rounded[...] = summed(*sums).astype(BF16)


def final_kernel(place, *refs):
    *sums, rounded, own, value = refs
    value[...] = summed(*sums)
    rounded[...] = value[...].astype(BF16)
    rank = own.shape[0]
    own[...] = value[pl.ds(pl.multiple_of(place[1] * rank, rank), rank), :]


def basis_kernel(inverse, both, columns):
    rank2 = both.shape[0] // 2
    raw = both[:rank2, :].astype(F32) + both[rank2:, :].astype(F32)
    basis = normalised(inverse[...], raw[: rank2 // 2], raw[rank2 // 2 :])
    columns[...] = basis.T.astype(BF16)


def update_kernel(place, columns, *refs):
    *pieces, weight, result, factor, made, sems = refs
    gathered(place, pieces, factor)
    tile = made.shape[0] // sems.shape[0]
    copies = []
    for i in range(sems.shape[0]):
        span = slice(i * tile, (i + 1) * tile)
        delta = jnp.dot(columns[span, :], factor[...], preferred_element_type=F32)
        made[span, :] = (weight[span, :].astype(F32) - MIXING * delta).astype(BF16)
        copy = pltpu.make_async_copy(made.at[span, :], result.at[span, :], sems.at[i])
        copy.start()
        copies.append(copy)
    for copy in copies:
        copy.wait()


def on_device(weights, warm_factor):
    peers = lax.axis_size("blk")
    shards = lax.axis_size("shard")
    shard = lax.axis_index("shard")
    parity = lax.rem(lax.axis_index("blk"), 2)
    place = jnp.stack([shard, parity]).astype(jnp.int32)
    bits = [1 << i for i in range(shards.bit_length() - 1)]
    last = bits[-1]
    partner = {
        0: [i + 1 if i % 2 == 0 else i - 1 for i in range(peers)],
        1: [(i + 1) % peers if i % 2 else (i - 1) % peers for i in range(peers)],
    }

    def across(value, bit):
        return lax.ppermute(value, "shard", [(i, i ^ bit) for i in range(shards)])

    def paired(value, slot):
        return lax.ppermute(value, "blk", list(enumerate(partner[slot])))

    def far(value, slot):
        pairs = [
            (i * shards + j, k * shards + (j ^ last))
            for i, k in enumerate(partner[slot])
            for j in range(shards)
        ]
        return lax.ppermute(value, ("blk", "shard"), pairs)

    own = warm_factor[0].astype(BF16)
    rank, wid = own.shape
    prior = lax.ppermute(own, "blk", [(i, (i + 1) % peers) for i in range(peers)])
    weight, turned = hold(weights[0])
    rows = weight.shape[0]
    width = wid // shards
    factor_scratch = [pltpu.VMEM((2 * rank, wid), BF16)]
    product_outs = (out((rank, rows), F32), out((rank, rows), F32))
    full_cost = dict(flops=4 * rank * rows * wid, moved=rows * wid * 2)
    gram_out = out((2 * rank, LANES), F32)
    piece = out((rank, width), F32)

    products = kernel_call(
        first_kernel, product_outs, "first", place, own, prior, turned,
        scratch=factor_scratch, mib=8, **full_cost,
    )
    for iteration in range(POWER):
        even, odd = products
        even_other = paired(even, 0)
        odd_other = paired(odd, 1)
        slices = shards
        half = slices // 2 * width
        both, send = kernel_call(
            functools.partial(back_send_kernel, slices),
            (out((4 * rank, rows), BF16), out((2 * rank, half + LANES), F32)), "back_send",
            place, even, odd, even_other, odd_other, weight, mib=8, **full_cost,
        )
        keep = kernel_call(
            functools.partial(back_keep_kernel, slices), out((2 * rank, half), F32), "back_keep",
            place, both, weight, mib=8, **full_cost,
        )
        gram = send
        for bit in bits[:-1]:
            came = across(send, bit)
            slices //= 2
            if 2 * bit == last:
                even_sum, odd_sum, even_sent, odd_sent, gram, send = kernel_call(
                    functools.partial(part_kernel, last),
                    (piece, piece, piece, piece, gram_out, out((2 * rank, width + LANES), F32)),
                    "part", place, keep, gram, came,
                )
                break
            half = slices // 2 * width
            keep, gram, send = kernel_call(
                functools.partial(merge_kernel, 2 * bit, slices),
                (out((2 * rank, half), F32), gram_out, out((2 * rank, half + LANES), F32)),
                "merge", place, keep, gram, came,
            )
        came = across(send, last)
        sums = (
            came, even_sum, odd_sum, paired(even_sum, 0), paired(odd_sum, 1),
            far(even_sent, 0), far(odd_sent, 1),
        )
        inverse = kernel_call(
            inverse_kernel, out((2 * rank, rank), F32), "inverse", gram, came,
            flops=1000000, moved=8 * MIB,
        )
        rounded_out = out((2 * rank, width), BF16)
        if iteration < POWER - 1:
            rounded = kernel_call(round_kernel, rounded_out, "round", inverse, *sums)
        else:
            columns = kernel_call(
                basis_kernel, out((rows, 2 * rank), BF16), "basis", inverse, both,
                mib=8, flops=8 * rank * rank * rows, moved=2 * MIB,
            )
            rounded, new_factor = kernel_call(
                final_kernel, (rounded_out, piece), "final", place, inverse, *sums,
                scratch=[pltpu.VMEM((2 * rank, width), F32)],
            )
        pieces = {0: rounded}
        for bit in reversed(bits):
            for offset in list(pieces):
                pieces[offset ^ bit] = across(pieces[offset], bit)
        pieces = [pieces[offset] for offset in range(shards)]
        if iteration < POWER - 1:
            products = kernel_call(
                next_kernel, product_outs, "next", place, *pieces, turned,
                scratch=factor_scratch, mib=8, **full_cost,
            )
    new_weight = pl.pallas_call(
        update_kernel,
        out_shape=out((rows, wid), BF16),
        in_specs=[SMEM] + [VMEM] * (len(pieces) + 2),
        out_specs=HBM,
        scratch_shapes=factor_scratch
        + [pltpu.VMEM((rows, wid), BF16), pltpu.SemaphoreType.DMA((max(1, rows // 256),))],
        compiler_params=pltpu.CompilerParams(vmem_limit_bytes=16 * MIB),
        cost_estimate=pl.CostEstimate(
            flops=4 * rank * rows * wid, bytes_accessed=2 * rows * wid, transcendentals=0
        ),
        name="update",
    )(place, columns, *pieces, weight)
    return (new_weight[None], new_factor[None])


def solution(mesh):
    placed = (P("blk", "shard", None), P("blk", None, None))
    return jax.shard_map(
        on_device,
        mesh=mesh,
        in_specs=placed,
        out_specs=(P("blk", "shard", None), P("blk", None, "shard")),
        check_vma=False,
    )
```

time: 184 us -> 168 us (0.913)
  waiting for transfers between devices: 95.2 us -> 74 us
  starting transfers between devices: 37 us -> 46.6 us
  local copies, waits for them, and re-layouts: 3.38 us -> 0 us
    ppermute x36 -> x44, waiting for transfers between devices: 92.7 us -> 71.6 us  [the longest x16 47.2 us: paired(): return lax.ppermute(value, 'blk', list(enumerate(partner[slot])))]
    ppermute x36 -> x44, starting transfers between devices: 33.9 us -> 43.6 us  [the longest x16 20.2 us: paired(): return lax.ppermute(value, 'blk', list(enumerate(partner[slot])))]
    unnamed x2 -> x0, local copies, waits for them, and re-layouts: 3.38 us -> none
    pallas_call x25, Pallas kernels: 38.9 us -> 36.6 us  [kernel_call(): pl.pallas_call(body, out_shape=outs, in_specs=specs, out_specs=jax.tree.m...]
  transfers between devices with their start and end apart: 37 -> 45, of which waited for: 25 -> 26; matrix products, arithmetic and copies ran while one was open for 0% -> 0% of each run, Pallas kernels for 7% -> 13%
where the time goes in v2:
time: 168 us
  waiting for transfers between devices  74 us (44%)
  starting transfers between devices  46.6 us (28%)
  Pallas kernels  45.1 us (27%)
    ppermute x16, waiting for transfers between devices, paired(): return lax.ppermute(value, 'blk', list(enumerate(partner[slot])))  47.2 us
    pallas_call x25, Pallas kernels, kernel_call(): pl.pallas_call(body, out_shape=outs, in_specs=specs, out_specs=jax.tree.m...  36.6 us
    ppermute x20, waiting for transfers between devices, across(): return lax.ppermute(value, 'shard', [(i, i ^ bit) for i in range(shards)])  24.4 us
    ppermute x16, starting transfers between devices, paired(): return lax.ppermute(value, 'blk', list(enumerate(partner[slot])))  20.2 us
    ppermute x8, starting transfers between devices, far(): return lax.ppermute(value, ('blk', 'shard'), pairs)  16.2 us
    ppermute x20, starting transfers between devices, across(): return lax.ppermute(value, 'shard', [(i, i ^ bit) for i in range(shards)])  7.14 us
    pallas_call x1, Pallas kernels, on_device(): pl.pallas_call(update_kernel, out_shape=out((rows, wid), BF16), in_specs=...  4.34 us
    pallas_call x1, Pallas kernels, hold(): pl.pallas_call(hold_kernel, out_shape=(pltpu.VMEM((rows, wid), weight.dty...  4.11 us
  transfers between devices with their start and end apart: 45, of which 26 were waited for; matrix products, arithmetic and copies ran while one was open for 0% of the time, Pallas kernels for 13%

profile of v2, /device:TPU:0, one launch (start us, length us, event | category | flops | bytes accessed | tf_op | source)
XLA Modules:
  0.0 167.8 jit_solution(4724952581989463993)
XLA Ops:
  1.6 3.0 %collective-permute-start = (bf16[32,2048]{1,0:T(8,128)(2,1)S(1)}, bf16[32,2048]{1,0:T(8,128)(2,1)S(1)}, u32[]{:S(2)}, u32[]{:S(2)}) collective-permute-start(bf16[32,2048]{1,0:T(8,128)(2,1)S(1)} %convert_bitcast_fusion.own), channel_id=1, source_target_pairs={{0,4},{4,8},{8,12},{12,16},{16,20},{20,24},{24,28},{28,0},{1,5},{5... | collective-permute-start | bytes 393224 | tf_op jit(solution)/shard_map/ppermute | solution.py:261
  4.6 4.1 %hold.1 = (bf16[2048,2048]{1,0:T(8,128)(2,1)S(1)}, bf16[2048,2048]{1,0:T(8,128)(2,1)S(1)}) custom-call(bf16[2048,2048]{1,0:T(8,128)(2,1)} %bitcast.8), custom_call_target="tpu_custom_call" | custom-call | bytes 8388608 | tf_op jit(solution)/shard_map/hold/pallas_call | solution.py:58
  8.8 2.3 %collective-permute-done.prior = bf16[32,2048]{1,0:T(8,128)(2,1)S(1)} collective-permute-done((bf16[32,2048]{1,0:T(8,128)(2,1)S(1)}, bf16[32,2048]{1,0:T(8,128)(2,1)S(1)}, u32[]{:S(2)}, u32[]{:S(2)}) %collective-permute-start) | collective-permute-done | bytes 131104 | tf_op jit(solution)/shard_map/ppermute | solution.py:261
  11.2 2.1 %first.1 = (f32[32,2048]{1,0:T(8,128)S(1)}, f32[32,2048]{1,0:T(8,128)S(1)}) custom-call(s32[2]{0:T(128)S(1)} %pad_add_fusion.place, bf16[32,2048]{1,0:T(8,128)(2,1)S(1)} %convert_bitcast_fusion.own, bf16[32,2048]{1,0:T(8,128)(2,1)S(1)} %collective-permute-done.prior, bf16[2048,2048]{1,0:T(8,128)(2,1)S(1)} %get-tuple-element.46.turned.refs_4_), custom_call_target="tpu_custom_call" | custom-call | flops 536870912 | bytes 8388608 | tf_op jit(solution)/shard_map/first/pallas_call | solution.py:26
  13.3 3.1 %collective-permute-start.2 = (f32[32,2048]{1,0:T(8,128)S(1)}, f32[32,2048]{1,0:T(8,128)S(1)}, u32[]{:S(2)}, u32[]{:S(2)}) collective-permute-start(f32[32,2048]{1,0:T(8,128)S(1)} %get-tuple-element.48.odd), channel_id=1, source_target_pairs={{0,28},{4,8},{8,4},{12,16},{16,12},{20,24},{24,20},{28,0},{1,29},{... | collective-permute-start | bytes 786440 | tf_op jit(solution)/shard_map/ppermute | solution.py:249
  16.5 10.0 %collective-permute-done.1.even_other = f32[32,2048]{1,0:T(8,128)S(1)} collective-permute-done((f32[32,2048]{1,0:T(8,128)S(1)}, f32[32,2048]{1,0:T(8,128)S(1)}, u32[]{:S(2)}, u32[]{:S(2)}) %collective-permute-start.1) | collective-permute-done | bytes 262176 | tf_op jit(solution)/shard_map/ppermute | solution.py:249
  32.1 3.6 %collective-permute-start.8 = (f32[32,512]{1,0:T(8,128)S(1)}, f32[32,512]{1,0:T(8,128)S(1)}, u32[]{:S(2)}, u32[]{:S(2)}) collective-permute-start(f32[32,512]{1,0:T(8,128)S(1)} %get-tuple-element.57), channel_id=1, source_target_pairs={{0,30},{1,31},{2,28},{3,29},{4,10},{5,11},{6,8},{7,9},{8,6},{9,7},... | collective-permute-start | bytes 196616 | tf_op jit(solution)/shard_map/ppermute | solution.py:257
  35.7 1.9 %collective-permute-start.6 = (f32[32,512]{1,0:T(8,128)S(1)}, f32[32,512]{1,0:T(8,128)S(1)}, u32[]{:S(2)}, u32[]{:S(2)}) collective-permute-start(f32[32,512]{1,0:T(8,128)S(1)} %get-tuple-element.55.refs_3_), channel_id=1, source_target_pairs={{0,28},{4,8},{8,4},{12,16},{16,12},{20,24},{24,20},{28,0},{1,29},{... | collective-permute-start | bytes 196616 | tf_op jit(solution)/shard_map/ppermute | solution.py:249
  38.8 2.8 %inverse.4.refs_0_ = f32[64,32]{1,0:T(8,128)S(1)} custom-call(f32[64,128]{1,0:T(8,128)S(1)} %get-tuple-element.52.gram, f32[64,640]{1,0:T(8,128)S(1)} %collective-permute-done.4.came.refs_1_), custom_call_target="tpu_custom_call" | custom-call | flops 1000000 | bytes 8388608 | tf_op jit(solution)/shard_map/inverse/pallas_call | solution.py:26
  43.5 3.7 %collective-permute-done.10.refs_2_ = bf16[64,512]{1,0:T(8,128)(2,1)S(1)} collective-permute-done((bf16[64,512]{1,0:T(8,128)(2,1)S(1)}, bf16[64,512]{1,0:T(8,128)(2,1)S(1)}, u32[]{:S(2)}, u32[]{:S(2)}) %collective-permute-start.10) | collective-permute-done | bytes 65568 | tf_op jit(solution)/shard_map/ppermute | solution.py:246
  48.5 2.1 %next.3 = (f32[32,2048]{1,0:T(8,128)S(1)}, f32[32,2048]{1,0:T(8,128)S(1)}) custom-call(s32[2]{0:T(128)S(1)} %pad_add_fusion.place, bf16[64,512]{1,0:T(8,128)(2,1)S(1)} %round.3.refs_0_, bf16[64,512]{1,0:T(8,128)(2,1)S(1)} %collective-permute-done.9.refs_1_, bf16[64,512]{1,0:T(8,128)(2,1)S(1)} %collective-permute-done.10.refs_2_, ...), custom_call_target="tpu_custom_call" | custom-call | flops 536870912 | bytes 8388608 | tf_op jit(solution)/shard_map/next/pallas_call | solution.py:26
  52.7 11.9 %collective-permute-done.12.even_other = f32[32,2048]{1,0:T(8,128)S(1)} collective-permute-done((f32[32,2048]{1,0:T(8,128)S(1)}, f32[32,2048]{1,0:T(8,128)S(1)}, u32[]{:S(2)}, u32[]{:S(2)}) %collective-permute-start.12) | collective-permute-done | bytes 262176 | tf_op jit(solution)/shard_map/ppermute | solution.py:249
  70.7 2.2 %collective-permute-start.19 = (f32[32,512]{1,0:T(8,128)S(1)}, f32[32,512]{1,0:T(8,128)S(1)}, u32[]{:S(2)}, u32[]{:S(2)}) collective-permute-start(f32[32,512]{1,0:T(8,128)S(1)} %get-tuple-element.67), channel_id=1, source_target_pairs={{0,30},{1,31},{2,28},{3,29},{4,10},{5,11},{6,8},{7,9},{8,6},{9,7},... | collective-permute-start | bytes 196616 | tf_op jit(solution)/shard_map/ppermute | solution.py:257
  72.9 2.8 %collective-permute-start.17 = (f32[32,512]{1,0:T(8,128)S(1)}, f32[32,512]{1,0:T(8,128)S(1)}, u32[]{:S(2)}, u32[]{:S(2)}) collective-permute-start(f32[32,512]{1,0:T(8,128)S(1)} %get-tuple-element.65.refs_3_), channel_id=1, source_target_pairs={{0,28},{4,8},{8,4},{12,16},{16,12},{20,24},{24,20},{28,0},{1,29},{... | collective-permute-start | bytes 196616 | tf_op jit(solution)/shard_map/ppermute | solution.py:249
  77.0 2.8 %inverse.5.refs_0_ = f32[64,32]{1,0:T(8,128)S(1)} custom-call(f32[64,128]{1,0:T(8,128)S(1)} %get-tuple-element.62.gram, f32[64,640]{1,0:T(8,128)S(1)} %collective-permute-done.15.came.refs_1_), custom_call_target="tpu_custom_call" | custom-call | flops 1000000 | bytes 8388608 | tf_op jit(solution)/shard_map/inverse/pallas_call | solution.py:26
  81.3 3.4 %collective-permute-done.21.refs_2_ = bf16[64,512]{1,0:T(8,128)(2,1)S(1)} collective-permute-done((bf16[64,512]{1,0:T(8,128)(2,1)S(1)}, bf16[64,512]{1,0:T(8,128)(2,1)S(1)}, u32[]{:S(2)}, u32[]{:S(2)}) %collective-permute-start.21) | collective-permute-done | bytes 65568 | tf_op jit(solution)/shard_map/ppermute | solution.py:246
  86.0 2.1 %next.4 = (f32[32,2048]{1,0:T(8,128)S(1)}, f32[32,2048]{1,0:T(8,128)S(1)}) custom-call(s32[2]{0:T(128)S(1)} %pad_add_fusion.place, bf16[64,512]{1,0:T(8,128)(2,1)S(1)} %round.4.refs_0_, bf16[64,512]{1,0:T(8,128)(2,1)S(1)} %collective-permute-done.20.refs_1_, bf16[64,512]{1,0:T(8,128)(2,1)S(1)} %collective-permute-done.21.refs_2_, ...), custom_call_target="tpu_custom_call" | custom-call | flops 536870912 | bytes 8388608 | tf_op jit(solution)/shard_map/next/pallas_call | solution.py:26
  88.8 2.5 %collective-permute-start.24 = (f32[32,2048]{1,0:T(8,128)S(1)}, f32[32,2048]{1,0:T(8,128)S(1)}, u32[]{:S(2)}, u32[]{:S(2)}) collective-permute-start(f32[32,2048]{1,0:T(8,128)S(1)} %get-tuple-element.69.odd), channel_id=1, source_target_pairs={{0,28},{4,8},{8,4},{12,16},{16,12},{20,24},{24,20},{28,0},{1,29},{... | collective-permute-start | bytes 786440 | tf_op jit(solution)/shard_map/ppermute | solution.py:249
  91.4 10.8 %collective-permute-done.23.even_other = f32[32,2048]{1,0:T(8,128)S(1)} collective-permute-done((f32[32,2048]{1,0:T(8,128)S(1)}, f32[32,2048]{1,0:T(8,128)S(1)}, u32[]{:S(2)}, u32[]{:S(2)}) %collective-permute-start.23) | collective-permute-done | bytes 262176 | tf_op jit(solution)/shard_map/ppermute | solution.py:249
  102.2 1.8 %back_send.6 = (bf16[128,2048]{1,0:T(8,128)(2,1)S(1)}, f32[64,1152]{1,0:T(8,128)S(1)}) custom-call(s32[2]{0:T(128)S(1)} %pad_add_fusion.place, f32[32,2048]{1,0:T(8,128)S(1)} %get-tuple-element.68.even, f32[32,2048]{1,0:T(8,128)S(1)} %get-tuple-element.69.odd, f32[32,2048]{1,0:T(8,128)S(1)} %collective-permute-done.23.even_other, ...), custom_call_target="tpu_custom_call" | custom-call | flops 536870912 | bytes 8388608 | tf_op jit(solution)/shard_map/back_send/pallas_call | solution.py:26
  108.4 3.1 %collective-permute-start.30 = (f32[32,512]{1,0:T(8,128)S(1)}, f32[32,512]{1,0:T(8,128)S(1)}, u32[]{:S(2)}, u32[]{:S(2)}) collective-permute-start(f32[32,512]{1,0:T(8,128)S(1)} %get-tuple-element.77), channel_id=1, source_target_pairs={{0,30},{1,31},{2,28},{3,29},{4,10},{5,11},{6,8},{7,9},{8,6},{9,7},... | collective-permute-start | bytes 196616 | tf_op jit(solution)/shard_map/ppermute | solution.py:257
  111.5 1.8 %collective-permute-start.28 = (f32[32,512]{1,0:T(8,128)S(1)}, f32[32,512]{1,0:T(8,128)S(1)}, u32[]{:S(2)}, u32[]{:S(2)}) collective-permute-start(f32[32,512]{1,0:T(8,128)S(1)} %get-tuple-element.75.refs_3_), channel_id=1, source_target_pairs={{0,28},{4,8},{8,4},{12,16},{16,12},{20,24},{24,20},{28,0},{1,29},{... | collective-permute-start | bytes 196616 | tf_op jit(solution)/shard_map/ppermute | solution.py:249
  114.7 2.8 %inverse.6.refs_0_ = f32[64,32]{1,0:T(8,128)S(1)} custom-call(f32[64,128]{1,0:T(8,128)S(1)} %get-tuple-element.72.gram, f32[64,640]{1,0:T(8,128)S(1)} %collective-permute-done.26.came.refs_1_), custom_call_target="tpu_custom_call" | custom-call | flops 1000000 | bytes 8388608 | tf_op jit(solution)/shard_map/inverse/pallas_call | solution.py:26
  119.6 3.4 %collective-permute-done.32.refs_2_ = bf16[64,512]{1,0:T(8,128)(2,1)S(1)} collective-permute-done((bf16[64,512]{1,0:T(8,128)(2,1)S(1)}, bf16[64,512]{1,0:T(8,128)(2,1)S(1)}, u32[]{:S(2)}, u32[]{:S(2)}) %collective-permute-start.32) | collective-permute-done | bytes 65568 | tf_op jit(solution)/shard_map/ppermute | solution.py:246
  124.3 2.1 %next.5 = (f32[32,2048]{1,0:T(8,128)S(1)}, f32[32,2048]{1,0:T(8,128)S(1)}) custom-call(s32[2]{0:T(128)S(1)} %pad_add_fusion.place, bf16[64,512]{1,0:T(8,128)(2,1)S(1)} %round.5.refs_0_, bf16[64,512]{1,0:T(8,128)(2,1)S(1)} %collective-permute-done.31.refs_1_, bf16[64,512]{1,0:T(8,128)(2,1)S(1)} %collective-permute-done.32.refs_2_, ...), custom_call_target="tpu_custom_call" | custom-call | flops 536870912 | bytes 8388608 | tf_op jit(solution)/shard_map/next/pallas_call | solution.py:26
  127.2 2.0 %collective-permute-start.35 = (f32[32,2048]{1,0:T(8,128)S(1)}, f32[32,2048]{1,0:T(8,128)S(1)}, u32[]{:S(2)}, u32[]{:S(2)}) collective-permute-start(f32[32,2048]{1,0:T(8,128)S(1)} %get-tuple-element.79.odd), channel_id=1, source_target_pairs={{0,28},{4,8},{8,4},{12,16},{16,12},{20,24},{24,20},{28,0},{1,29},{... | collective-permute-start | bytes 786440 | tf_op jit(solution)/shard_map/ppermute | solution.py:249
  129.1 11.3 %collective-permute-done.34.even_other = f32[32,2048]{1,0:T(8,128)S(1)} collective-permute-done((f32[32,2048]{1,0:T(8,128)S(1)}, f32[32,2048]{1,0:T(8,128)S(1)}, u32[]{:S(2)}, u32[]{:S(2)}) %collective-permute-start.34) | collective-permute-done | bytes 262176 | tf_op jit(solution)/shard_map/ppermute | solution.py:249
  146.5 2.7 %collective-permute-start.41 = (f32[32,512]{1,0:T(8,128)S(1)}, f32[32,512]{1,0:T(8,128)S(1)}, u32[]{:S(2)}, u32[]{:S(2)}) collective-permute-start(f32[32,512]{1,0:T(8,128)S(1)} %get-tuple-element.87), channel_id=1, source_target_pairs={{0,30},{1,31},{2,28},{3,29},{4,10},{5,11},{6,8},{7,9},{8,6},{9,7},... | collective-permute-start | bytes 196616 | tf_op jit(solution)/shard_map/ppermute | solution.py:257
  149.2 2.3 %collective-permute-start.39 = (f32[32,512]{1,0:T(8,128)S(1)}, f32[32,512]{1,0:T(8,128)S(1)}, u32[]{:S(2)}, u32[]{:S(2)}) collective-permute-start(f32[32,512]{1,0:T(8,128)S(1)} %get-tuple-element.85.refs_3_), channel_id=1, source_target_pairs={{0,28},{4,8},{8,4},{12,16},{16,12},{20,24},{24,20},{28,0},{1,29},{... | collective-permute-start | bytes 196616 | tf_op jit(solution)/shard_map/ppermute | solution.py:249
  152.8 2.8 %inverse.7.refs_0_ = f32[64,32]{1,0:T(8,128)S(1)} custom-call(f32[64,128]{1,0:T(8,128)S(1)} %get-tuple-element.82.gram, f32[64,640]{1,0:T(8,128)S(1)} %collective-permute-done.37.came.refs_1_), custom_call_target="tpu_custom_call" | custom-call | flops 1000000 | bytes 8388608 | tf_op jit(solution)/shard_map/inverse/pallas_call | solution.py:26
  158.5 3.5 %collective-permute-done.43.refs_2_ = bf16[64,512]{1,0:T(8,128)(2,1)S(1)} collective-permute-done((bf16[64,512]{1,0:T(8,128)(2,1)S(1)}, bf16[64,512]{1,0:T(8,128)(2,1)S(1)}, u32[]{:S(2)}, u32[]{:S(2)}) %collective-permute-start.43) | collective-permute-done | bytes 65568 | tf_op jit(solution)/shard_map/ppermute | solution.py:246
  163.3 4.3 %update.1 = bf16[2048,2048]{1,0:T(8,128)(2,1)} custom-call(s32[2]{0:T(128)S(1)} %pad_add_fusion.place, bf16[2048,64]{1,0:T(8,128)(2,1)S(1)} %basis.1.columns, bf16[64,512]{1,0:T(8,128)(2,1)S(1)} %get-tuple-element.88.refs_0_, bf16[64,512]{1,0:T(8,128)(2,1)S(1)} %collective-permute-done.42.refs_1_, bf16[64,512]{1,0:T(8,128)(2,1)S(1)} %collective-permute-done.43.refs_2_, ...), custom_call_target="tpu_custom_call" | custom-call | flops 536870912 | bytes 8388608 | tf_op jit(solution)/shard_map/update/pallas_call | solution.py:338
  (87 shorter events, 45.5 us)
Async XLA Ops:
  1.6 9.6 %collective-permute-start = (bf16[32,2048]{1,0:T(8,128)(2,1)S(1)}, bf16[32,2048]{1,0:T(8,128)(2,1)S(1)}, u32[]{:S(2)}, u32[]{:S(2)}) collective-permute-start(bf16[32,2048]{1,0:T(8,128)(2,1)S(1)} %convert_bitcast_fusion.own), channel_id=1, source_target_pairs={{0,4},{4,8},{8,12},{12,16},{16,20},{20,24},{24,28},{28,0},{1,5},{5... | collective-permute-start | bytes 393224 | tf_op jit(solution)/shard_map/ppermute | solution.py:261
  13.3 13.2 %collective-permute-start.1 = (f32[32,2048]{1,0:T(8,128)S(1)}, f32[32,2048]{1,0:T(8,128)S(1)}, u32[]{:S(2)}, u32[]{:S(2)}) collective-permute-start(f32[32,2048]{1,0:T(8,128)S(1)} %get-tuple-element.47.even), channel_id=1, source_target_pairs={{0,4},{4,0},{8,12},{12,8},{16,20},{20,16},{24,28},{28,24},{1,5},{5... | collective-permute-start | bytes 786440 | tf_op jit(solution)/shard_map/ppermute | solution.py:249
  13.3 13.1 %collective-permute-start.2 = (f32[32,2048]{1,0:T(8,128)S(1)}, f32[32,2048]{1,0:T(8,128)S(1)}, u32[]{:S(2)}, u32[]{:S(2)}) collective-permute-start(f32[32,2048]{1,0:T(8,128)S(1)} %get-tuple-element.48.odd), channel_id=1, source_target_pairs={{0,28},{4,8},{8,4},{12,16},{16,12},{20,24},{24,20},{28,0},{1,29},{... | collective-permute-start | bytes 786440 | tf_op jit(solution)/shard_map/ppermute | solution.py:249
  30.3 8.5 %collective-permute-start.4 = (f32[64,640]{1,0:T(8,128)S(1)}, f32[64,640]{1,0:T(8,128)S(1)}, u32[]{:S(2)}, u32[]{:S(2)}) collective-permute-start(f32[64,640]{1,0:T(8,128)S(1)} %get-tuple-element.53), channel_id=1, source_target_pairs={{0,2},{1,3},{2,0},{3,1},{4,6},{5,7},{6,4},{7,5},{8,10},{9,11},{10,... | collective-permute-start | bytes 491528 | tf_op jit(solution)/shard_map/ppermute | solution.py:246
  31.7 9.9 %collective-permute-start.7 = (f32[32,512]{1,0:T(8,128)S(1)}, f32[32,512]{1,0:T(8,128)S(1)}, u32[]{:S(2)}, u32[]{:S(2)}) collective-permute-start(f32[32,512]{1,0:T(8,128)S(1)} %get-tuple-element.56), channel_id=1, source_target_pairs={{0,6},{1,7},{2,4},{3,5},{4,2},{5,3},{6,0},{7,1},{8,14},{9,15},{10,... | collective-permute-start | bytes 196616 | tf_op jit(solution)/shard_map/ppermute | solution.py:257
  32.1 9.5 %collective-permute-start.8 = (f32[32,512]{1,0:T(8,128)S(1)}, f32[32,512]{1,0:T(8,128)S(1)}, u32[]{:S(2)}, u32[]{:S(2)}) collective-permute-start(f32[32,512]{1,0:T(8,128)S(1)} %get-tuple-element.57), channel_id=1, source_target_pairs={{0,30},{1,31},{2,28},{3,29},{4,10},{5,11},{6,8},{7,9},{8,6},{9,7},... | collective-permute-start | bytes 196616 | tf_op jit(solution)/shard_map/ppermute | solution.py:257
  35.7 5.8 %collective-permute-start.5 = (f32[32,512]{1,0:T(8,128)S(1)}, f32[32,512]{1,0:T(8,128)S(1)}, u32[]{:S(2)}, u32[]{:S(2)}) collective-permute-start(f32[32,512]{1,0:T(8,128)S(1)} %get-tuple-element.54.refs_2_), channel_id=1, source_target_pairs={{0,4},{4,0},{8,12},{12,8},{16,20},{20,16},{24,28},{28,24},{1,5},{5... | collective-permute-start | bytes 196616 | tf_op jit(solution)/shard_map/ppermute | solution.py:249
  35.7 7.0 %collective-permute-start.6 = (f32[32,512]{1,0:T(8,128)S(1)}, f32[32,512]{1,0:T(8,128)S(1)}, u32[]{:S(2)}, u32[]{:S(2)}) collective-permute-start(f32[32,512]{1,0:T(8,128)S(1)} %get-tuple-element.55.refs_3_), channel_id=1, source_target_pairs={{0,28},{4,8},{8,4},{12,16},{16,12},{20,24},{24,20},{28,0},{1,29},{... | collective-permute-start | bytes 196616 | tf_op jit(solution)/shard_map/ppermute | solution.py:249
  42.9 4.3 %collective-permute-start.10 = (bf16[64,512]{1,0:T(8,128)(2,1)S(1)}, bf16[64,512]{1,0:T(8,128)(2,1)S(1)}, u32[]{:S(2)}, u32[]{:S(2)}) collective-permute-start(bf16[64,512]{1,0:T(8,128)(2,1)S(1)} %round.3.refs_0_), channel_id=1, source_target_pairs={{0,2},{1,3},{2,0},{3,1},{4,6},{5,7},{6,4},{7,5},{8,10},{9,11},{10,... | collective-permute-start | bytes 196616 | tf_op jit(solution)/shard_map/ppermute | solution.py:246
  50.6 14.1 %collective-permute-start.12 = (f32[32,2048]{1,0:T(8,128)S(1)}, f32[32,2048]{1,0:T(8,128)S(1)}, u32[]{:S(2)}, u32[]{:S(2)}) collective-permute-start(f32[32,2048]{1,0:T(8,128)S(1)} %get-tuple-element.58.even), channel_id=1, source_target_pairs={{0,4},{4,0},{8,12},{12,8},{16,20},{20,16},{24,28},{28,24},{1,5},{5... | collective-permute-start | bytes 786440 | tf_op jit(solution)/shard_map/ppermute | solution.py:249
  51.3 13.4 %collective-permute-start.13 = (f32[32,2048]{1,0:T(8,128)S(1)}, f32[32,2048]{1,0:T(8,128)S(1)}, u32[]{:S(2)}, u32[]{:S(2)}) collective-permute-start(f32[32,2048]{1,0:T(8,128)S(1)} %get-tuple-element.59.odd), channel_id=1, source_target_pairs={{0,28},{4,8},{8,4},{12,16},{16,12},{20,24},{24,20},{28,0},{1,29},{... | collective-permute-start | bytes 786440 | tf_op jit(solution)/shard_map/ppermute | solution.py:249
  68.5 8.5 %collective-permute-start.15 = (f32[64,640]{1,0:T(8,128)S(1)}, f32[64,640]{1,0:T(8,128)S(1)}, u32[]{:S(2)}, u32[]{:S(2)}) collective-permute-start(f32[64,640]{1,0:T(8,128)S(1)} %get-tuple-element.63), channel_id=1, source_target_pairs={{0,2},{1,3},{2,0},{3,1},{4,6},{5,7},{6,4},{7,5},{8,10},{9,11},{10,... | collective-permute-start | bytes 491528 | tf_op jit(solution)/shard_map/ppermute | solution.py:246
  69.1 10.6 %collective-permute-start.18 = (f32[32,512]{1,0:T(8,128)S(1)}, f32[32,512]{1,0:T(8,128)S(1)}, u32[]{:S(2)}, u32[]{:S(2)}) collective-permute-start(f32[32,512]{1,0:T(8,128)S(1)} %get-tuple-element.66), channel_id=1, source_target_pairs={{0,6},{1,7},{2,4},{3,5},{4,2},{5,3},{6,0},{7,1},{8,14},{9,15},{10,... | collective-permute-start | bytes 196616 | tf_op jit(solution)/shard_map/ppermute | solution.py:257
  70.7 9.1 %collective-permute-start.19 = (f32[32,512]{1,0:T(8,128)S(1)}, f32[32,512]{1,0:T(8,128)S(1)}, u32[]{:S(2)}, u32[]{:S(2)}) collective-permute-start(f32[32,512]{1,0:T(8,128)S(1)} %get-tuple-element.67), channel_id=1, source_target_pairs={{0,30},{1,31},{2,28},{3,29},{4,10},{5,11},{6,8},{7,9},{8,6},{9,7},... | collective-permute-start | bytes 196616 | tf_op jit(solution)/shard_map/ppermute | solution.py:257
  72.8 7.3 %collective-permute-start.16 = (f32[32,512]{1,0:T(8,128)S(1)}, f32[32,512]{1,0:T(8,128)S(1)}, u32[]{:S(2)}, u32[]{:S(2)}) collective-permute-start(f32[32,512]{1,0:T(8,128)S(1)} %get-tuple-element.64.refs_2_), channel_id=1, source_target_pairs={{0,4},{4,0},{8,12},{12,8},{16,20},{20,16},{24,28},{28,24},{1,5},{5... | collective-permute-start | bytes 196616 | tf_op jit(solution)/shard_map/ppermute | solution.py:249
  72.9 7.3 %collective-permute-start.17 = (f32[32,512]{1,0:T(8,128)S(1)}, f32[32,512]{1,0:T(8,128)S(1)}, u32[]{:S(2)}, u32[]{:S(2)}) collective-permute-start(f32[32,512]{1,0:T(8,128)S(1)} %get-tuple-element.65.refs_3_), channel_id=1, source_target_pairs={{0,28},{4,8},{8,4},{12,16},{16,12},{20,24},{24,20},{28,0},{1,29},{... | collective-permute-start | bytes 196616 | tf_op jit(solution)/shard_map/ppermute | solution.py:249
  80.4 4.3 %collective-permute-start.21 = (bf16[64,512]{1,0:T(8,128)(2,1)S(1)}, bf16[64,512]{1,0:T(8,128)(2,1)S(1)}, u32[]{:S(2)}, u32[]{:S(2)}) collective-permute-start(bf16[64,512]{1,0:T(8,128)(2,1)S(1)} %round.4.refs_0_), channel_id=1, source_target_pairs={{0,2},{1,3},{2,0},{3,1},{4,6},{5,7},{6,4},{7,5},{8,10},{9,11},{10,... | collective-permute-start | bytes 196616 | tf_op jit(solution)/shard_map/ppermute | solution.py:246
  88.1 14.1 %collective-permute-start.23 = (f32[32,2048]{1,0:T(8,128)S(1)}, f32[32,2048]{1,0:T(8,128)S(1)}, u32[]{:S(2)}, u32[]{:S(2)}) collective-permute-start(f32[32,2048]{1,0:T(8,128)S(1)} %get-tuple-element.68.even), channel_id=1, source_target_pairs={{0,4},{4,0},{8,12},{12,8},{16,20},{20,16},{24,28},{28,24},{1,5},{5... | collective-permute-start | bytes 786440 | tf_op jit(solution)/shard_map/ppermute | solution.py:249
  88.8 13.3 %collective-permute-start.24 = (f32[32,2048]{1,0:T(8,128)S(1)}, f32[32,2048]{1,0:T(8,128)S(1)}, u32[]{:S(2)}, u32[]{:S(2)}) collective-permute-start(f32[32,2048]{1,0:T(8,128)S(1)} %get-tuple-element.69.odd), channel_id=1, source_target_pairs={{0,28},{4,8},{8,4},{12,16},{16,12},{20,24},{24,20},{28,0},{1,29},{... | collective-permute-start | bytes 786440 | tf_op jit(solution)/shard_map/ppermute | solution.py:249
  106.2 8.5 %collective-permute-start.26 = (f32[64,640]{1,0:T(8,128)S(1)}, f32[64,640]{1,0:T(8,128)S(1)}, u32[]{:S(2)}, u32[]{:S(2)}) collective-permute-start(f32[64,640]{1,0:T(8,128)S(1)} %get-tuple-element.73), channel_id=1, source_target_pairs={{0,2},{1,3},{2,0},{3,1},{4,6},{5,7},{6,4},{7,5},{8,10},{9,11},{10,... | collective-permute-start | bytes 491528 | tf_op jit(solution)/shard_map/ppermute | solution.py:246
  107.1 10.4 %collective-permute-start.29 = (f32[32,512]{1,0:T(8,128)S(1)}, f32[32,512]{1,0:T(8,128)S(1)}, u32[]{:S(2)}, u32[]{:S(2)}) collective-permute-start(f32[32,512]{1,0:T(8,128)S(1)} %get-tuple-element.76), channel_id=1, source_target_pairs={{0,6},{1,7},{2,4},{3,5},{4,2},{5,3},{6,0},{7,1},{8,14},{9,15},{10,... | collective-permute-start | bytes 196616 | tf_op jit(solution)/shard_map/ppermute | solution.py:257
  108.4 9.1 %collective-permute-start.30 = (f32[32,512]{1,0:T(8,128)S(1)}, f32[32,512]{1,0:T(8,128)S(1)}, u32[]{:S(2)}, u32[]{:S(2)}) collective-permute-start(f32[32,512]{1,0:T(8,128)S(1)} %get-tuple-element.77), channel_id=1, source_target_pairs={{0,30},{1,31},{2,28},{3,29},{4,10},{5,11},{6,8},{7,9},{8,6},{9,7},... | collective-permute-start | bytes 196616 | tf_op jit(solution)/shard_map/ppermute | solution.py:257
  111.5 6.1 %collective-permute-start.27 = (f32[32,512]{1,0:T(8,128)S(1)}, f32[32,512]{1,0:T(8,128)S(1)}, u32[]{:S(2)}, u32[]{:S(2)}) collective-permute-start(f32[32,512]{1,0:T(8,128)S(1)} %get-tuple-element.74.refs_2_), channel_id=1, source_target_pairs={{0,4},{4,0},{8,12},{12,8},{16,20},{20,16},{24,28},{28,24},{1,5},{5... | collective-permute-start | bytes 196616 | tf_op jit(solution)/shard_map/ppermute | solution.py:249
  111.5 7.0 %collective-permute-start.28 = (f32[32,512]{1,0:T(8,128)S(1)}, f32[32,512]{1,0:T(8,128)S(1)}, u32[]{:S(2)}, u32[]{:S(2)}) collective-permute-start(f32[32,512]{1,0:T(8,128)S(1)} %get-tuple-element.75.refs_3_), channel_id=1, source_target_pairs={{0,28},{4,8},{8,4},{12,16},{16,12},{20,24},{24,20},{28,0},{1,29},{... | collective-permute-start | bytes 196616 | tf_op jit(solution)/shard_map/ppermute | solution.py:249
  118.7 4.3 %collective-permute-start.32 = (bf16[64,512]{1,0:T(8,128)(2,1)S(1)}, bf16[64,512]{1,0:T(8,128)(2,1)S(1)}, u32[]{:S(2)}, u32[]{:S(2)}) collective-permute-start(bf16[64,512]{1,0:T(8,128)(2,1)S(1)} %round.5.refs_0_), channel_id=1, source_target_pairs={{0,2},{1,3},{2,0},{3,1},{4,6},{5,7},{6,4},{7,5},{8,10},{9,11},{10,... | collective-permute-start | bytes 196616 | tf_op jit(solution)/shard_map/ppermute | solution.py:246
  126.4 14.1 %collective-permute-start.34 = (f32[32,2048]{1,0:T(8,128)S(1)}, f32[32,2048]{1,0:T(8,128)S(1)}, u32[]{:S(2)}, u32[]{:S(2)}) collective-permute-start(f32[32,2048]{1,0:T(8,128)S(1)} %get-tuple-element.78.even), channel_id=1, source_target_pairs={{0,4},{4,0},{8,12},{12,8},{16,20},{20,16},{24,28},{28,24},{1,5},{5... | collective-permute-start | bytes 786440 | tf_op jit(solution)/shard_map/ppermute | solution.py:249
  127.2 13.3 %collective-permute-start.35 = (f32[32,2048]{1,0:T(8,128)S(1)}, f32[32,2048]{1,0:T(8,128)S(1)}, u32[]{:S(2)}, u32[]{:S(2)}) collective-permute-start(f32[32,2048]{1,0:T(8,128)S(1)} %get-tuple-element.79.odd), channel_id=1, source_target_pairs={{0,28},{4,8},{8,4},{12,16},{16,12},{20,24},{24,20},{28,0},{1,29},{... | collective-permute-start | bytes 786440 | tf_op jit(solution)/shard_map/ppermute | solution.py:249
  144.3 8.5 %collective-permute-start.37 = (f32[64,640]{1,0:T(8,128)S(1)}, f32[64,640]{1,0:T(8,128)S(1)}, u32[]{:S(2)}, u32[]{:S(2)}) collective-permute-start(f32[64,640]{1,0:T(8,128)S(1)} %get-tuple-element.83), channel_id=1, source_target_pairs={{0,2},{1,3},{2,0},{3,1},{4,6},{5,7},{6,4},{7,5},{8,10},{9,11},{10,... | collective-permute-start | bytes 491528 | tf_op jit(solution)/shard_map/ppermute | solution.py:246
  145.2 10.3 %collective-permute-start.40 = (f32[32,512]{1,0:T(8,128)S(1)}, f32[32,512]{1,0:T(8,128)S(1)}, u32[]{:S(2)}, u32[]{:S(2)}) collective-permute-start(f32[32,512]{1,0:T(8,128)S(1)} %get-tuple-element.86), channel_id=1, source_target_pairs={{0,6},{1,7},{2,4},{3,5},{4,2},{5,3},{6,0},{7,1},{8,14},{9,15},{10,... | collective-permute-start | bytes 196616 | tf_op jit(solution)/shard_map/ppermute | solution.py:257
  146.5 9.0 %collective-permute-start.41 = (f32[32,512]{1,0:T(8,128)S(1)}, f32[32,512]{1,0:T(8,128)S(1)}, u32[]{:S(2)}, u32[]{:S(2)}) collective-permute-start(f32[32,512]{1,0:T(8,128)S(1)} %get-tuple-element.87), channel_id=1, source_target_pairs={{0,30},{1,31},{2,28},{3,29},{4,10},{5,11},{6,8},{7,9},{8,6},{9,7},... | collective-permute-start | bytes 196616 | tf_op jit(solution)/shard_map/ppermute | solution.py:257
  149.2 7.1 %collective-permute-start.38 = (f32[32,512]{1,0:T(8,128)S(1)}, f32[32,512]{1,0:T(8,128)S(1)}, u32[]{:S(2)}, u32[]{:S(2)}) collective-permute-start(f32[32,512]{1,0:T(8,128)S(1)} %get-tuple-element.84.refs_2_), channel_id=1, source_target_pairs={{0,4},{4,0},{8,12},{12,8},{16,20},{20,16},{24,28},{28,24},{1,5},{5... | collective-permute-start | bytes 196616 | tf_op jit(solution)/shard_map/ppermute | solution.py:249
  149.2 7.1 %collective-permute-start.39 = (f32[32,512]{1,0:T(8,128)S(1)}, f32[32,512]{1,0:T(8,128)S(1)}, u32[]{:S(2)}, u32[]{:S(2)}) collective-permute-start(f32[32,512]{1,0:T(8,128)S(1)} %get-tuple-element.85.refs_3_), channel_id=1, source_target_pairs={{0,28},{4,8},{8,4},{12,16},{16,12},{20,24},{24,20},{28,0},{1,29},{... | collective-permute-start | bytes 196616 | tf_op jit(solution)/shard_map/ppermute | solution.py:249
  (13 other events, 30.4 us)

commit v3 on v2

v3 whole, which is shorter than its diff:
```python
import functools

import jax
import jax.numpy as jnp
from jax import lax
from jax.experimental import pallas as pl
from jax.experimental.pallas import tpu as pltpu
from jax.sharding import PartitionSpec as P

POWER = 4
MIXING = 1.0 / 3.0
LANES = 128
MIB = 1024 * 1024
F32 = jnp.float32
BF16 = jnp.bfloat16
HIGHEST = lax.Precision.HIGHEST
VMEM = pl.BlockSpec(memory_space=pltpu.VMEM)
SMEM = pl.BlockSpec(memory_space=pltpu.SMEM)
HBM = pl.BlockSpec(memory_space=pl.ANY)


def kernel_call(body, outs, name, *operands, scratch=(), mib=8, flops=0, moved=0):
    specs = []
    for operand in operands:
        specs.append(SMEM if operand.dtype == jnp.int32 else VMEM)
    return pl.pallas_call(
        body,
        out_shape=outs,
        in_specs=specs,
        out_specs=jax.tree.map(lambda _: VMEM, outs),
        scratch_shapes=list(scratch),
        compiler_params=pltpu.CompilerParams(vmem_limit_bytes=mib * MIB),
        cost_estimate=pl.CostEstimate(flops=flops, bytes_accessed=moved, transcendentals=0),
        name=name,
    )(*operands)


def out(shape, dtype):
    return jax.ShapeDtypeStruct(shape, dtype)


def hold_kernel(source, held, turned, sems):
    tile = source.shape[0] // sems.shape[0]
    spans = [slice(i * tile, (i + 1) * tile) for i in range(sems.shape[0])]
    copies = [
        pltpu.make_async_copy(source.at[span, :], held.at[span, :], sems.at[i])
        for i, span in enumerate(spans)
    ]
    for copy in copies:
        copy.start()
    for copy, span in zip(copies, spans):
        copy.wait()
        turned[:, span] = held[span, :].T


def hold(weight):
    rows, wid = weight.shape
    return pl.pallas_call(
        hold_kernel,
        out_shape=(pltpu.VMEM((rows, wid), weight.dtype), pltpu.VMEM((wid, rows), weight.dtype)),
        in_specs=[HBM],
        out_specs=(VMEM, VMEM),
        scratch_shapes=[pltpu.SemaphoreType.DMA((max(1, rows // 256),))],
        compiler_params=pltpu.CompilerParams(vmem_limit_bytes=32 * MIB),
        cost_estimate=pl.CostEstimate(flops=0, bytes_accessed=2 * rows * wid, transcendentals=0),
        name="hold",
    )(weight)


CHUNKS = 2


def first_kernel(chunk, place, own, prior, turned, even, odd, factor):
    rank, rows = even.shape
    parity = place[1]
    factor[pl.ds(pl.multiple_of(parity * rank, rank), rank), :] = own[...]
    factor[pl.ds(pl.multiple_of((1 - parity) * rank, rank), rank), :] = prior[...]
    product = jnp.dot(
        factor[...], turned[:, chunk * rows : (chunk + 1) * rows], preferred_element_type=F32
    )
    even[...] = product[:rank]
    odd[...] = product[rank:]


def slice_starts(place, offset, count, width, wid):
    low = jnp.bitwise_xor(jnp.bitwise_and(place[0], count - 1), offset) * width
    return pl.multiple_of(low, width), pl.multiple_of(low + wid // 2, width)


def piece_product(place, offset, count, piece, turned, columns):
    width = piece.shape[1] // 2
    low, high = slice_starts(place, offset, count, width, turned.shape[0])
    return jnp.dot(
        piece[:, :width], turned[pl.ds(low, width), columns], preferred_element_type=F32
    ) + jnp.dot(piece[:, width:], turned[pl.ds(high, width), columns], preferred_element_type=F32)


def own_kernel(count, place, piece, turned, partial):
    partial[...] = piece_product(place, 0, count, piece, turned, slice(None))


def next_kernel(chunk, place, *refs):
    *pieces, partial, turned, even, odd = refs
    rank, rows = even.shape
    columns = slice(chunk * rows, (chunk + 1) * rows)
    product = partial[:, columns]
    for offset, piece in enumerate(pieces, 1):
        product += piece_product(place, offset, len(pieces) + 1, piece, turned, columns)
    even[...] = product[:rank]
    odd[...] = product[rank:]


def gathered(place, pieces, factor):
    width = pieces[0].shape[1] // 2
    for offset, piece in enumerate(pieces):
        low, high = slice_starts(place, offset, len(pieces), width, factor.shape[1])
        factor[:, pl.ds(low, width)] = piece[:, :width]
        factor[:, pl.ds(high, width)] = piece[:, width:]


def chosen(place, bit):
    return jnp.bitwise_and(lax.div(place[0], jnp.int32(bit)), 1)


def split_raw(even, odd, even_other, odd_other, both):
    rank = even.shape[0]
    for slot, (mine, theirs) in enumerate(((even, even_other), (odd, odd_other))):
        raw = mine[...] - theirs[...]
        high = raw.astype(BF16)
        both[slot * rank : (slot + 1) * rank, :] = high
        both[(2 + slot) * rank : (3 + slot) * rank, :] = (raw - high.astype(F32)).astype(BF16)


def gram_of(both):
    rank = both.shape[0] // 4
    parts = lax.dot_general(
        both[...], both[...], (((1,), (1,)), ((), ())), preferred_element_type=F32
    )
    parts = parts[: 2 * rank] + parts[2 * rank :]
    parts = parts[:, : 2 * rank] + parts[:, 2 * rank :]
    gram = jnp.concatenate([parts[:rank, :rank], parts[rank:, rank:]], axis=0)
    return jnp.concatenate([gram, jnp.zeros((2 * rank, LANES - rank), F32)], axis=1)


def folded(product):
    rank2 = product.shape[0] // 2
    return product[:rank2] + product[rank2:]


def back_kernel(chunk, *refs):
    *products, weight, both, total, gram = refs
    rows = both.shape[1]
    split_raw(*products, both)
    total[...] = folded(
        jnp.dot(
            both[...], weight[chunk * rows : (chunk + 1) * rows, :], preferred_element_type=F32
        )
    )
    gram[...] = gram_of(both)


def half_product(wanted, slices, both, total, weight, result):
    rows = both.shape[1]
    width = weight.shape[1] // slices
    for i in range(slices // 2):
        columns = pl.ds(pl.multiple_of((2 * i + wanted) * width, width), width)
        product = jnp.dot(
            both[...], weight[weight.shape[0] - rows :, columns], preferred_element_type=F32
        )
        result[:, i * width : (i + 1) * width] = total[:, columns] + folded(product)


def back_send_kernel(slices, place, *refs):
    *products, total, gram, weight, both, send = refs
    split_raw(*products, both)
    half_product(1 - chosen(place, 1), slices, both, total, weight, send)
    send[:, -LANES:] = gram[...] + gram_of(both)


def back_keep_kernel(slices, place, both, total, weight, keep):
    half_product(chosen(place, 1), slices, both, total, weight, keep)


def merge_kernel(bit, slices, place, held, held_gram, came, keep, send):
    width = held.shape[1] // slices
    mine = chosen(place, bit)
    for i in range(slices // 2):
        kept = pl.ds(pl.multiple_of((2 * i + mine) * width, width), width)
        sent = pl.ds(pl.multiple_of((2 * i + 1 - mine) * width, width), width)
        keep[:, i * width : (i + 1) * width] = held[:, kept] + came[:, kept]
        send[:, i * width : (i + 1) * width] = held[:, sent] + came[:, sent]
    send[:, -LANES:] = held_gram[:, -LANES:] + came[:, -LANES:]


def add_kernel(held, held_gram, came, even, odd, gram):
    rank = even.shape[0]
    even[...] = held[:rank, :] + came[:rank, :-LANES]
    odd[...] = held[rank:, :] + came[rank:, :-LANES]
    gram[...] = held_gram[:, -LANES:] + came[:, -LANES:]


def inverse_kernel(gram, came, inverse):
    rank = gram.shape[0] // 2
    shape = (2, rank, LANES)
    lane = lax.broadcasted_iota(jnp.int32, shape, 2)
    row = lax.broadcasted_iota(jnp.int32, shape, 1)
    work = (gram[...] + came[...]).reshape(shape)
    work = jnp.where(lane < rank, work, jnp.where(lane - rank == row, 1.0, 0.0))
    for k in range(rank):
        pivot = work[:, k : k + 1, :]
        scaled = pivot / pivot[:, :, k : k + 1]
        column = jnp.where(row[:, :, :1] > k, work[:, :, k : k + 1], 0.0)
        work = work - column * scaled
    diagonal = jnp.sum(jnp.where(lane == row, work, 0.0), axis=2, keepdims=True)
    work = work / jnp.sqrt(diagonal)
    inverse[...] = work.reshape(2 * rank, LANES)[:, rank : 2 * rank]


def normalised(inverse, even, odd):
    rank = even.shape[0]
    return jnp.concatenate(
        [
            jnp.dot(inverse[:rank, :], even, precision=HIGHEST, preferred_element_type=F32),
            jnp.dot(inverse[rank:, :], odd, precision=HIGHEST, preferred_element_type=F32),
        ],
        axis=0,
    )


def share_kernel(inverse, even, odd, even_pair, odd_pair, share):
    value = normalised(inverse[...], even[...] + even_pair[...], odd[...] + odd_pair[...])
    share[...] = value.astype(share.dtype)


def blend_kernel(share, came, rounded):
    rounded[...] = (share[...].astype(F32) + came[...].astype(F32)).astype(BF16)


def final_kernel(bit, place, share, came, rounded, own):
    rank, width = own.shape
    value = share[...] + came[...]
    rounded[...] = value.astype(BF16)
    rows = pl.ds(pl.multiple_of(place[1] * rank, rank), rank)
    columns = pl.ds(pl.multiple_of(chosen(place, bit) * width, width), width)
    own[...] = share[rows, columns] + came[rows, columns]


def basis_kernel(inverse, *refs):
    *chunks, columns = refs
    for i, both in enumerate(chunks):
        rank2 = both.shape[0] // 2
        rows = both.shape[1]
        raw = both[:rank2, :].astype(F32) + both[rank2:, :].astype(F32)
        basis = normalised(inverse[...], raw[: rank2 // 2], raw[rank2 // 2 :])
        columns[i * rows : (i + 1) * rows, :] = basis.T.astype(BF16)


def update_kernel(place, columns, *refs):
    *pieces, weight, result, factor, made, sems = refs
    gathered(place, pieces, factor)
    tile = made.shape[0] // sems.shape[0]
    copies = []
    for i in range(sems.shape[0]):
        span = slice(i * tile, (i + 1) * tile)
        delta = jnp.dot(columns[span, :], factor[...], preferred_element_type=F32)
        made[span, :] = (weight[span, :].astype(F32) - MIXING * delta).astype(BF16)
        copy = pltpu.make_async_copy(made.at[span, :], result.at[span, :], sems.at[i])
        copy.start()
        copies.append(copy)
    for copy in copies:
        copy.wait()


def on_device(weights, warm_factor):
    peers = lax.axis_size("blk")
    shards = lax.axis_size("shard")
    shard = lax.axis_index("shard")
    parity = lax.rem(lax.axis_index("blk"), 2)
    place = jnp.stack([shard, parity]).astype(jnp.int32)
    bits = [1 << i for i in range(shards.bit_length() - 1)]
    last = bits[-1]
    partner = {
        0: [i + 1 if i % 2 == 0 else i - 1 for i in range(peers)],
        1: [(i + 1) % peers if i % 2 else (i - 1) % peers for i in range(peers)],
    }

    def across(value, bit):
        return lax.ppermute(value, "shard", [(i, i ^ bit) for i in range(shards)])

    def paired(value, slot):
        return lax.ppermute(value, "blk", list(enumerate(partner[slot])))

    own = warm_factor[0].astype(BF16)
    rank, wid = own.shape
    prior = lax.ppermute(own, "blk", [(i, (i + 1) % peers) for i in range(peers)])
    weight, turned = hold(weights[0])
    rows = weight.shape[0]
    width = wid // shards
    chunk_rows = rows // CHUNKS
    cost = dict(flops=4 * rank * chunk_rows * wid, moved=chunk_rows * wid * 2)
    product_outs = (out((rank, chunk_rows), F32), out((rank, chunk_rows), F32))
    factor_scratch = [pltpu.VMEM((2 * rank, wid), BF16)]
    gram_out = out((2 * rank, LANES), F32)
    both_out = out((4 * rank, chunk_rows), BF16)
    part_out = out((rank, 2 * width), F32)

    products = [
        kernel_call(
            functools.partial(first_kernel, chunk), product_outs, "first",
            place, own, prior, turned, scratch=factor_scratch, mib=8, **cost,
        )
        for chunk in range(CHUNKS)
    ]
    for iteration in range(POWER):
        final = iteration == POWER - 1
        exchanged = [
            [*pair, *(paired(product, slot) for slot, product in enumerate(pair))]
            for pair in products
        ]
        slices = shards
        half = slices // 2 * width
        both, total, gram = kernel_call(
            functools.partial(back_kernel, 0), (both_out, out((2 * rank, wid), F32), gram_out),
            "back", *exchanged[0], weight, mib=8, **cost,
        )
        both_last, send = kernel_call(
            functools.partial(back_send_kernel, slices),
            (both_out, out((2 * rank, half + LANES), F32)), "back_send",
            place, *exchanged[1], total, gram, weight, mib=8, **cost,
        )
        keep = kernel_call(
            functools.partial(back_keep_kernel, slices), out((2 * rank, half), F32), "back_keep",
            place, both_last, total, weight, mib=8, **cost,
        )
        gram = send
        for bit in bits[:-1]:
            came = across(send, bit)
            slices //= 2
            half = slices // 2 * width
            if 2 * bit == last:
                even, odd, gram = kernel_call(
                    add_kernel, (part_out, part_out, gram_out), "add", keep, gram, came
                )
                break
            keep, send = kernel_call(
                functools.partial(merge_kernel, 2 * bit, slices),
                (out((2 * rank, half), F32), out((2 * rank, half + LANES), F32)), "merge",
                place, keep, gram, came,
            )
            gram = send
        gram_came = across(gram, last)
        pair = (paired(even, 0), paired(odd, 1))
        inverse = kernel_call(
            inverse_kernel, out((2 * rank, rank), F32), "inverse", gram, gram_came,
            flops=1000000, moved=8 * MIB,
        )
        share = kernel_call(
            share_kernel, out((2 * rank, 2 * width), F32 if final else BF16), "share",
            inverse, even, odd, *pair,
        )
        came = across(share, last)
        rounded_out = out((2 * rank, 2 * width), BF16)
        if final:
            columns = kernel_call(
                basis_kernel, out((rows, 2 * rank), BF16), "basis", inverse, both, both_last,
                mib=8, flops=8 * rank * rank * rows, moved=2 * MIB,
            )
            rounded, new_factor = kernel_call(
                functools.partial(final_kernel, last), (rounded_out, out((rank, width), F32)),
                "final", place, share, came,
            )
        else:
            rounded = kernel_call(blend_kernel, rounded_out, "blend", share, came)
        pieces = {0: rounded}
        for bit in reversed(bits[:-1]):
            for offset in list(pieces):
                pieces[offset ^ bit] = across(pieces[offset], bit)
        pieces = [pieces[offset] for offset in range(last)]
        if not final:
            partial = kernel_call(
                functools.partial(own_kernel, last), out((2 * rank, rows), F32), "own",
                place, rounded, turned, mib=8, **cost,
            )
            products = [
                kernel_call(
                    functools.partial(next_kernel, chunk), product_outs, "next",
                    place, *pieces[1:], partial, turned, mib=8, **cost,
                )
                for chunk in range(CHUNKS)
            ]
    new_weight = pl.pallas_call(
        update_kernel,
        out_shape=out((rows, wid), BF16),
        in_specs=[SMEM] + [VMEM] * (len(pieces) + 2),
        out_specs=HBM,
        scratch_shapes=[*factor_scratch, pltpu.VMEM((rows, wid), BF16), pltpu.SemaphoreType.DMA((max(1, rows // 256),))],
        compiler_params=pltpu.CompilerParams(vmem_limit_bytes=16 * MIB),
        cost_estimate=pl.CostEstimate(
            flops=4 * rank * rows * wid, bytes_accessed=2 * rows * wid, transcendentals=0
        ),
        name="update",
    )(place, columns, *pieces, weight)
    return (new_weight[None], new_factor[None])


def solution(mesh):
    placed = (P("blk", "shard", None), P("blk", None, None))
    return jax.shard_map(
        on_device,
        mesh=mesh,
        in_specs=placed,
        out_specs=(P("blk", "shard", None), P("blk", None, "shard")),
        check_vma=False,
    )
```

time: 168 us -> 157 us (0.935)
  waiting for transfers between devices: 74 us -> 57.1 us
  Pallas kernels: 45.1 us -> 49.3 us
  starting transfers between devices: 46.6 us -> 48.3 us
    ppermute x16 -> x24, waiting for transfers between devices: 47.2 us -> 26.4 us  [paired(): return lax.ppermute(value, 'blk', list(enumerate(partner[slot])))]
    ppermute x8 -> x0, starting transfers between devices: 16.2 us -> none  [far(): return lax.ppermute(value, ('blk', 'shard'), pairs)]
    ppermute x16 -> x24, starting transfers between devices: 20.2 us -> 32.7 us  [paired(): return lax.ppermute(value, 'blk', list(enumerate(partner[slot])))]
    ppermute x20 -> x16, starting transfers between devices: 7.14 us -> 12.5 us  [across(): return lax.ppermute(value, 'shard', [(i, i ^ bit) for i in range(shards)])]
    pallas_call x25 -> x40, Pallas kernels: 36.6 us -> 40.8 us  [kernel_call(): pl.pallas_call(body, out_shape=outs, in_specs=specs, out_specs=jax.tree.m...]
    ppermute x20 -> x16, waiting for transfers between devices: 24.4 us -> 28.4 us  [across(): return lax.ppermute(value, 'shard', [(i, i ^ bit) for i in range(shards)])]
  transfers between devices with their start and end apart: 45 -> 41, of which waited for: 26 -> 22; matrix products, arithmetic and copies ran while one was open for 0% -> 0% of each run, Pallas kernels for 13% -> 21%
where the time goes in v3:
time: 157 us
  waiting for transfers between devices  57.1 us (36%)
  Pallas kernels  49.3 us (31%)
  starting transfers between devices  48.3 us (31%)
    pallas_call x40, Pallas kernels, kernel_call(): pl.pallas_call(body, out_shape=outs, in_specs=specs, out_specs=jax.tree.m...  40.8 us
    ppermute x24, starting transfers between devices, paired(): return lax.ppermute(value, 'blk', list(enumerate(partner[slot])))  32.7 us
    ppermute x16, waiting for transfers between devices, across(): return lax.ppermute(value, 'shard', [(i, i ^ bit) for i in range(shards)])  28.4 us
    ppermute x24, waiting for transfers between devices, paired(): return lax.ppermute(value, 'blk', list(enumerate(partner[slot])))  26.4 us
    ppermute x16, starting transfers between devices, across(): return lax.ppermute(value, 'shard', [(i, i ^ bit) for i in range(shards)])  12.5 us
    pallas_call x1, Pallas kernels, on_device(): pl.pallas_call(update_kernel, out_shape=out((rows, wid), BF16), in_specs=...  4.34 us
    pallas_call x1, Pallas kernels, hold(): pl.pallas_call(hold_kernel, out_shape=(pltpu.VMEM((rows, wid), weight.dty...  4.11 us
  transfers between devices with their start and end apart: 41, of which 22 were waited for; matrix products, arithmetic and copies ran while one was open for 0% of the time, Pallas kernels for 21%

profile of v3, /device:TPU:0, one launch (start us, length us, event | category | flops | bytes accessed | tf_op | source)
XLA Modules:
  0.0 156.8 jit_solution(7235825156379603144)
XLA Ops:
  1.6 3.0 %collective-permute-start = (bf16[32,2048]{1,0:T(8,128)(2,1)S(1)}, bf16[32,2048]{1,0:T(8,128)(2,1)S(1)}, u32[]{:S(2)}, u32[]{:S(2)}) collective-permute-start(bf16[32,2048]{1,0:T(8,128)(2,1)S(1)} %convert_bitcast_fusion.own), channel_id=1, source_target_pairs={{0,4},{4,8},{8,12},{12,16},{16,20},{20,24},{24,28},{28,0},{1,5},{5... | collective-permute-start | bytes 393224 | tf_op jit(solution)/shard_map/ppermute | solution.py:295
  4.6 4.1 %hold.1 = (bf16[2048,2048]{1,0:T(8,128)(2,1)S(1)}, bf16[2048,2048]{1,0:T(8,128)(2,1)S(1)}) custom-call(bf16[2048,2048]{1,0:T(8,128)(2,1)} %bitcast.8), custom_call_target="tpu_custom_call" | custom-call | bytes 8388608 | tf_op jit(solution)/shard_map/hold/pallas_call | solution.py:58
  8.8 2.3 %collective-permute-done.prior = bf16[32,2048]{1,0:T(8,128)(2,1)S(1)} collective-permute-done((bf16[32,2048]{1,0:T(8,128)(2,1)S(1)}, bf16[32,2048]{1,0:T(8,128)(2,1)S(1)}, u32[]{:S(2)}, u32[]{:S(2)}) %collective-permute-start) | collective-permute-done | bytes 131104 | tf_op jit(solution)/shard_map/ppermute | solution.py:295
  12.6 3.1 %collective-permute-start.4 = (f32[32,1024]{1,0:T(8,128)S(1)}, f32[32,1024]{1,0:T(8,128)S(1)}, u32[]{:S(2)}, u32[]{:S(2)}) collective-permute-start(f32[32,1024]{1,0:T(8,128)S(1)} %get-tuple-element.55.refs_1_), channel_id=1, source_target_pairs={{0,28},{4,8},{8,4},{12,16},{16,12},{20,24},{24,20},{28,0},{1,29},{... | collective-permute-start | bytes 393224 | tf_op jit(solution)/shard_map/ppermute | solution.py:291
  21.5 4.5 %collective-permute-done.1.refs_2_ = f32[32,1024]{1,0:T(8,128)S(1)} collective-permute-done((f32[32,1024]{1,0:T(8,128)S(1)}, f32[32,1024]{1,0:T(8,128)S(1)}, u32[]{:S(2)}, u32[]{:S(2)}) %collective-permute-start.1) | collective-permute-done | bytes 131104 | tf_op jit(solution)/shard_map/ppermute | solution.py:291
  29.0 2.7 %collective-permute-start.8 = (f32[32,1024]{1,0:T(8,128)S(1)}, f32[32,1024]{1,0:T(8,128)S(1)}, u32[]{:S(2)}, u32[]{:S(2)}) collective-permute-start(f32[32,1024]{1,0:T(8,128)S(1)} %get-tuple-element.63.odd), channel_id=1, source_target_pairs={{0,28},{4,8},{8,4},{12,16},{16,12},{20,24},{24,20},{28,0},{1,29},{... | collective-permute-start | bytes 393224 | tf_op jit(solution)/shard_map/ppermute | solution.py:291
  33.2 2.4 %collective-permute-done.6.came = f32[64,128]{1,0:T(8,128)S(1)} collective-permute-done((f32[64,128]{1,0:T(8,128)S(1)}, f32[64,128]{1,0:T(8,128)S(1)}, u32[]{:S(2)}, u32[]{:S(2)}) %collective-permute-start.6) | collective-permute-done | bytes 32800 | tf_op jit(solution)/shard_map/ppermute | solution.py:288
  35.6 2.8 %inverse.4 = f32[64,32]{1,0:T(8,128)S(1)} custom-call(f32[64,128]{1,0:T(8,128)S(1)} %get-tuple-element.61.gram, f32[64,128]{1,0:T(8,128)S(1)} %collective-permute-done.6.came), custom_call_target="tpu_custom_call" | custom-call | flops 1000000 | bytes 8388608 | tf_op jit(solution)/shard_map/inverse/pallas_call | solution.py:26
  40.3 3.5 %collective-permute-done.9.came = bf16[64,1024]{1,0:T(8,128)(2,1)S(1)} collective-permute-done((bf16[64,1024]{1,0:T(8,128)(2,1)S(1)}, bf16[64,1024]{1,0:T(8,128)(2,1)S(1)}, u32[]{:S(2)}, u32[]{:S(2)}) %collective-permute-start.9) | collective-permute-done | bytes 131104 | tf_op jit(solution)/shard_map/ppermute | solution.py:288
  46.4 2.3 %collective-permute-start.14 = (f32[32,1024]{1,0:T(8,128)S(1)}, f32[32,1024]{1,0:T(8,128)S(1)}, u32[]{:S(2)}, u32[]{:S(2)}) collective-permute-start(f32[32,1024]{1,0:T(8,128)S(1)} %get-tuple-element.67.refs_1_), channel_id=1, source_target_pairs={{0,28},{4,8},{8,4},{12,16},{16,12},{20,24},{24,20},{28,0},{1,29},{... | collective-permute-start | bytes 393224 | tf_op jit(solution)/shard_map/ppermute | solution.py:291
  50.0 2.3 %collective-permute-start.12 = (f32[32,1024]{1,0:T(8,128)S(1)}, f32[32,1024]{1,0:T(8,128)S(1)}, u32[]{:S(2)}, u32[]{:S(2)}) collective-permute-start(f32[32,1024]{1,0:T(8,128)S(1)} %get-tuple-element.65.refs_1_), channel_id=1, source_target_pairs={{0,28},{4,8},{8,4},{12,16},{16,12},{20,24},{24,20},{28,0},{1,29},{... | collective-permute-start | bytes 393224 | tf_op jit(solution)/shard_map/ppermute | solution.py:291
  52.4 3.4 %collective-permute-done.13.refs_2_ = f32[32,1024]{1,0:T(8,128)S(1)} collective-permute-done((f32[32,1024]{1,0:T(8,128)S(1)}, f32[32,1024]{1,0:T(8,128)S(1)}, u32[]{:S(2)}, u32[]{:S(2)}) %collective-permute-start.13) | collective-permute-done | bytes 131104 | tf_op jit(solution)/shard_map/ppermute | solution.py:291
  56.7 4.0 %collective-permute-done.11.refs_2_ = f32[32,1024]{1,0:T(8,128)S(1)} collective-permute-done((f32[32,1024]{1,0:T(8,128)S(1)}, f32[32,1024]{1,0:T(8,128)S(1)}, u32[]{:S(2)}, u32[]{:S(2)}) %collective-permute-start.11) | collective-permute-done | bytes 131104 | tf_op jit(solution)/shard_map/ppermute | solution.py:291
  67.5 2.4 %collective-permute-done.16.came = f32[64,128]{1,0:T(8,128)S(1)} collective-permute-done((f32[64,128]{1,0:T(8,128)S(1)}, f32[64,128]{1,0:T(8,128)S(1)}, u32[]{:S(2)}, u32[]{:S(2)}) %collective-permute-start.16) | collective-permute-done | bytes 32800 | tf_op jit(solution)/shard_map/ppermute | solution.py:288
  69.9 2.8 %inverse.5 = f32[64,32]{1,0:T(8,128)S(1)} custom-call(f32[64,128]{1,0:T(8,128)S(1)} %get-tuple-element.72.gram, f32[64,128]{1,0:T(8,128)S(1)} %collective-permute-done.16.came), custom_call_target="tpu_custom_call" | custom-call | flops 1000000 | bytes 8388608 | tf_op jit(solution)/shard_map/inverse/pallas_call | solution.py:26
  74.6 3.5 %collective-permute-done.19.came = bf16[64,1024]{1,0:T(8,128)(2,1)S(1)} collective-permute-done((bf16[64,1024]{1,0:T(8,128)(2,1)S(1)}, bf16[64,1024]{1,0:T(8,128)(2,1)S(1)}, u32[]{:S(2)}, u32[]{:S(2)}) %collective-permute-start.19) | collective-permute-done | bytes 131104 | tf_op jit(solution)/shard_map/ppermute | solution.py:288
  80.9 2.6 %collective-permute-start.24 = (f32[32,1024]{1,0:T(8,128)S(1)}, f32[32,1024]{1,0:T(8,128)S(1)}, u32[]{:S(2)}, u32[]{:S(2)}) collective-permute-start(f32[32,1024]{1,0:T(8,128)S(1)} %get-tuple-element.78.refs_1_), channel_id=1, source_target_pairs={{0,28},{4,8},{8,4},{12,16},{16,12},{20,24},{24,20},{28,0},{1,29},{... | collective-permute-start | bytes 393224 | tf_op jit(solution)/shard_map/ppermute | solution.py:291
  85.3 2.4 %collective-permute-start.22 = (f32[32,1024]{1,0:T(8,128)S(1)}, f32[32,1024]{1,0:T(8,128)S(1)}, u32[]{:S(2)}, u32[]{:S(2)}) collective-permute-start(f32[32,1024]{1,0:T(8,128)S(1)} %get-tuple-element.76.refs_1_), channel_id=1, source_target_pairs={{0,28},{4,8},{8,4},{12,16},{16,12},{20,24},{24,20},{28,0},{1,29},{... | collective-permute-start | bytes 393224 | tf_op jit(solution)/shard_map/ppermute | solution.py:291
  90.5 4.5 %collective-permute-done.21.refs_2_ = f32[32,1024]{1,0:T(8,128)S(1)} collective-permute-done((f32[32,1024]{1,0:T(8,128)S(1)}, f32[32,1024]{1,0:T(8,128)S(1)}, u32[]{:S(2)}, u32[]{:S(2)}) %collective-permute-start.21) | collective-permute-done | bytes 131104 | tf_op jit(solution)/shard_map/ppermute | solution.py:291
  98.3 2.6 %collective-permute-start.28 = (f32[32,1024]{1,0:T(8,128)S(1)}, f32[32,1024]{1,0:T(8,128)S(1)}, u32[]{:S(2)}, u32[]{:S(2)}) collective-permute-start(f32[32,1024]{1,0:T(8,128)S(1)} %get-tuple-element.85.odd), channel_id=1, source_target_pairs={{0,28},{4,8},{8,4},{12,16},{16,12},{20,24},{24,20},{28,0},{1,29},{... | collective-permute-start | bytes 393224 | tf_op jit(solution)/shard_map/ppermute | solution.py:291
  102.4 2.4 %collective-permute-done.26.came = f32[64,128]{1,0:T(8,128)S(1)} collective-permute-done((f32[64,128]{1,0:T(8,128)S(1)}, f32[64,128]{1,0:T(8,128)S(1)}, u32[]{:S(2)}, u32[]{:S(2)}) %collective-permute-start.26) | collective-permute-done | bytes 32800 | tf_op jit(solution)/shard_map/ppermute | solution.py:288
  104.9 2.8 %inverse.6 = f32[64,32]{1,0:T(8,128)S(1)} custom-call(f32[64,128]{1,0:T(8,128)S(1)} %get-tuple-element.83.gram, f32[64,128]{1,0:T(8,128)S(1)} %collective-permute-done.26.came), custom_call_target="tpu_custom_call" | custom-call | flops 1000000 | bytes 8388608 | tf_op jit(solution)/shard_map/inverse/pallas_call | solution.py:26
  109.6 3.5 %collective-permute-done.29.came = bf16[64,1024]{1,0:T(8,128)(2,1)S(1)} collective-permute-done((bf16[64,1024]{1,0:T(8,128)(2,1)S(1)}, bf16[64,1024]{1,0:T(8,128)(2,1)S(1)}, u32[]{:S(2)}, u32[]{:S(2)}) %collective-permute-start.29) | collective-permute-done | bytes 131104 | tf_op jit(solution)/shard_map/ppermute | solution.py:288
  116.1 2.4 %collective-permute-start.34 = (f32[32,1024]{1,0:T(8,128)S(1)}, f32[32,1024]{1,0:T(8,128)S(1)}, u32[]{:S(2)}, u32[]{:S(2)}) collective-permute-start(f32[32,1024]{1,0:T(8,128)S(1)} %get-tuple-element.89.refs_1_), channel_id=1, source_target_pairs={{0,28},{4,8},{8,4},{12,16},{16,12},{20,24},{24,20},{28,0},{1,29},{... | collective-permute-start | bytes 393224 | tf_op jit(solution)/shard_map/ppermute | solution.py:291
  119.6 2.6 %collective-permute-start.32 = (f32[32,1024]{1,0:T(8,128)S(1)}, f32[32,1024]{1,0:T(8,128)S(1)}, u32[]{:S(2)}, u32[]{:S(2)}) collective-permute-start(f32[32,1024]{1,0:T(8,128)S(1)} %get-tuple-element.87.refs_1_), channel_id=1, source_target_pairs={{0,28},{4,8},{8,4},{12,16},{16,12},{20,24},{24,20},{28,0},{1,29},{... | collective-permute-start | bytes 393224 | tf_op jit(solution)/shard_map/ppermute | solution.py:291
  122.3 3.1 %collective-permute-done.33.refs_2_ = f32[32,1024]{1,0:T(8,128)S(1)} collective-permute-done((f32[32,1024]{1,0:T(8,128)S(1)}, f32[32,1024]{1,0:T(8,128)S(1)}, u32[]{:S(2)}, u32[]{:S(2)}) %collective-permute-start.33) | collective-permute-done | bytes 131104 | tf_op jit(solution)/shard_map/ppermute | solution.py:291
  126.3 3.7 %collective-permute-done.31.refs_2_ = f32[32,1024]{1,0:T(8,128)S(1)} collective-permute-done((f32[32,1024]{1,0:T(8,128)S(1)}, f32[32,1024]{1,0:T(8,128)S(1)}, u32[]{:S(2)}, u32[]{:S(2)}) %collective-permute-start.31) | collective-permute-done | bytes 131104 | tf_op jit(solution)/shard_map/ppermute | solution.py:291
  133.3 2.4 %collective-permute-start.38 = (f32[32,1024]{1,0:T(8,128)S(1)}, f32[32,1024]{1,0:T(8,128)S(1)}, u32[]{:S(2)}, u32[]{:S(2)}) collective-permute-start(f32[32,1024]{1,0:T(8,128)S(1)} %get-tuple-element.97.odd), channel_id=1, source_target_pairs={{0,28},{4,8},{8,4},{12,16},{16,12},{20,24},{24,20},{28,0},{1,29},{... | collective-permute-start | bytes 393224 | tf_op jit(solution)/shard_map/ppermute | solution.py:291
  137.2 2.4 %collective-permute-done.36.came = f32[64,128]{1,0:T(8,128)S(1)} collective-permute-done((f32[64,128]{1,0:T(8,128)S(1)}, f32[64,128]{1,0:T(8,128)S(1)}, u32[]{:S(2)}, u32[]{:S(2)}) %collective-permute-start.36) | collective-permute-done | bytes 32800 | tf_op jit(solution)/shard_map/ppermute | solution.py:288
  139.6 2.8 %inverse.7 = f32[64,32]{1,0:T(8,128)S(1)} custom-call(f32[64,128]{1,0:T(8,128)S(1)} %get-tuple-element.94.gram, f32[64,128]{1,0:T(8,128)S(1)} %collective-permute-done.36.came), custom_call_target="tpu_custom_call" | custom-call | flops 1000000 | bytes 8388608 | tf_op jit(solution)/shard_map/inverse/pallas_call | solution.py:26
  144.3 5.4 %collective-permute-done.39.came = f32[64,1024]{1,0:T(8,128)S(1)} collective-permute-done((f32[64,1024]{1,0:T(8,128)S(1)}, f32[64,1024]{1,0:T(8,128)S(1)}, u32[]{:S(2)}, u32[]{:S(2)}) %collective-permute-start.39) | collective-permute-done | bytes 262176 | tf_op jit(solution)/shard_map/ppermute | solution.py:288
  152.3 4.3 %update.1 = bf16[2048,2048]{1,0:T(8,128)(2,1)} custom-call(s32[2]{0:T(128)S(1)} %pad_add_fusion.place, bf16[2048,64]{1,0:T(8,128)(2,1)S(1)} %basis.1.columns, bf16[64,1024]{1,0:T(8,128)(2,1)S(1)} %get-tuple-element.98.refs_0_, bf16[64,1024]{1,0:T(8,128)(2,1)S(1)} %collective-permute-done.40.refs_1_, ...), custom_call_target="tpu_custom_call" | custom-call | flops 536870912 | bytes 8388608 | tf_op jit(solution)/shard_map/update/pallas_call | solution.py:391
  (94 shorter events, 56.6 us)
Async XLA Ops:
  1.6 9.6 %collective-permute-start = (bf16[32,2048]{1,0:T(8,128)(2,1)S(1)}, bf16[32,2048]{1,0:T(8,128)(2,1)S(1)}, u32[]{:S(2)}, u32[]{:S(2)}) collective-permute-start(bf16[32,2048]{1,0:T(8,128)(2,1)S(1)} %convert_bitcast_fusion.own), channel_id=1, source_target_pairs={{0,4},{4,8},{8,12},{12,16},{16,20},{20,24},{24,28},{28,0},{1,5},{5... | collective-permute-start | bytes 393224 | tf_op jit(solution)/shard_map/ppermute | solution.py:295
  12.5 8.0 %collective-permute-start.3 = (f32[32,1024]{1,0:T(8,128)S(1)}, f32[32,1024]{1,0:T(8,128)S(1)}, u32[]{:S(2)}, u32[]{:S(2)}) collective-permute-start(f32[32,1024]{1,0:T(8,128)S(1)} %get-tuple-element.54.refs_0_), channel_id=1, source_target_pairs={{0,4},{4,0},{8,12},{12,8},{16,20},{20,16},{24,28},{28,24},{1,5},{5... | collective-permute-start | bytes 393224 | tf_op jit(solution)/shard_map/ppermute | solution.py:291
  12.6 7.9 %collective-permute-start.4 = (f32[32,1024]{1,0:T(8,128)S(1)}, f32[32,1024]{1,0:T(8,128)S(1)}, u32[]{:S(2)}, u32[]{:S(2)}) collective-permute-start(f32[32,1024]{1,0:T(8,128)S(1)} %get-tuple-element.55.refs_1_), channel_id=1, source_target_pairs={{0,28},{4,8},{8,4},{12,16},{16,12},{20,24},{24,20},{28,0},{1,29},{... | collective-permute-start | bytes 393224 | tf_op jit(solution)/shard_map/ppermute | solution.py:291
  17.1 8.9 %collective-permute-start.1 = (f32[32,1024]{1,0:T(8,128)S(1)}, f32[32,1024]{1,0:T(8,128)S(1)}, u32[]{:S(2)}, u32[]{:S(2)}) collective-permute-start(f32[32,1024]{1,0:T(8,128)S(1)} %get-tuple-element.52.refs_0_), channel_id=1, source_target_pairs={{0,4},{4,0},{8,12},{12,8},{16,20},{20,16},{24,28},{28,24},{1,5},{5... | collective-permute-start | bytes 393224 | tf_op jit(solution)/shard_map/ppermute | solution.py:291
  17.2 8.8 %collective-permute-start.2 = (f32[32,1024]{1,0:T(8,128)S(1)}, f32[32,1024]{1,0:T(8,128)S(1)}, u32[]{:S(2)}, u32[]{:S(2)}) collective-permute-start(f32[32,1024]{1,0:T(8,128)S(1)} %get-tuple-element.53.refs_1_), channel_id=1, source_target_pairs={{0,28},{4,8},{8,4},{12,16},{16,12},{20,24},{24,20},{28,0},{1,29},{... | collective-permute-start | bytes 393224 | tf_op jit(solution)/shard_map/ppermute | solution.py:291
  28.9 9.5 %collective-permute-start.7 = (f32[32,1024]{1,0:T(8,128)S(1)}, f32[32,1024]{1,0:T(8,128)S(1)}, u32[]{:S(2)}, u32[]{:S(2)}) collective-permute-start(f32[32,1024]{1,0:T(8,128)S(1)} %get-tuple-element.62.even), channel_id=1, source_target_pairs={{0,4},{4,0},{8,12},{12,8},{16,20},{20,16},{24,28},{28,24},{1,5},{5... | collective-permute-start | bytes 393224 | tf_op jit(solution)/shard_map/ppermute | solution.py:291
  29.0 9.4 %collective-permute-start.8 = (f32[32,1024]{1,0:T(8,128)S(1)}, f32[32,1024]{1,0:T(8,128)S(1)}, u32[]{:S(2)}, u32[]{:S(2)}) collective-permute-start(f32[32,1024]{1,0:T(8,128)S(1)} %get-tuple-element.63.odd), channel_id=1, source_target_pairs={{0,28},{4,8},{8,4},{12,16},{16,12},{20,24},{24,20},{28,0},{1,29},{... | collective-permute-start | bytes 393224 | tf_op jit(solution)/shard_map/ppermute | solution.py:291
  31.7 3.9 %collective-permute-start.6 = (f32[64,128]{1,0:T(8,128)S(1)}, f32[64,128]{1,0:T(8,128)S(1)}, u32[]{:S(2)}, u32[]{:S(2)}) collective-permute-start(f32[64,128]{1,0:T(8,128)S(1)} %get-tuple-element.61.gram), channel_id=1, source_target_pairs={{0,2},{1,3},{2,0},{3,1},{4,6},{5,7},{6,4},{7,5},{8,10},{9,11},{10,... | collective-permute-start | bytes 98312 | tf_op jit(solution)/shard_map/ppermute | solution.py:288
  38.7 5.0 %collective-permute-start.9 = (bf16[64,1024]{1,0:T(8,128)(2,1)S(1)}, bf16[64,1024]{1,0:T(8,128)(2,1)S(1)}, u32[]{:S(2)}, u32[]{:S(2)}) collective-permute-start(bf16[64,1024]{1,0:T(8,128)(2,1)S(1)} %share.4), channel_id=1, source_target_pairs={{0,2},{1,3},{2,0},{3,1},{4,6},{5,7},{6,4},{7,5},{8,10},{9,11},{10,... | collective-permute-start | bytes 393224 | tf_op jit(solution)/shard_map/ppermute | solution.py:288
  46.3 9.4 %collective-permute-start.13 = (f32[32,1024]{1,0:T(8,128)S(1)}, f32[32,1024]{1,0:T(8,128)S(1)}, u32[]{:S(2)}, u32[]{:S(2)}) collective-permute-start(f32[32,1024]{1,0:T(8,128)S(1)} %get-tuple-element.66.refs_0_), channel_id=1, source_target_pairs={{0,4},{4,0},{8,12},{12,8},{16,20},{20,16},{24,28},{28,24},{1,5},{5... | collective-permute-start | bytes 393224 | tf_op jit(solution)/shard_map/ppermute | solution.py:291
  46.4 9.4 %collective-permute-start.14 = (f32[32,1024]{1,0:T(8,128)S(1)}, f32[32,1024]{1,0:T(8,128)S(1)}, u32[]{:S(2)}, u32[]{:S(2)}) collective-permute-start(f32[32,1024]{1,0:T(8,128)S(1)} %get-tuple-element.67.refs_1_), channel_id=1, source_target_pairs={{0,28},{4,8},{8,4},{12,16},{16,12},{20,24},{24,20},{28,0},{1,29},{... | collective-permute-start | bytes 393224 | tf_op jit(solution)/shard_map/ppermute | solution.py:291
  49.8 11.0 %collective-permute-start.11 = (f32[32,1024]{1,0:T(8,128)S(1)}, f32[32,1024]{1,0:T(8,128)S(1)}, u32[]{:S(2)}, u32[]{:S(2)}) collective-permute-start(f32[32,1024]{1,0:T(8,128)S(1)} %get-tuple-element.64.refs_0_), channel_id=1, source_target_pairs={{0,4},{4,0},{8,12},{12,8},{16,20},{20,16},{24,28},{28,24},{1,5},{5... | collective-permute-start | bytes 393224 | tf_op jit(solution)/shard_map/ppermute | solution.py:291
  50.0 10.7 %collective-permute-start.12 = (f32[32,1024]{1,0:T(8,128)S(1)}, f32[32,1024]{1,0:T(8,128)S(1)}, u32[]{:S(2)}, u32[]{:S(2)}) collective-permute-start(f32[32,1024]{1,0:T(8,128)S(1)} %get-tuple-element.65.refs_1_), channel_id=1, source_target_pairs={{0,28},{4,8},{8,4},{12,16},{16,12},{20,24},{24,20},{28,0},{1,29},{... | collective-permute-start | bytes 393224 | tf_op jit(solution)/shard_map/ppermute | solution.py:291
  63.6 9.1 %collective-permute-start.17 = (f32[32,1024]{1,0:T(8,128)S(1)}, f32[32,1024]{1,0:T(8,128)S(1)}, u32[]{:S(2)}, u32[]{:S(2)}) collective-permute-start(f32[32,1024]{1,0:T(8,128)S(1)} %get-tuple-element.73.even), channel_id=1, source_target_pairs={{0,4},{4,0},{8,12},{12,8},{16,20},{20,16},{24,28},{28,24},{1,5},{5... | collective-permute-start | bytes 393224 | tf_op jit(solution)/shard_map/ppermute | solution.py:291
  63.9 8.8 %collective-permute-start.18 = (f32[32,1024]{1,0:T(8,128)S(1)}, f32[32,1024]{1,0:T(8,128)S(1)}, u32[]{:S(2)}, u32[]{:S(2)}) collective-permute-start(f32[32,1024]{1,0:T(8,128)S(1)} %get-tuple-element.74.odd), channel_id=1, source_target_pairs={{0,28},{4,8},{8,4},{12,16},{16,12},{20,24},{24,20},{28,0},{1,29},{... | collective-permute-start | bytes 393224 | tf_op jit(solution)/shard_map/ppermute | solution.py:291
  66.0 3.9 %collective-permute-start.16 = (f32[64,128]{1,0:T(8,128)S(1)}, f32[64,128]{1,0:T(8,128)S(1)}, u32[]{:S(2)}, u32[]{:S(2)}) collective-permute-start(f32[64,128]{1,0:T(8,128)S(1)} %get-tuple-element.72.gram), channel_id=1, source_target_pairs={{0,2},{1,3},{2,0},{3,1},{4,6},{5,7},{6,4},{7,5},{8,10},{9,11},{10,... | collective-permute-start | bytes 98312 | tf_op jit(solution)/shard_map/ppermute | solution.py:288
  73.1 5.0 %collective-permute-start.19 = (bf16[64,1024]{1,0:T(8,128)(2,1)S(1)}, bf16[64,1024]{1,0:T(8,128)(2,1)S(1)}, u32[]{:S(2)}, u32[]{:S(2)}) collective-permute-start(bf16[64,1024]{1,0:T(8,128)(2,1)S(1)} %share.5), channel_id=1, source_target_pairs={{0,2},{1,3},{2,0},{3,1},{4,6},{5,7},{6,4},{7,5},{8,10},{9,11},{10,... | collective-permute-start | bytes 393224 | tf_op jit(solution)/shard_map/ppermute | solution.py:288
  80.7 7.1 %collective-permute-start.23 = (f32[32,1024]{1,0:T(8,128)S(1)}, f32[32,1024]{1,0:T(8,128)S(1)}, u32[]{:S(2)}, u32[]{:S(2)}) collective-permute-start(f32[32,1024]{1,0:T(8,128)S(1)} %get-tuple-element.77.refs_0_), channel_id=1, source_target_pairs={{0,4},{4,0},{8,12},{12,8},{16,20},{20,16},{24,28},{28,24},{1,5},{5... | collective-permute-start | bytes 393224 | tf_op jit(solution)/shard_map/ppermute | solution.py:291
  80.9 8.6 %collective-permute-start.24 = (f32[32,1024]{1,0:T(8,128)S(1)}, f32[32,1024]{1,0:T(8,128)S(1)}, u32[]{:S(2)}, u32[]{:S(2)}) collective-permute-start(f32[32,1024]{1,0:T(8,128)S(1)} %get-tuple-element.78.refs_1_), channel_id=1, source_target_pairs={{0,28},{4,8},{8,4},{12,16},{16,12},{20,24},{24,20},{28,0},{1,29},{... | collective-permute-start | bytes 393224 | tf_op jit(solution)/shard_map/ppermute | solution.py:291
  84.7 10.4 %collective-permute-start.21 = (f32[32,1024]{1,0:T(8,128)S(1)}, f32[32,1024]{1,0:T(8,128)S(1)}, u32[]{:S(2)}, u32[]{:S(2)}) collective-permute-start(f32[32,1024]{1,0:T(8,128)S(1)} %get-tuple-element.75.refs_0_), channel_id=1, source_target_pairs={{0,4},{4,0},{8,12},{12,8},{16,20},{20,16},{24,28},{28,24},{1,5},{5... | collective-permute-start | bytes 393224 | tf_op jit(solution)/shard_map/ppermute | solution.py:291
  85.3 9.7 %collective-permute-start.22 = (f32[32,1024]{1,0:T(8,128)S(1)}, f32[32,1024]{1,0:T(8,128)S(1)}, u32[]{:S(2)}, u32[]{:S(2)}) collective-permute-start(f32[32,1024]{1,0:T(8,128)S(1)} %get-tuple-element.76.refs_1_), channel_id=1, source_target_pairs={{0,28},{4,8},{8,4},{12,16},{16,12},{20,24},{24,20},{28,0},{1,29},{... | collective-permute-start | bytes 393224 | tf_op jit(solution)/shard_map/ppermute | solution.py:291
  97.9 9.7 %collective-permute-start.27 = (f32[32,1024]{1,0:T(8,128)S(1)}, f32[32,1024]{1,0:T(8,128)S(1)}, u32[]{:S(2)}, u32[]{:S(2)}) collective-permute-start(f32[32,1024]{1,0:T(8,128)S(1)} %get-tuple-element.84.even), channel_id=1, source_target_pairs={{0,4},{4,0},{8,12},{12,8},{16,20},{20,16},{24,28},{28,24},{1,5},{5... | collective-permute-start | bytes 393224 | tf_op jit(solution)/shard_map/ppermute | solution.py:291
  98.3 9.4 %collective-permute-start.28 = (f32[32,1024]{1,0:T(8,128)S(1)}, f32[32,1024]{1,0:T(8,128)S(1)}, u32[]{:S(2)}, u32[]{:S(2)}) collective-permute-start(f32[32,1024]{1,0:T(8,128)S(1)} %get-tuple-element.85.odd), channel_id=1, source_target_pairs={{0,28},{4,8},{8,4},{12,16},{16,12},{20,24},{24,20},{28,0},{1,29},{... | collective-permute-start | bytes 393224 | tf_op jit(solution)/shard_map/ppermute | solution.py:291
  100.9 3.9 %collective-permute-start.26 = (f32[64,128]{1,0:T(8,128)S(1)}, f32[64,128]{1,0:T(8,128)S(1)}, u32[]{:S(2)}, u32[]{:S(2)}) collective-permute-start(f32[64,128]{1,0:T(8,128)S(1)} %get-tuple-element.83.gram), channel_id=1, source_target_pairs={{0,2},{1,3},{2,0},{3,1},{4,6},{5,7},{6,4},{7,5},{8,10},{9,11},{10,... | collective-permute-start | bytes 98312 | tf_op jit(solution)/shard_map/ppermute | solution.py:288
  108.0 5.0 %collective-permute-start.29 = (bf16[64,1024]{1,0:T(8,128)(2,1)S(1)}, bf16[64,1024]{1,0:T(8,128)(2,1)S(1)}, u32[]{:S(2)}, u32[]{:S(2)}) collective-permute-start(bf16[64,1024]{1,0:T(8,128)(2,1)S(1)} %share.6), channel_id=1, source_target_pairs={{0,2},{1,3},{2,0},{3,1},{4,6},{5,7},{6,4},{7,5},{8,10},{9,11},{10,... | collective-permute-start | bytes 393224 | tf_op jit(solution)/shard_map/ppermute | solution.py:288
  115.6 9.7 %collective-permute-start.33 = (f32[32,1024]{1,0:T(8,128)S(1)}, f32[32,1024]{1,0:T(8,128)S(1)}, u32[]{:S(2)}, u32[]{:S(2)}) collective-permute-start(f32[32,1024]{1,0:T(8,128)S(1)} %get-tuple-element.88.refs_0_), channel_id=1, source_target_pairs={{0,4},{4,0},{8,12},{12,8},{16,20},{20,16},{24,28},{28,24},{1,5},{5... | collective-permute-start | bytes 393224 | tf_op jit(solution)/shard_map/ppermute | solution.py:291
  116.1 9.3 %collective-permute-start.34 = (f32[32,1024]{1,0:T(8,128)S(1)}, f32[32,1024]{1,0:T(8,128)S(1)}, u32[]{:S(2)}, u32[]{:S(2)}) collective-permute-start(f32[32,1024]{1,0:T(8,128)S(1)} %get-tuple-element.89.refs_1_), channel_id=1, source_target_pairs={{0,28},{4,8},{8,4},{12,16},{16,12},{20,24},{24,20},{28,0},{1,29},{... | collective-permute-start | bytes 393224 | tf_op jit(solution)/shard_map/ppermute | solution.py:291
  119.5 10.5 %collective-permute-start.31 = (f32[32,1024]{1,0:T(8,128)S(1)}, f32[32,1024]{1,0:T(8,128)S(1)}, u32[]{:S(2)}, u32[]{:S(2)}) collective-permute-start(f32[32,1024]{1,0:T(8,128)S(1)} %get-tuple-element.86.refs_0_), channel_id=1, source_target_pairs={{0,4},{4,0},{8,12},{12,8},{16,20},{20,16},{24,28},{28,24},{1,5},{5... | collective-permute-start | bytes 393224 | tf_op jit(solution)/shard_map/ppermute | solution.py:291
  119.6 10.4 %collective-permute-start.32 = (f32[32,1024]{1,0:T(8,128)S(1)}, f32[32,1024]{1,0:T(8,128)S(1)}, u32[]{:S(2)}, u32[]{:S(2)}) collective-permute-start(f32[32,1024]{1,0:T(8,128)S(1)} %get-tuple-element.87.refs_1_), channel_id=1, source_target_pairs={{0,28},{4,8},{8,4},{12,16},{16,12},{20,24},{24,20},{28,0},{1,29},{... | collective-permute-start | bytes 393224 | tf_op jit(solution)/shard_map/ppermute | solution.py:291
  132.9 9.5 %collective-permute-start.37 = (f32[32,1024]{1,0:T(8,128)S(1)}, f32[32,1024]{1,0:T(8,128)S(1)}, u32[]{:S(2)}, u32[]{:S(2)}) collective-permute-start(f32[32,1024]{1,0:T(8,128)S(1)} %get-tuple-element.96.even), channel_id=1, source_target_pairs={{0,4},{4,0},{8,12},{12,8},{16,20},{20,16},{24,28},{28,24},{1,5},{5... | collective-permute-start | bytes 393224 | tf_op jit(solution)/shard_map/ppermute | solution.py:291
  133.3 9.1 %collective-permute-start.38 = (f32[32,1024]{1,0:T(8,128)S(1)}, f32[32,1024]{1,0:T(8,128)S(1)}, u32[]{:S(2)}, u32[]{:S(2)}) collective-permute-start(f32[32,1024]{1,0:T(8,128)S(1)} %get-tuple-element.97.odd), channel_id=1, source_target_pairs={{0,28},{4,8},{8,4},{12,16},{16,12},{20,24},{24,20},{28,0},{1,29},{... | collective-permute-start | bytes 393224 | tf_op jit(solution)/shard_map/ppermute | solution.py:291
  142.8 7.0 %collective-permute-start.39 = (f32[64,1024]{1,0:T(8,128)S(1)}, f32[64,1024]{1,0:T(8,128)S(1)}, u32[]{:S(2)}, u32[]{:S(2)}) collective-permute-start(f32[64,1024]{1,0:T(8,128)S(1)} %share.7), channel_id=1, source_target_pairs={{0,2},{1,3},{2,0},{3,1},{4,6},{5,7},{6,4},{7,5},{8,10},{9,11},{10,... | collective-permute-start | bytes 786440 | tf_op jit(solution)/shard_map/ppermute | solution.py:288
  (9 other events, 16.1 us)

commit v4 on v3

--- a/solution.py
+++ b/solution.py
@@ -9,7 +9,9 @@
 
 POWER = 4
 MIXING = 1.0 / 3.0
+CHUNKS = 2
 LANES = 128
+PIVOTS = 4
 MIB = 1024 * 1024
 F32 = jnp.float32
 BF16 = jnp.bfloat16
@@ -67,9 +69,6 @@
     )(weight)
 
 
-CHUNKS = 2
-
-
 def first_kernel(chunk, place, own, prior, turned, even, odd, factor):
     rank, rows = even.shape
     parity = place[1]
@@ -110,14 +109,6 @@
     odd[...] = product[rank:]
 
 
-def gathered(place, pieces, factor):
-    width = pieces[0].shape[1] // 2
-    for offset, piece in enumerate(pieces):
-        low, high = slice_starts(place, offset, len(pieces), width, factor.shape[1])
-        factor[:, pl.ds(low, width)] = piece[:, :width]
-        factor[:, pl.ds(high, width)] = piece[:, width:]
-
-
 def chosen(place, bit):
     return jnp.bitwise_and(lax.div(place[0], jnp.int32(bit)), 1)
 
@@ -206,11 +197,16 @@
     row = lax.broadcasted_iota(jnp.int32, shape, 1)
     work = (gram[...] + came[...]).reshape(shape)
     work = jnp.where(lane < rank, work, jnp.where(lane - rank == row, 1.0, 0.0))
-    for k in range(rank):
-        pivot = work[:, k : k + 1, :]
-        scaled = pivot / pivot[:, :, k : k + 1]
-        column = jnp.where(row[:, :, :1] > k, work[:, :, k : k + 1], 0.0)
-        work = work - column * scaled
+    for k in range(0, rank, PIVOTS):
+        span = range(k, min(k + PIVOTS, rank))
+        columns = [jnp.broadcast_to(work[:, :, j : j + 1], shape) for j in span]
+        for i, j in enumerate(span):
+            scale = 1.0 / columns[i][:, j : j + 1, :]
+            below = jnp.where(row > j, columns[i], 0.0)
+            work = work - below * (work[:, j : j + 1, :] * scale)
+            for later in range(i + 1, len(columns)):
+                other = columns[later]
+                columns[later] = other - below * (other[:, j : j + 1, :] * scale)
     diagonal = jnp.sum(jnp.where(lane == row, work, 0.0), axis=2, keepdims=True)
     work = work / jnp.sqrt(diagonal)
     inverse[...] = work.reshape(2 * rank, LANES)[:, rank : 2 * rank]
@@ -232,17 +228,8 @@
     share[...] = value.astype(share.dtype)
 
 
-def blend_kernel(share, came, rounded):
-    rounded[...] = (share[...].astype(F32) + came[...].astype(F32)).astype(BF16)
-
-
-def final_kernel(bit, place, share, came, rounded, own):
-    rank, width = own.shape
-    value = share[...] + came[...]
-    rounded[...] = value.astype(BF16)
-    rows = pl.ds(pl.multiple_of(place[1] * rank, rank), rank)
-    columns = pl.ds(pl.multiple_of(chosen(place, bit) * width, width), width)
-    own[...] = share[rows, columns] + came[rows, columns]
+def blend_kernel(share, came, *refs):
+    refs[-1][...] = (share[...].astype(F32) + came[...].astype(F32)).astype(BF16)
 
 
 def basis_kernel(inverse, *refs):
@@ -255,18 +242,51 @@
         columns[i * rows : (i + 1) * rows, :] = basis.T.astype(BF16)
 
 
-def update_kernel(place, columns, *refs):
-    *pieces, weight, result, factor, made, sems = refs
-    gathered(place, pieces, factor)
-    tile = made.shape[0] // sems.shape[0]
-    copies = []
-    for i in range(sems.shape[0]):
-        span = slice(i * tile, (i + 1) * tile)
-        delta = jnp.dot(columns[span, :], factor[...], preferred_element_type=F32)
-        made[span, :] = (weight[span, :].astype(F32) - MIXING * delta).astype(BF16)
-        copy = pltpu.make_async_copy(made.at[span, :], result.at[span, :], sems.at[i])
+def updated(columns, piece, weight, rows, there, held):
+    delta = jnp.dot(columns[rows, :], piece[:, held], preferred_element_type=F32)
+    return (weight[rows, there].astype(F32) - MIXING * delta).astype(BF16)
+
+
+def update_own_kernel(count, place, columns, piece, weight, made):
+    rows, width = made.shape[1:]
+    tile = min(512, rows)
+    for j, start in enumerate(slice_starts(place, 0, count, width, weight.shape[1])):
+        for first in range(0, rows, tile):
+            span = slice(first, first + tile)
+            held = slice(j * width, (j + 1) * width)
+            made[j, span, :] = updated(columns, piece, weight, span, pl.ds(start, width), held)
+
+
+def update_kernel(bit, count, place, columns, *refs):
+    pieces = refs[: count - 1]
+    own_made, share, came, weight, result, own, made, value, own_sem, sems = refs[count - 1 :]
+    rank, width = own.shape
+    mine = pl.ds(pl.multiple_of(chosen(place, bit) * width, width), width)
+    ours = pl.ds(pl.multiple_of(place[1] * rank, rank), rank)
+    value[...] = share[ours, mine] + came[ours, mine]
+    copies = [pltpu.make_async_copy(value, own, own_sem)]
+    copies[0].start()
+    rows = weight.shape[0]
+
+    def put(source, index, span, there):
+        copy = pltpu.make_async_copy(source, result.at[span, there], sems.at[index])
         copy.start()
         copies.append(copy)
+
+    index = 0
+    for j, start in enumerate(slice_starts(place, 0, count, width, weight.shape[1])):
+        put(own_made.at[j], index, slice(None), pl.ds(start, width))
+        index += 1
+    tile = rows // ((sems.shape[0] - 2) // (2 * (count - 1)))
+    for i, piece in enumerate(pieces):
+        for j, start in enumerate(slice_starts(place, i + 1, count, width, weight.shape[1])):
+            there = pl.ds(start, width)
+            held = slice(j * width, (j + 1) * width)
+            for first in range(0, rows, tile):
+                span = slice(first, first + tile)
+                made[2 * i + j, span, :] = updated(columns, piece, weight, span, there, held)
+                put(made.at[2 * i + j, span, :], index, span, there)
+                index += 1
     for copy in copies:
         copy.wait()
 
@@ -313,10 +333,11 @@
     ]
     for iteration in range(POWER):
         final = iteration == POWER - 1
-        exchanged = [
-            [*pair, *(paired(product, slot) for slot, product in enumerate(pair))]
-            for pair in products
-        ]
+        even_other = paired(products[0][0], 0)
+        odd_other = paired(products[0][1], 1)
+        odd_last = paired(products[1][1], 1)
+        even_last = paired(products[1][0], 0)
+        exchanged = [(*products[0], even_other, odd_other), (*products[1], even_last, odd_last)]
         slices = shards
         half = slices // 2 * width
         both, total, gram = kernel_call(
@@ -349,28 +370,26 @@
             )
             gram = send
         gram_came = across(gram, last)
-        pair = (paired(even, 0), paired(odd, 1))
+        odd_pair = paired(odd, 1)
+        even_pair = paired(even, 0)
         inverse = kernel_call(
             inverse_kernel, out((2 * rank, rank), F32), "inverse", gram, gram_came,
             flops=1000000, moved=8 * MIB,
         )
         share = kernel_call(
             share_kernel, out((2 * rank, 2 * width), F32 if final else BF16), "share",
-            inverse, even, odd, *pair,
+            inverse, even, odd, even_pair, odd_pair,
         )
         came = across(share, last)
-        rounded_out = out((2 * rank, 2 * width), BF16)
         if final:
             columns = kernel_call(
                 basis_kernel, out((rows, 2 * rank), BF16), "basis", inverse, both, both_last,
                 mib=8, flops=8 * rank * rank * rows, moved=2 * MIB,
             )
-            rounded, new_factor = kernel_call(
-                functools.partial(final_kernel, last), (rounded_out, out((rank, width), F32)),
-                "final", place, share, came,
-            )
-        else:
-            rounded = kernel_call(blend_kernel, rounded_out, "blend", share, came)
+        rounded = kernel_call(
+            blend_kernel, out((2 * rank, 2 * width), BF16), "blend",
+            share, came, *([columns] if final else []),
+        )
         pieces = {0: rounded}
         for bit in reversed(bits[:-1]):
             for offset in list(pieces):
@@ -388,18 +407,28 @@
                 )
                 for chunk in range(CHUNKS)
             ]
-    new_weight = pl.pallas_call(
-        update_kernel,
-        out_shape=out((rows, wid), BF16),
-        in_specs=[SMEM] + [VMEM] * (len(pieces) + 2),
-        out_specs=HBM,
-        scratch_shapes=[*factor_scratch, pltpu.VMEM((rows, wid), BF16), pltpu.SemaphoreType.DMA((max(1, rows // 256),))],
-        compiler_params=pltpu.CompilerParams(vmem_limit_bytes=16 * MIB),
+    made = kernel_call(
+        functools.partial(update_own_kernel, last), out((2, rows, width), BF16), "update_own",
+        place, columns, rounded, weight, mib=8, flops=8 * rank * rows * width, moved=6 * rows * width,
+    )
+    tiles = max(1, rows // 512)
+    new_weight, new_factor = pl.pallas_call(
+        functools.partial(update_kernel, last, last),
+        out_shape=(out((rows, wid), BF16), out((rank, width), F32)),
+        in_specs=[SMEM] + [VMEM] * (last + 4),
+        out_specs=(HBM, HBM),
+        scratch_shapes=[
+            pltpu.VMEM((2 * (last - 1), rows, width), BF16),
+            pltpu.VMEM((rank, width), F32),
+            pltpu.SemaphoreType.DMA,
+            pltpu.SemaphoreType.DMA((2 + 2 * (last - 1) * tiles,)),
+        ],
+        compiler_params=pltpu.CompilerParams(vmem_limit_bytes=14 * MIB),
         cost_estimate=pl.CostEstimate(
             flops=4 * rank * rows * wid, bytes_accessed=2 * rows * wid, transcendentals=0
         ),
         name="update",
-    )(place, columns, *pieces, weight)
+    )(place, columns, *pieces[1:], made, share, came, weight)
     return (new_weight[None], new_factor[None])
 
 

time: 157 us -> 152 us (0.968)
  Pallas kernels: 49.3 us -> 42.7 us
  waiting for transfers between devices: 57.1 us -> 59.1 us
    pallas_call x40 -> x41, Pallas kernels: 40.8 us -> 34.6 us  [kernel_call(): pl.pallas_call(body, out_shape=outs, in_specs=specs, out_specs=jax.tree.m...]
    ppermute x24, waiting for transfers between devices: 26.4 us -> 29.5 us  [paired(): return lax.ppermute(value, 'blk', list(enumerate(partner[slot])))]
  transfers between devices with their start and end apart: 41 -> 41, of which waited for: 22 -> 28; matrix products, arithmetic and copies ran while one was open for 0% -> 0% of each run, Pallas kernels for 21% -> 18%
where the time goes in v4:
time: 152 us
  waiting for transfers between devices  59.1 us (39%)
  starting transfers between devices  47.9 us (32%)
  Pallas kernels  42.7 us (28%)
    pallas_call x41, Pallas kernels, kernel_call(): pl.pallas_call(body, out_shape=outs, in_specs=specs, out_specs=jax.tree.m...  34.6 us
    ppermute x24, starting transfers between devices, paired(): return lax.ppermute(value, 'blk', list(enumerate(partner[slot])))  32.2 us
    ppermute x24, waiting for transfers between devices, paired(): return lax.ppermute(value, 'blk', list(enumerate(partner[slot])))  29.5 us
    ppermute x16, waiting for transfers between devices, across(): return lax.ppermute(value, 'shard', [(i, i ^ bit) for i in range(shards)])  27.3 us
    ppermute x16, starting transfers between devices, across(): return lax.ppermute(value, 'shard', [(i, i ^ bit) for i in range(shards)])  12.7 us
    pallas_call x1, Pallas kernels, hold(): pl.pallas_call(hold_kernel, out_shape=(pltpu.VMEM((rows, wid), weight.dty...  4.11 us
    pallas_call x1, Pallas kernels, on_device(): pl.pallas_call(functools.partial(update_kernel, last, last), out_shape=(o...  3.95 us
  transfers between devices with their start and end apart: 41, of which 28 were waited for; matrix products, arithmetic and copies ran while one was open for 0% of the time, Pallas kernels for 18%

profile of v4, /device:TPU:0, one launch (start us, length us, event | category | flops | bytes accessed | tf_op | source)
XLA Modules:
  0.0 151.8 jit_solution(12830699523452410676)
XLA Ops:
  1.6 3.0 %collective-permute-start = (bf16[32,2048]{1,0:T(8,128)(2,1)S(1)}, bf16[32,2048]{1,0:T(8,128)(2,1)S(1)}, u32[]{:S(2)}, u32[]{:S(2)}) collective-permute-start(bf16[32,2048]{1,0:T(8,128)(2,1)S(1)} %convert_bitcast_fusion.own), channel_id=1, source_target_pairs={{0,4},{4,8},{8,12},{12,16},{16,20},{20,24},{24,28},{28,0},{1,5},{5... | collective-permute-start | bytes 393224 | tf_op jit(solution)/shard_map/ppermute | solution.py:315
  4.6 4.1 %hold.1 = (bf16[2048,2048]{1,0:T(8,128)(2,1)S(1)}, bf16[2048,2048]{1,0:T(8,128)(2,1)S(1)}) custom-call(bf16[2048,2048]{1,0:T(8,128)(2,1)} %bitcast.7), custom_call_target="tpu_custom_call" | custom-call | bytes 8388608 | tf_op jit(solution)/shard_map/hold/pallas_call | solution.py:60
  8.8 2.3 %collective-permute-done.prior = bf16[32,2048]{1,0:T(8,128)(2,1)S(1)} collective-permute-done((bf16[32,2048]{1,0:T(8,128)(2,1)S(1)}, bf16[32,2048]{1,0:T(8,128)(2,1)S(1)}, u32[]{:S(2)}, u32[]{:S(2)}) %collective-permute-start) | collective-permute-done | bytes 131104 | tf_op jit(solution)/shard_map/ppermute | solution.py:315
  12.6 3.1 %collective-permute-start.4 = (f32[32,1024]{1,0:T(8,128)S(1)}, f32[32,1024]{1,0:T(8,128)S(1)}, u32[]{:S(2)}, u32[]{:S(2)}) collective-permute-start(f32[32,1024]{1,0:T(8,128)S(1)} %get-tuple-element.55.refs_1_), channel_id=1, source_target_pairs={{0,28},{4,8},{8,4},{12,16},{16,12},{20,24},{24,20},{28,0},{1,29},{... | collective-permute-start | bytes 393224 | tf_op jit(solution)/shard_map/ppermute | solution.py:311
  17.2 1.9 %collective-permute-start.2 = (f32[32,1024]{1,0:T(8,128)S(1)}, f32[32,1024]{1,0:T(8,128)S(1)}, u32[]{:S(2)}, u32[]{:S(2)}) collective-permute-start(f32[32,1024]{1,0:T(8,128)S(1)} %get-tuple-element.53.refs_1_), channel_id=1, source_target_pairs={{0,28},{4,8},{8,4},{12,16},{16,12},{20,24},{24,20},{28,0},{1,29},{... | collective-permute-start | bytes 393224 | tf_op jit(solution)/shard_map/ppermute | solution.py:311
  21.5 4.5 %collective-permute-done.1.refs_2_ = f32[32,1024]{1,0:T(8,128)S(1)} collective-permute-done((f32[32,1024]{1,0:T(8,128)S(1)}, f32[32,1024]{1,0:T(8,128)S(1)}, u32[]{:S(2)}, u32[]{:S(2)}) %collective-permute-start.1) | collective-permute-done | bytes 131104 | tf_op jit(solution)/shard_map/ppermute | solution.py:311
  29.0 2.7 %collective-permute-start.8 = (f32[32,1024]{1,0:T(8,128)S(1)}, f32[32,1024]{1,0:T(8,128)S(1)}, u32[]{:S(2)}, u32[]{:S(2)}) collective-permute-start(f32[32,1024]{1,0:T(8,128)S(1)} %get-tuple-element.63.odd), channel_id=1, source_target_pairs={{0,28},{4,8},{8,4},{12,16},{16,12},{20,24},{24,20},{28,0},{1,29},{... | collective-permute-start | bytes 393224 | tf_op jit(solution)/shard_map/ppermute | solution.py:311
  33.2 2.4 %collective-permute-done.6.came = f32[64,128]{1,0:T(8,128)S(1)} collective-permute-done((f32[64,128]{1,0:T(8,128)S(1)}, f32[64,128]{1,0:T(8,128)S(1)}, u32[]{:S(2)}, u32[]{:S(2)}) %collective-permute-start.6) | collective-permute-done | bytes 32800 | tf_op jit(solution)/shard_map/ppermute | solution.py:308
  39.2 3.5 %collective-permute-done.9.came = bf16[64,1024]{1,0:T(8,128)(2,1)S(1)} collective-permute-done((bf16[64,1024]{1,0:T(8,128)(2,1)S(1)}, bf16[64,1024]{1,0:T(8,128)(2,1)S(1)}, u32[]{:S(2)}, u32[]{:S(2)}) %collective-permute-start.9) | collective-permute-done | bytes 131104 | tf_op jit(solution)/shard_map/ppermute | solution.py:308
  45.6 2.4 %collective-permute-start.14 = (f32[32,1024]{1,0:T(8,128)S(1)}, f32[32,1024]{1,0:T(8,128)S(1)}, u32[]{:S(2)}, u32[]{:S(2)}) collective-permute-start(f32[32,1024]{1,0:T(8,128)S(1)} %get-tuple-element.67.refs_1_), channel_id=1, source_target_pairs={{0,28},{4,8},{8,4},{12,16},{16,12},{20,24},{24,20},{28,0},{1,29},{... | collective-permute-start | bytes 393224 | tf_op jit(solution)/shard_map/ppermute | solution.py:311
  49.1 2.3 %collective-permute-start.12 = (f32[32,1024]{1,0:T(8,128)S(1)}, f32[32,1024]{1,0:T(8,128)S(1)}, u32[]{:S(2)}, u32[]{:S(2)}) collective-permute-start(f32[32,1024]{1,0:T(8,128)S(1)} %get-tuple-element.65.refs_1_), channel_id=1, source_target_pairs={{0,28},{4,8},{8,4},{12,16},{16,12},{20,24},{24,20},{28,0},{1,29},{... | collective-permute-start | bytes 393224 | tf_op jit(solution)/shard_map/ppermute | solution.py:311
  52.0 2.1 %collective-permute-done.14.refs_3_ = f32[32,1024]{1,0:T(8,128)S(1)} collective-permute-done((f32[32,1024]{1,0:T(8,128)S(1)}, f32[32,1024]{1,0:T(8,128)S(1)}, u32[]{:S(2)}, u32[]{:S(2)}) %collective-permute-start.14) | collective-permute-done | bytes 131104 | tf_op jit(solution)/shard_map/ppermute | solution.py:311
  55.0 4.6 %collective-permute-done.11.refs_2_ = f32[32,1024]{1,0:T(8,128)S(1)} collective-permute-done((f32[32,1024]{1,0:T(8,128)S(1)}, f32[32,1024]{1,0:T(8,128)S(1)}, u32[]{:S(2)}, u32[]{:S(2)}) %collective-permute-start.11) | collective-permute-done | bytes 131104 | tf_op jit(solution)/shard_map/ppermute | solution.py:311
  62.9 2.4 %collective-permute-start.18 = (f32[32,1024]{1,0:T(8,128)S(1)}, f32[32,1024]{1,0:T(8,128)S(1)}, u32[]{:S(2)}, u32[]{:S(2)}) collective-permute-start(f32[32,1024]{1,0:T(8,128)S(1)} %get-tuple-element.74.odd), channel_id=1, source_target_pairs={{0,28},{4,8},{8,4},{12,16},{16,12},{20,24},{24,20},{28,0},{1,29},{... | collective-permute-start | bytes 393224 | tf_op jit(solution)/shard_map/ppermute | solution.py:311
  66.8 2.4 %collective-permute-done.16.came = f32[64,128]{1,0:T(8,128)S(1)} collective-permute-done((f32[64,128]{1,0:T(8,128)S(1)}, f32[64,128]{1,0:T(8,128)S(1)}, u32[]{:S(2)}, u32[]{:S(2)}) %collective-permute-start.16) | collective-permute-done | bytes 32800 | tf_op jit(solution)/shard_map/ppermute | solution.py:308
  72.8 3.5 %collective-permute-done.19.came = bf16[64,1024]{1,0:T(8,128)(2,1)S(1)} collective-permute-done((bf16[64,1024]{1,0:T(8,128)(2,1)S(1)}, bf16[64,1024]{1,0:T(8,128)(2,1)S(1)}, u32[]{:S(2)}, u32[]{:S(2)}) %collective-permute-start.19) | collective-permute-done | bytes 131104 | tf_op jit(solution)/shard_map/ppermute | solution.py:308
  79.2 2.4 %collective-permute-start.24 = (f32[32,1024]{1,0:T(8,128)S(1)}, f32[32,1024]{1,0:T(8,128)S(1)}, u32[]{:S(2)}, u32[]{:S(2)}) collective-permute-start(f32[32,1024]{1,0:T(8,128)S(1)} %get-tuple-element.78.refs_1_), channel_id=1, source_target_pairs={{0,28},{4,8},{8,4},{12,16},{16,12},{20,24},{24,20},{28,0},{1,29},{... | collective-permute-start | bytes 393224 | tf_op jit(solution)/shard_map/ppermute | solution.py:311
  82.9 2.3 %collective-permute-start.22 = (f32[32,1024]{1,0:T(8,128)S(1)}, f32[32,1024]{1,0:T(8,128)S(1)}, u32[]{:S(2)}, u32[]{:S(2)}) collective-permute-start(f32[32,1024]{1,0:T(8,128)S(1)} %get-tuple-element.76.refs_1_), channel_id=1, source_target_pairs={{0,28},{4,8},{8,4},{12,16},{16,12},{20,24},{24,20},{28,0},{1,29},{... | collective-permute-start | bytes 393224 | tf_op jit(solution)/shard_map/ppermute | solution.py:311
  85.6 2.1 %collective-permute-done.24.refs_3_ = f32[32,1024]{1,0:T(8,128)S(1)} collective-permute-done((f32[32,1024]{1,0:T(8,128)S(1)}, f32[32,1024]{1,0:T(8,128)S(1)}, u32[]{:S(2)}, u32[]{:S(2)}) %collective-permute-start.24) | collective-permute-done | bytes 131104 | tf_op jit(solution)/shard_map/ppermute | solution.py:311
  88.7 4.6 %collective-permute-done.21.refs_2_ = f32[32,1024]{1,0:T(8,128)S(1)} collective-permute-done((f32[32,1024]{1,0:T(8,128)S(1)}, f32[32,1024]{1,0:T(8,128)S(1)}, u32[]{:S(2)}, u32[]{:S(2)}) %collective-permute-start.21) | collective-permute-done | bytes 131104 | tf_op jit(solution)/shard_map/ppermute | solution.py:311
  96.5 2.4 %collective-permute-start.28 = (f32[32,1024]{1,0:T(8,128)S(1)}, f32[32,1024]{1,0:T(8,128)S(1)}, u32[]{:S(2)}, u32[]{:S(2)}) collective-permute-start(f32[32,1024]{1,0:T(8,128)S(1)} %get-tuple-element.85.odd), channel_id=1, source_target_pairs={{0,28},{4,8},{8,4},{12,16},{16,12},{20,24},{24,20},{28,0},{1,29},{... | collective-permute-start | bytes 393224 | tf_op jit(solution)/shard_map/ppermute | solution.py:311
  100.4 2.4 %collective-permute-done.26.came = f32[64,128]{1,0:T(8,128)S(1)} collective-permute-done((f32[64,128]{1,0:T(8,128)S(1)}, f32[64,128]{1,0:T(8,128)S(1)}, u32[]{:S(2)}, u32[]{:S(2)}) %collective-permute-start.26) | collective-permute-done | bytes 32800 | tf_op jit(solution)/shard_map/ppermute | solution.py:308
  106.5 3.5 %collective-permute-done.29.came = bf16[64,1024]{1,0:T(8,128)(2,1)S(1)} collective-permute-done((bf16[64,1024]{1,0:T(8,128)(2,1)S(1)}, bf16[64,1024]{1,0:T(8,128)(2,1)S(1)}, u32[]{:S(2)}, u32[]{:S(2)}) %collective-permute-start.29) | collective-permute-done | bytes 131104 | tf_op jit(solution)/shard_map/ppermute | solution.py:308
  112.8 2.4 %collective-permute-start.34 = (f32[32,1024]{1,0:T(8,128)S(1)}, f32[32,1024]{1,0:T(8,128)S(1)}, u32[]{:S(2)}, u32[]{:S(2)}) collective-permute-start(f32[32,1024]{1,0:T(8,128)S(1)} %get-tuple-element.89.refs_1_), channel_id=1, source_target_pairs={{0,28},{4,8},{8,4},{12,16},{16,12},{20,24},{24,20},{28,0},{1,29},{... | collective-permute-start | bytes 393224 | tf_op jit(solution)/shard_map/ppermute | solution.py:311
  116.4 2.4 %collective-permute-start.32 = (f32[32,1024]{1,0:T(8,128)S(1)}, f32[32,1024]{1,0:T(8,128)S(1)}, u32[]{:S(2)}, u32[]{:S(2)}) collective-permute-start(f32[32,1024]{1,0:T(8,128)S(1)} %get-tuple-element.87.refs_1_), channel_id=1, source_target_pairs={{0,28},{4,8},{8,4},{12,16},{16,12},{20,24},{24,20},{28,0},{1,29},{... | collective-permute-start | bytes 393224 | tf_op jit(solution)/shard_map/ppermute | solution.py:311
  119.2 2.1 %collective-permute-done.34.refs_3_ = f32[32,1024]{1,0:T(8,128)S(1)} collective-permute-done((f32[32,1024]{1,0:T(8,128)S(1)}, f32[32,1024]{1,0:T(8,128)S(1)}, u32[]{:S(2)}, u32[]{:S(2)}) %collective-permute-start.34) | collective-permute-done | bytes 131104 | tf_op jit(solution)/shard_map/ppermute | solution.py:311
  122.3 4.6 %collective-permute-done.31.refs_2_ = f32[32,1024]{1,0:T(8,128)S(1)} collective-permute-done((f32[32,1024]{1,0:T(8,128)S(1)}, f32[32,1024]{1,0:T(8,128)S(1)}, u32[]{:S(2)}, u32[]{:S(2)}) %collective-permute-start.31) | collective-permute-done | bytes 131104 | tf_op jit(solution)/shard_map/ppermute | solution.py:311
  130.1 2.4 %collective-permute-start.38 = (f32[32,1024]{1,0:T(8,128)S(1)}, f32[32,1024]{1,0:T(8,128)S(1)}, u32[]{:S(2)}, u32[]{:S(2)}) collective-permute-start(f32[32,1024]{1,0:T(8,128)S(1)} %get-tuple-element.97.odd), channel_id=1, source_target_pairs={{0,28},{4,8},{8,4},{12,16},{16,12},{20,24},{24,20},{28,0},{1,29},{... | collective-permute-start | bytes 393224 | tf_op jit(solution)/shard_map/ppermute | solution.py:311
  134.0 2.4 %collective-permute-done.36.came = f32[64,128]{1,0:T(8,128)S(1)} collective-permute-done((f32[64,128]{1,0:T(8,128)S(1)}, f32[64,128]{1,0:T(8,128)S(1)}, u32[]{:S(2)}, u32[]{:S(2)}) %collective-permute-start.36) | collective-permute-done | bytes 32800 | tf_op jit(solution)/shard_map/ppermute | solution.py:308
  140.7 5.1 %collective-permute-done.39.came.refs_3_ = f32[64,1024]{1,0:T(8,128)S(1)} collective-permute-done((f32[64,1024]{1,0:T(8,128)S(1)}, f32[64,1024]{1,0:T(8,128)S(1)}, u32[]{:S(2)}, u32[]{:S(2)}) %collective-permute-start.39) | collective-permute-done | bytes 262176 | tf_op jit(solution)/shard_map/ppermute | solution.py:308
  145.9 1.8 %update_own.1.refs_1_ = bf16[2,2048,512]{2,1,0:T(8,128)(2,1)S(1)} custom-call(s32[2]{0:T(128)S(1)} %pad_add_fusion.place, bf16[2048,64]{1,0:T(8,128)(2,1)S(1)} %basis.1.refs_0_.columns, bf16[64,1024]{1,0:T(8,128)(2,1)S(1)} %blend.7.piece, bf16[2048,2048]{1,0:T(8,128)(2,1)S(1)} %get-tuple-element.56.refs_4_.refs_6_.weight), custom_call_target="tpu_custom_call" | custom-call | flops 268435456 | bytes 6291456 | tf_op jit(solution)/shard_map/update_own/pallas_call | solution.py:28
  147.7 3.9 %update.1 = (bf16[2048,2048]{1,0:T(8,128)(2,1)}, f32[32,512]{1,0:T(8,128)}) custom-call(s32[2]{0:T(128)S(1)} %pad_add_fusion.place, bf16[2048,64]{1,0:T(8,128)(2,1)S(1)} %basis.1.refs_0_.columns, bf16[64,1024]{1,0:T(8,128)(2,1)S(1)} %collective-permute-done.40.refs_0_, bf16[2,2048,512]{2,1,0:T(8,128)(2,1)S(1)} %update_own.1.refs_1_, ...), custom_call_target="tpu_custom_call" | custom-call | flops 536870912 | bytes 8388608 | tf_op jit(solution)/shard_map/update/pallas_call | solution.py:415
  (95 shorter events, 56.3 us)
Async XLA Ops:
  1.6 9.6 %collective-permute-start = (bf16[32,2048]{1,0:T(8,128)(2,1)S(1)}, bf16[32,2048]{1,0:T(8,128)(2,1)S(1)}, u32[]{:S(2)}, u32[]{:S(2)}) collective-permute-start(bf16[32,2048]{1,0:T(8,128)(2,1)S(1)} %convert_bitcast_fusion.own), channel_id=1, source_target_pairs={{0,4},{4,8},{8,12},{12,16},{16,20},{20,24},{24,28},{28,0},{1,5},{5... | collective-permute-start | bytes 393224 | tf_op jit(solution)/shard_map/ppermute | solution.py:315
  12.5 8.0 %collective-permute-start.3 = (f32[32,1024]{1,0:T(8,128)S(1)}, f32[32,1024]{1,0:T(8,128)S(1)}, u32[]{:S(2)}, u32[]{:S(2)}) collective-permute-start(f32[32,1024]{1,0:T(8,128)S(1)} %get-tuple-element.54.refs_0_), channel_id=1, source_target_pairs={{0,4},{4,0},{8,12},{12,8},{16,20},{20,16},{24,28},{28,24},{1,5},{5... | collective-permute-start | bytes 393224 | tf_op jit(solution)/shard_map/ppermute | solution.py:311
  12.6 7.9 %collective-permute-start.4 = (f32[32,1024]{1,0:T(8,128)S(1)}, f32[32,1024]{1,0:T(8,128)S(1)}, u32[]{:S(2)}, u32[]{:S(2)}) collective-permute-start(f32[32,1024]{1,0:T(8,128)S(1)} %get-tuple-element.55.refs_1_), channel_id=1, source_target_pairs={{0,28},{4,8},{8,4},{12,16},{16,12},{20,24},{24,20},{28,0},{1,29},{... | collective-permute-start | bytes 393224 | tf_op jit(solution)/shard_map/ppermute | solution.py:311
  17.1 8.9 %collective-permute-start.1 = (f32[32,1024]{1,0:T(8,128)S(1)}, f32[32,1024]{1,0:T(8,128)S(1)}, u32[]{:S(2)}, u32[]{:S(2)}) collective-permute-start(f32[32,1024]{1,0:T(8,128)S(1)} %get-tuple-element.52.refs_0_), channel_id=1, source_target_pairs={{0,4},{4,0},{8,12},{12,8},{16,20},{20,16},{24,28},{28,24},{1,5},{5... | collective-permute-start | bytes 393224 | tf_op jit(solution)/shard_map/ppermute | solution.py:311
  17.2 8.8 %collective-permute-start.2 = (f32[32,1024]{1,0:T(8,128)S(1)}, f32[32,1024]{1,0:T(8,128)S(1)}, u32[]{:S(2)}, u32[]{:S(2)}) collective-permute-start(f32[32,1024]{1,0:T(8,128)S(1)} %get-tuple-element.53.refs_1_), channel_id=1, source_target_pairs={{0,28},{4,8},{8,4},{12,16},{16,12},{20,24},{24,20},{28,0},{1,29},{... | collective-permute-start | bytes 393224 | tf_op jit(solution)/shard_map/ppermute | solution.py:311
  28.9 7.8 %collective-permute-start.7 = (f32[32,1024]{1,0:T(8,128)S(1)}, f32[32,1024]{1,0:T(8,128)S(1)}, u32[]{:S(2)}, u32[]{:S(2)}) collective-permute-start(f32[32,1024]{1,0:T(8,128)S(1)} %get-tuple-element.62.even), channel_id=1, source_target_pairs={{0,4},{4,0},{8,12},{12,8},{16,20},{20,16},{24,28},{28,24},{1,5},{5... | collective-permute-start | bytes 393224 | tf_op jit(solution)/shard_map/ppermute | solution.py:311
  29.0 8.3 %collective-permute-start.8 = (f32[32,1024]{1,0:T(8,128)S(1)}, f32[32,1024]{1,0:T(8,128)S(1)}, u32[]{:S(2)}, u32[]{:S(2)}) collective-permute-start(f32[32,1024]{1,0:T(8,128)S(1)} %get-tuple-element.63.odd), channel_id=1, source_target_pairs={{0,28},{4,8},{8,4},{12,16},{16,12},{20,24},{24,20},{28,0},{1,29},{... | collective-permute-start | bytes 393224 | tf_op jit(solution)/shard_map/ppermute | solution.py:311
  37.6 5.0 %collective-permute-start.9 = (bf16[64,1024]{1,0:T(8,128)(2,1)S(1)}, bf16[64,1024]{1,0:T(8,128)(2,1)S(1)}, u32[]{:S(2)}, u32[]{:S(2)}) collective-permute-start(bf16[64,1024]{1,0:T(8,128)(2,1)S(1)} %share.4), channel_id=1, source_target_pairs={{0,2},{1,3},{2,0},{3,1},{4,6},{5,7},{6,4},{7,5},{8,10},{9,11},{10,... | collective-permute-start | bytes 393224 | tf_op jit(solution)/shard_map/ppermute | solution.py:308
  45.2 6.7 %collective-permute-start.13 = (f32[32,1024]{1,0:T(8,128)S(1)}, f32[32,1024]{1,0:T(8,128)S(1)}, u32[]{:S(2)}, u32[]{:S(2)}) collective-permute-start(f32[32,1024]{1,0:T(8,128)S(1)} %get-tuple-element.66.refs_0_), channel_id=1, source_target_pairs={{0,4},{4,0},{8,12},{12,8},{16,20},{20,16},{24,28},{28,24},{1,5},{5... | collective-permute-start | bytes 393224 | tf_op jit(solution)/shard_map/ppermute | solution.py:311
  45.6 8.5 %collective-permute-start.14 = (f32[32,1024]{1,0:T(8,128)S(1)}, f32[32,1024]{1,0:T(8,128)S(1)}, u32[]{:S(2)}, u32[]{:S(2)}) collective-permute-start(f32[32,1024]{1,0:T(8,128)S(1)} %get-tuple-element.67.refs_1_), channel_id=1, source_target_pairs={{0,28},{4,8},{8,4},{12,16},{16,12},{20,24},{24,20},{28,0},{1,29},{... | collective-permute-start | bytes 393224 | tf_op jit(solution)/shard_map/ppermute | solution.py:311
  49.1 10.6 %collective-permute-start.11 = (f32[32,1024]{1,0:T(8,128)S(1)}, f32[32,1024]{1,0:T(8,128)S(1)}, u32[]{:S(2)}, u32[]{:S(2)}) collective-permute-start(f32[32,1024]{1,0:T(8,128)S(1)} %get-tuple-element.64.refs_0_), channel_id=1, source_target_pairs={{0,4},{4,0},{8,12},{12,8},{16,20},{20,16},{24,28},{28,24},{1,5},{5... | collective-permute-start | bytes 393224 | tf_op jit(solution)/shard_map/ppermute | solution.py:311
  49.1 10.5 %collective-permute-start.12 = (f32[32,1024]{1,0:T(8,128)S(1)}, f32[32,1024]{1,0:T(8,128)S(1)}, u32[]{:S(2)}, u32[]{:S(2)}) collective-permute-start(f32[32,1024]{1,0:T(8,128)S(1)} %get-tuple-element.65.refs_1_), channel_id=1, source_target_pairs={{0,28},{4,8},{8,4},{12,16},{16,12},{20,24},{24,20},{28,0},{1,29},{... | collective-permute-start | bytes 393224 | tf_op jit(solution)/shard_map/ppermute | solution.py:311
  62.5 7.8 %collective-permute-start.17 = (f32[32,1024]{1,0:T(8,128)S(1)}, f32[32,1024]{1,0:T(8,128)S(1)}, u32[]{:S(2)}, u32[]{:S(2)}) collective-permute-start(f32[32,1024]{1,0:T(8,128)S(1)} %get-tuple-element.73.even), channel_id=1, source_target_pairs={{0,4},{4,0},{8,12},{12,8},{16,20},{20,16},{24,28},{28,24},{1,5},{5... | collective-permute-start | bytes 393224 | tf_op jit(solution)/shard_map/ppermute | solution.py:311
  62.9 8.1 %collective-permute-start.18 = (f32[32,1024]{1,0:T(8,128)S(1)}, f32[32,1024]{1,0:T(8,128)S(1)}, u32[]{:S(2)}, u32[]{:S(2)}) collective-permute-start(f32[32,1024]{1,0:T(8,128)S(1)} %get-tuple-element.74.odd), channel_id=1, source_target_pairs={{0,28},{4,8},{8,4},{12,16},{16,12},{20,24},{24,20},{28,0},{1,29},{... | collective-permute-start | bytes 393224 | tf_op jit(solution)/shard_map/ppermute | solution.py:311
  65.3 3.9 %collective-permute-start.16 = (f32[64,128]{1,0:T(8,128)S(1)}, f32[64,128]{1,0:T(8,128)S(1)}, u32[]{:S(2)}, u32[]{:S(2)}) collective-permute-start(f32[64,128]{1,0:T(8,128)S(1)} %get-tuple-element.72.gram), channel_id=1, source_target_pairs={{0,2},{1,3},{2,0},{3,1},{4,6},{5,7},{6,4},{7,5},{8,10},{9,11},{10,... | collective-permute-start | bytes 98312 | tf_op jit(solution)/shard_map/ppermute | solution.py:308
  71.3 5.0 %collective-permute-start.19 = (bf16[64,1024]{1,0:T(8,128)(2,1)S(1)}, bf16[64,1024]{1,0:T(8,128)(2,1)S(1)}, u32[]{:S(2)}, u32[]{:S(2)}) collective-permute-start(bf16[64,1024]{1,0:T(8,128)(2,1)S(1)} %share.5), channel_id=1, source_target_pairs={{0,2},{1,3},{2,0},{3,1},{4,6},{5,7},{6,4},{7,5},{8,10},{9,11},{10,... | collective-permute-start | bytes 393224 | tf_op jit(solution)/shard_map/ppermute | solution.py:308
  78.9 6.7 %collective-permute-start.23 = (f32[32,1024]{1,0:T(8,128)S(1)}, f32[32,1024]{1,0:T(8,128)S(1)}, u32[]{:S(2)}, u32[]{:S(2)}) collective-permute-start(f32[32,1024]{1,0:T(8,128)S(1)} %get-tuple-element.77.refs_0_), channel_id=1, source_target_pairs={{0,4},{4,0},{8,12},{12,8},{16,20},{20,16},{24,28},{28,24},{1,5},{5... | collective-permute-start | bytes 393224 | tf_op jit(solution)/shard_map/ppermute | solution.py:311
  79.2 8.5 %collective-permute-start.24 = (f32[32,1024]{1,0:T(8,128)S(1)}, f32[32,1024]{1,0:T(8,128)S(1)}, u32[]{:S(2)}, u32[]{:S(2)}) collective-permute-start(f32[32,1024]{1,0:T(8,128)S(1)} %get-tuple-element.78.refs_1_), channel_id=1, source_target_pairs={{0,28},{4,8},{8,4},{12,16},{16,12},{20,24},{24,20},{28,0},{1,29},{... | collective-permute-start | bytes 393224 | tf_op jit(solution)/shard_map/ppermute | solution.py:311
  82.7 10.6 %collective-permute-start.21 = (f32[32,1024]{1,0:T(8,128)S(1)}, f32[32,1024]{1,0:T(8,128)S(1)}, u32[]{:S(2)}, u32[]{:S(2)}) collective-permute-start(f32[32,1024]{1,0:T(8,128)S(1)} %get-tuple-element.75.refs_0_), channel_id=1, source_target_pairs={{0,4},{4,0},{8,12},{12,8},{16,20},{20,16},{24,28},{28,24},{1,5},{5... | collective-permute-start | bytes 393224 | tf_op jit(solution)/shard_map/ppermute | solution.py:311
  82.9 10.3 %collective-permute-start.22 = (f32[32,1024]{1,0:T(8,128)S(1)}, f32[32,1024]{1,0:T(8,128)S(1)}, u32[]{:S(2)}, u32[]{:S(2)}) collective-permute-start(f32[32,1024]{1,0:T(8,128)S(1)} %get-tuple-element.76.refs_1_), channel_id=1, source_target_pairs={{0,28},{4,8},{8,4},{12,16},{16,12},{20,24},{24,20},{28,0},{1,29},{... | collective-permute-start | bytes 393224 | tf_op jit(solution)/shard_map/ppermute | solution.py:311
  96.1 7.8 %collective-permute-start.27 = (f32[32,1024]{1,0:T(8,128)S(1)}, f32[32,1024]{1,0:T(8,128)S(1)}, u32[]{:S(2)}, u32[]{:S(2)}) collective-permute-start(f32[32,1024]{1,0:T(8,128)S(1)} %get-tuple-element.84.even), channel_id=1, source_target_pairs={{0,4},{4,0},{8,12},{12,8},{16,20},{20,16},{24,28},{28,24},{1,5},{5... | collective-permute-start | bytes 393224 | tf_op jit(solution)/shard_map/ppermute | solution.py:311
  96.5 8.0 %collective-permute-start.28 = (f32[32,1024]{1,0:T(8,128)S(1)}, f32[32,1024]{1,0:T(8,128)S(1)}, u32[]{:S(2)}, u32[]{:S(2)}) collective-permute-start(f32[32,1024]{1,0:T(8,128)S(1)} %get-tuple-element.85.odd), channel_id=1, source_target_pairs={{0,28},{4,8},{8,4},{12,16},{16,12},{20,24},{24,20},{28,0},{1,29},{... | collective-permute-start | bytes 393224 | tf_op jit(solution)/shard_map/ppermute | solution.py:311
  98.9 3.9 %collective-permute-start.26 = (f32[64,128]{1,0:T(8,128)S(1)}, f32[64,128]{1,0:T(8,128)S(1)}, u32[]{:S(2)}, u32[]{:S(2)}) collective-permute-start(f32[64,128]{1,0:T(8,128)S(1)} %get-tuple-element.83.gram), channel_id=1, source_target_pairs={{0,2},{1,3},{2,0},{3,1},{4,6},{5,7},{6,4},{7,5},{8,10},{9,11},{10,... | collective-permute-start | bytes 98312 | tf_op jit(solution)/shard_map/ppermute | solution.py:308
  104.9 5.0 %collective-permute-start.29 = (bf16[64,1024]{1,0:T(8,128)(2,1)S(1)}, bf16[64,1024]{1,0:T(8,128)(2,1)S(1)}, u32[]{:S(2)}, u32[]{:S(2)}) collective-permute-start(bf16[64,1024]{1,0:T(8,128)(2,1)S(1)} %share.6), channel_id=1, source_target_pairs={{0,2},{1,3},{2,0},{3,1},{4,6},{5,7},{6,4},{7,5},{8,10},{9,11},{10,... | collective-permute-start | bytes 393224 | tf_op jit(solution)/shard_map/ppermute | solution.py:308
  112.5 6.7 %collective-permute-start.33 = (f32[32,1024]{1,0:T(8,128)S(1)}, f32[32,1024]{1,0:T(8,128)S(1)}, u32[]{:S(2)}, u32[]{:S(2)}) collective-permute-start(f32[32,1024]{1,0:T(8,128)S(1)} %get-tuple-element.88.refs_0_), channel_id=1, source_target_pairs={{0,4},{4,0},{8,12},{12,8},{16,20},{20,16},{24,28},{28,24},{1,5},{5... | collective-permute-start | bytes 393224 | tf_op jit(solution)/shard_map/ppermute | solution.py:311
  112.8 8.5 %collective-permute-start.34 = (f32[32,1024]{1,0:T(8,128)S(1)}, f32[32,1024]{1,0:T(8,128)S(1)}, u32[]{:S(2)}, u32[]{:S(2)}) collective-permute-start(f32[32,1024]{1,0:T(8,128)S(1)} %get-tuple-element.89.refs_1_), channel_id=1, source_target_pairs={{0,28},{4,8},{8,4},{12,16},{16,12},{20,24},{24,20},{28,0},{1,29},{... | collective-permute-start | bytes 393224 | tf_op jit(solution)/shard_map/ppermute | solution.py:311
  116.3 10.6 %collective-permute-start.31 = (f32[32,1024]{1,0:T(8,128)S(1)}, f32[32,1024]{1,0:T(8,128)S(1)}, u32[]{:S(2)}, u32[]{:S(2)}) collective-permute-start(f32[32,1024]{1,0:T(8,128)S(1)} %get-tuple-element.86.refs_0_), channel_id=1, source_target_pairs={{0,4},{4,0},{8,12},{12,8},{16,20},{20,16},{24,28},{28,24},{1,5},{5... | collective-permute-start | bytes 393224 | tf_op jit(solution)/shard_map/ppermute | solution.py:311
  116.4 10.5 %collective-permute-start.32 = (f32[32,1024]{1,0:T(8,128)S(1)}, f32[32,1024]{1,0:T(8,128)S(1)}, u32[]{:S(2)}, u32[]{:S(2)}) collective-permute-start(f32[32,1024]{1,0:T(8,128)S(1)} %get-tuple-element.87.refs_1_), channel_id=1, source_target_pairs={{0,28},{4,8},{8,4},{12,16},{16,12},{20,24},{24,20},{28,0},{1,29},{... | collective-permute-start | bytes 393224 | tf_op jit(solution)/shard_map/ppermute | solution.py:311
  129.7 7.9 %collective-permute-start.37 = (f32[32,1024]{1,0:T(8,128)S(1)}, f32[32,1024]{1,0:T(8,128)S(1)}, u32[]{:S(2)}, u32[]{:S(2)}) collective-permute-start(f32[32,1024]{1,0:T(8,128)S(1)} %get-tuple-element.96.even), channel_id=1, source_target_pairs={{0,4},{4,0},{8,12},{12,8},{16,20},{20,16},{24,28},{28,24},{1,5},{5... | collective-permute-start | bytes 393224 | tf_op jit(solution)/shard_map/ppermute | solution.py:311
  130.1 8.0 %collective-permute-start.38 = (f32[32,1024]{1,0:T(8,128)S(1)}, f32[32,1024]{1,0:T(8,128)S(1)}, u32[]{:S(2)}, u32[]{:S(2)}) collective-permute-start(f32[32,1024]{1,0:T(8,128)S(1)} %get-tuple-element.97.odd), channel_id=1, source_target_pairs={{0,28},{4,8},{8,4},{12,16},{16,12},{20,24},{24,20},{28,0},{1,29},{... | collective-permute-start | bytes 393224 | tf_op jit(solution)/shard_map/ppermute | solution.py:311
  132.6 3.9 %collective-permute-start.36 = (f32[64,128]{1,0:T(8,128)S(1)}, f32[64,128]{1,0:T(8,128)S(1)}, u32[]{:S(2)}, u32[]{:S(2)}) collective-permute-start(f32[64,128]{1,0:T(8,128)S(1)} %get-tuple-element.94.gram), channel_id=1, source_target_pairs={{0,2},{1,3},{2,0},{3,1},{4,6},{5,7},{6,4},{7,5},{8,10},{9,11},{10,... | collective-permute-start | bytes 98312 | tf_op jit(solution)/shard_map/ppermute | solution.py:308
  138.5 7.3 %collective-permute-start.39 = (f32[64,1024]{1,0:T(8,128)S(1)}, f32[64,1024]{1,0:T(8,128)S(1)}, u32[]{:S(2)}, u32[]{:S(2)}) collective-permute-start(f32[64,1024]{1,0:T(8,128)S(1)} %share.7.refs_2_), channel_id=1, source_target_pairs={{0,2},{1,3},{2,0},{3,1},{4,6},{5,7},{6,4},{7,5},{8,10},{9,11},{10,... | collective-permute-start | bytes 786440 | tf_op jit(solution)/shard_map/ppermute | solution.py:308
  (9 other events, 16.6 us)

commit v5 on v4

--- a/solution.py
+++ b/solution.py
@@ -12,6 +12,7 @@
 CHUNKS = 2
 LANES = 128
 PIVOTS = 4
+TILE = 512
 MIB = 1024 * 1024
 F32 = jnp.float32
 BF16 = jnp.bfloat16
@@ -232,6 +233,16 @@
     refs[-1][...] = (share[...].astype(F32) + came[...].astype(F32)).astype(BF16)
 
 
+def slice_kernel(bit, place, inverse, even, odd, even_pair, odd_pair, own):
+    rank, width = own.shape
+    mine = pl.ds(pl.multiple_of(chosen(place, bit) * width, width), width)
+    total = jnp.where(
+        place[1] == 0, even[:, mine] + even_pair[:, mine], odd[:, mine] + odd_pair[:, mine]
+    )
+    lower = jnp.where(place[1] == 0, inverse[:rank, :], inverse[rank:, :])
+    own[...] = jnp.dot(lower, total, precision=HIGHEST, preferred_element_type=F32)
+
+
 def basis_kernel(inverse, *refs):
     *chunks, columns = refs
     for i, both in enumerate(chunks):
@@ -249,7 +260,7 @@
 
 def update_own_kernel(count, place, columns, piece, weight, made):
     rows, width = made.shape[1:]
-    tile = min(512, rows)
+    tile = min(TILE, rows)
     for j, start in enumerate(slice_starts(place, 0, count, width, weight.shape[1])):
         for first in range(0, rows, tile):
             span = slice(first, first + tile)
@@ -259,11 +270,11 @@
 
 def update_kernel(bit, count, place, columns, *refs):
     pieces = refs[: count - 1]
-    own_made, share, came, weight, result, own, made, value, own_sem, sems = refs[count - 1 :]
+    own_made, factor, came, weight, result, own, made, value, own_sem, sems = refs[count - 1 :]
     rank, width = own.shape
     mine = pl.ds(pl.multiple_of(chosen(place, bit) * width, width), width)
     ours = pl.ds(pl.multiple_of(place[1] * rank, rank), rank)
-    value[...] = share[ours, mine] + came[ours, mine]
+    value[...] = factor[...] + came[ours, mine].astype(F32)
     copies = [pltpu.make_async_copy(value, own, own_sem)]
     copies[0].start()
     rows = weight.shape[0]
@@ -377,7 +388,7 @@
             flops=1000000, moved=8 * MIB,
         )
         share = kernel_call(
-            share_kernel, out((2 * rank, 2 * width), F32 if final else BF16), "share",
+            share_kernel, out((2 * rank, 2 * width), BF16), "share",
             inverse, even, odd, even_pair, odd_pair,
         )
         came = across(share, last)
@@ -386,9 +397,13 @@
                 basis_kernel, out((rows, 2 * rank), BF16), "basis", inverse, both, both_last,
                 mib=8, flops=8 * rank * rank * rows, moved=2 * MIB,
             )
+            factor = kernel_call(
+                functools.partial(slice_kernel, last), out((rank, width), F32), "slice",
+                place, inverse, even, odd, even_pair, odd_pair,
+            )
         rounded = kernel_call(
             blend_kernel, out((2 * rank, 2 * width), BF16), "blend",
-            share, came, *([columns] if final else []),
+            share, came, *([columns, factor] if final else []),
         )
         pieces = {0: rounded}
         for bit in reversed(bits[:-1]):
@@ -411,7 +426,7 @@
         functools.partial(update_own_kernel, last), out((2, rows, width), BF16), "update_own",
         place, columns, rounded, weight, mib=8, flops=8 * rank * rows * width, moved=6 * rows * width,
     )
-    tiles = max(1, rows // 512)
+    tiles = max(1, rows // TILE)
     new_weight, new_factor = pl.pallas_call(
         functools.partial(update_kernel, last, last),
         out_shape=(out((rows, wid), BF16), out((rank, width), F32)),
@@ -428,7 +443,7 @@
             flops=4 * rank * rows * wid, bytes_accessed=2 * rows * wid, transcendentals=0
         ),
         name="update",
-    )(place, columns, *pieces[1:], made, share, came, weight)
+    )(place, columns, *pieces[1:], made, factor, came, weight)
     return (new_weight[None], new_factor[None])
 
 

time: 152 us -> 150 us (0.987)
  waiting for transfers between devices: 59.1 us -> 56 us
    ppermute x16, waiting for transfers between devices: 27.3 us -> 24.3 us  [across(): return lax.ppermute(value, 'shard', [(i, i ^ bit) for i in range(shards)])]
    pallas_call x41 -> x42, Pallas kernels: 34.6 us -> 35.4 us  [kernel_call(): pl.pallas_call(body, out_shape=outs, in_specs=specs, out_specs=jax.tree.m...]
  transfers between devices with their start and end apart: 41 -> 41, of which waited for: 28 -> 28; matrix products, arithmetic and copies ran while one was open for 0% -> 0% of each run, Pallas kernels for 18% -> 19%
where the time goes in v5:
time: 150 us
  waiting for transfers between devices  56 us (37%)
  starting transfers between devices  47.9 us (32%)
  Pallas kernels  43.4 us (29%)
    pallas_call x42, Pallas kernels, kernel_call(): pl.pallas_call(body, out_shape=outs, in_specs=specs, out_specs=jax.tree.m...  35.4 us
    ppermute x24, starting transfers between devices, paired(): return lax.ppermute(value, 'blk', list(enumerate(partner[slot])))  32.2 us
    ppermute x24, waiting for transfers between devices, paired(): return lax.ppermute(value, 'blk', list(enumerate(partner[slot])))  29.5 us
    ppermute x16, waiting for transfers between devices, across(): return lax.ppermute(value, 'shard', [(i, i ^ bit) for i in range(shards)])  24.3 us
    ppermute x16, starting transfers between devices, across(): return lax.ppermute(value, 'shard', [(i, i ^ bit) for i in range(shards)])  12.7 us
    pallas_call x1, Pallas kernels, hold(): pl.pallas_call(hold_kernel, out_shape=(pltpu.VMEM((rows, wid), weight.dty...  4.11 us
    pallas_call x1, Pallas kernels, on_device(): pl.pallas_call(functools.partial(update_kernel, last, last), out_shape=(o...  3.95 us
    ppermute x1, starting transfers between devices, on_device(): lax.ppermute(own, 'blk', [(i, (i + 1) % peers) for i in range(peers)])  3.02 us
  transfers between devices with their start and end apart: 41, of which 28 were waited for; matrix products, arithmetic and copies ran while one was open for 0% of the time, Pallas kernels for 19%

profile of v5, /device:TPU:0, one launch (start us, length us, event | category | flops | bytes accessed | tf_op | source)
XLA Modules:
  0.0 149.6 jit_solution(10269247686374423258)
XLA Ops:
  1.6 3.0 %collective-permute-start = (bf16[32,2048]{1,0:T(8,128)(2,1)S(1)}, bf16[32,2048]{1,0:T(8,128)(2,1)S(1)}, u32[]{:S(2)}, u32[]{:S(2)}) collective-permute-start(bf16[32,2048]{1,0:T(8,128)(2,1)S(1)} %convert_bitcast_fusion.own), channel_id=1, source_target_pairs={{0,4},{4,8},{8,12},{12,16},{16,20},{20,24},{24,28},{28,0},{1,5},{5... | collective-permute-start | bytes 393224 | tf_op jit(solution)/shard_map/ppermute | solution.py:326
  4.6 4.1 %hold.1 = (bf16[2048,2048]{1,0:T(8,128)(2,1)S(1)}, bf16[2048,2048]{1,0:T(8,128)(2,1)S(1)}) custom-call(bf16[2048,2048]{1,0:T(8,128)(2,1)} %bitcast.7), custom_call_target="tpu_custom_call" | custom-call | bytes 8388608 | tf_op jit(solution)/shard_map/hold/pallas_call | solution.py:61
  8.8 2.3 %collective-permute-done.prior = bf16[32,2048]{1,0:T(8,128)(2,1)S(1)} collective-permute-done((bf16[32,2048]{1,0:T(8,128)(2,1)S(1)}, bf16[32,2048]{1,0:T(8,128)(2,1)S(1)}, u32[]{:S(2)}, u32[]{:S(2)}) %collective-permute-start) | collective-permute-done | bytes 131104 | tf_op jit(solution)/shard_map/ppermute | solution.py:326
  12.6 3.1 %collective-permute-start.4 = (f32[32,1024]{1,0:T(8,128)S(1)}, f32[32,1024]{1,0:T(8,128)S(1)}, u32[]{:S(2)}, u32[]{:S(2)}) collective-permute-start(f32[32,1024]{1,0:T(8,128)S(1)} %get-tuple-element.55.refs_1_), channel_id=1, source_target_pairs={{0,28},{4,8},{8,4},{12,16},{16,12},{20,24},{24,20},{28,0},{1,29},{... | collective-permute-start | bytes 393224 | tf_op jit(solution)/shard_map/ppermute | solution.py:322
  17.2 1.9 %collective-permute-start.2 = (f32[32,1024]{1,0:T(8,128)S(1)}, f32[32,1024]{1,0:T(8,128)S(1)}, u32[]{:S(2)}, u32[]{:S(2)}) collective-permute-start(f32[32,1024]{1,0:T(8,128)S(1)} %get-tuple-element.53.refs_1_), channel_id=1, source_target_pairs={{0,28},{4,8},{8,4},{12,16},{16,12},{20,24},{24,20},{28,0},{1,29},{... | collective-permute-start | bytes 393224 | tf_op jit(solution)/shard_map/ppermute | solution.py:322
  21.5 4.5 %collective-permute-done.1.refs_2_ = f32[32,1024]{1,0:T(8,128)S(1)} collective-permute-done((f32[32,1024]{1,0:T(8,128)S(1)}, f32[32,1024]{1,0:T(8,128)S(1)}, u32[]{:S(2)}, u32[]{:S(2)}) %collective-permute-start.1) | collective-permute-done | bytes 131104 | tf_op jit(solution)/shard_map/ppermute | solution.py:322
  29.0 2.7 %collective-permute-start.8 = (f32[32,1024]{1,0:T(8,128)S(1)}, f32[32,1024]{1,0:T(8,128)S(1)}, u32[]{:S(2)}, u32[]{:S(2)}) collective-permute-start(f32[32,1024]{1,0:T(8,128)S(1)} %get-tuple-element.63.odd), channel_id=1, source_target_pairs={{0,28},{4,8},{8,4},{12,16},{16,12},{20,24},{24,20},{28,0},{1,29},{... | collective-permute-start | bytes 393224 | tf_op jit(solution)/shard_map/ppermute | solution.py:322
  33.2 2.4 %collective-permute-done.6.came = f32[64,128]{1,0:T(8,128)S(1)} collective-permute-done((f32[64,128]{1,0:T(8,128)S(1)}, f32[64,128]{1,0:T(8,128)S(1)}, u32[]{:S(2)}, u32[]{:S(2)}) %collective-permute-start.6) | collective-permute-done | bytes 32800 | tf_op jit(solution)/shard_map/ppermute | solution.py:319
  39.2 3.5 %collective-permute-done.9.came = bf16[64,1024]{1,0:T(8,128)(2,1)S(1)} collective-permute-done((bf16[64,1024]{1,0:T(8,128)(2,1)S(1)}, bf16[64,1024]{1,0:T(8,128)(2,1)S(1)}, u32[]{:S(2)}, u32[]{:S(2)}) %collective-permute-start.9) | collective-permute-done | bytes 131104 | tf_op jit(solution)/shard_map/ppermute | solution.py:319
  45.6 2.4 %collective-permute-start.14 = (f32[32,1024]{1,0:T(8,128)S(1)}, f32[32,1024]{1,0:T(8,128)S(1)}, u32[]{:S(2)}, u32[]{:S(2)}) collective-permute-start(f32[32,1024]{1,0:T(8,128)S(1)} %get-tuple-element.67.refs_1_), channel_id=1, source_target_pairs={{0,28},{4,8},{8,4},{12,16},{16,12},{20,24},{24,20},{28,0},{1,29},{... | collective-permute-start | bytes 393224 | tf_op jit(solution)/shard_map/ppermute | solution.py:322
  49.1 2.3 %collective-permute-start.12 = (f32[32,1024]{1,0:T(8,128)S(1)}, f32[32,1024]{1,0:T(8,128)S(1)}, u32[]{:S(2)}, u32[]{:S(2)}) collective-permute-start(f32[32,1024]{1,0:T(8,128)S(1)} %get-tuple-element.65.refs_1_), channel_id=1, source_target_pairs={{0,28},{4,8},{8,4},{12,16},{16,12},{20,24},{24,20},{28,0},{1,29},{... | collective-permute-start | bytes 393224 | tf_op jit(solution)/shard_map/ppermute | solution.py:322
  52.0 2.1 %collective-permute-done.14.refs_3_ = f32[32,1024]{1,0:T(8,128)S(1)} collective-permute-done((f32[32,1024]{1,0:T(8,128)S(1)}, f32[32,1024]{1,0:T(8,128)S(1)}, u32[]{:S(2)}, u32[]{:S(2)}) %collective-permute-start.14) | collective-permute-done | bytes 131104 | tf_op jit(solution)/shard_map/ppermute | solution.py:322
  55.0 4.6 %collective-permute-done.11.refs_2_ = f32[32,1024]{1,0:T(8,128)S(1)} collective-permute-done((f32[32,1024]{1,0:T(8,128)S(1)}, f32[32,1024]{1,0:T(8,128)S(1)}, u32[]{:S(2)}, u32[]{:S(2)}) %collective-permute-start.11) | collective-permute-done | bytes 131104 | tf_op jit(solution)/shard_map/ppermute | solution.py:322
  62.9 2.4 %collective-permute-start.18 = (f32[32,1024]{1,0:T(8,128)S(1)}, f32[32,1024]{1,0:T(8,128)S(1)}, u32[]{:S(2)}, u32[]{:S(2)}) collective-permute-start(f32[32,1024]{1,0:T(8,128)S(1)} %get-tuple-element.74.odd), channel_id=1, source_target_pairs={{0,28},{4,8},{8,4},{12,16},{16,12},{20,24},{24,20},{28,0},{1,29},{... | collective-permute-start | bytes 393224 | tf_op jit(solution)/shard_map/ppermute | solution.py:322
  66.8 2.4 %collective-permute-done.16.came = f32[64,128]{1,0:T(8,128)S(1)} collective-permute-done((f32[64,128]{1,0:T(8,128)S(1)}, f32[64,128]{1,0:T(8,128)S(1)}, u32[]{:S(2)}, u32[]{:S(2)}) %collective-permute-start.16) | collective-permute-done | bytes 32800 | tf_op jit(solution)/shard_map/ppermute | solution.py:319
  72.8 3.5 %collective-permute-done.19.came = bf16[64,1024]{1,0:T(8,128)(2,1)S(1)} collective-permute-done((bf16[64,1024]{1,0:T(8,128)(2,1)S(1)}, bf16[64,1024]{1,0:T(8,128)(2,1)S(1)}, u32[]{:S(2)}, u32[]{:S(2)}) %collective-permute-start.19) | collective-permute-done | bytes 131104 | tf_op jit(solution)/shard_map/ppermute | solution.py:319
  79.2 2.4 %collective-permute-start.24 = (f32[32,1024]{1,0:T(8,128)S(1)}, f32[32,1024]{1,0:T(8,128)S(1)}, u32[]{:S(2)}, u32[]{:S(2)}) collective-permute-start(f32[32,1024]{1,0:T(8,128)S(1)} %get-tuple-element.78.refs_1_), channel_id=1, source_target_pairs={{0,28},{4,8},{8,4},{12,16},{16,12},{20,24},{24,20},{28,0},{1,29},{... | collective-permute-start | bytes 393224 | tf_op jit(solution)/shard_map/ppermute | solution.py:322
  82.9 2.3 %collective-permute-start.22 = (f32[32,1024]{1,0:T(8,128)S(1)}, f32[32,1024]{1,0:T(8,128)S(1)}, u32[]{:S(2)}, u32[]{:S(2)}) collective-permute-start(f32[32,1024]{1,0:T(8,128)S(1)} %get-tuple-element.76.refs_1_), channel_id=1, source_target_pairs={{0,28},{4,8},{8,4},{12,16},{16,12},{20,24},{24,20},{28,0},{1,29},{... | collective-permute-start | bytes 393224 | tf_op jit(solution)/shard_map/ppermute | solution.py:322
  85.6 2.1 %collective-permute-done.24.refs_3_ = f32[32,1024]{1,0:T(8,128)S(1)} collective-permute-done((f32[32,1024]{1,0:T(8,128)S(1)}, f32[32,1024]{1,0:T(8,128)S(1)}, u32[]{:S(2)}, u32[]{:S(2)}) %collective-permute-start.24) | collective-permute-done | bytes 131104 | tf_op jit(solution)/shard_map/ppermute | solution.py:322
  88.7 4.6 %collective-permute-done.21.refs_2_ = f32[32,1024]{1,0:T(8,128)S(1)} collective-permute-done((f32[32,1024]{1,0:T(8,128)S(1)}, f32[32,1024]{1,0:T(8,128)S(1)}, u32[]{:S(2)}, u32[]{:S(2)}) %collective-permute-start.21) | collective-permute-done | bytes 131104 | tf_op jit(solution)/shard_map/ppermute | solution.py:322
  96.5 2.4 %collective-permute-start.28 = (f32[32,1024]{1,0:T(8,128)S(1)}, f32[32,1024]{1,0:T(8,128)S(1)}, u32[]{:S(2)}, u32[]{:S(2)}) collective-permute-start(f32[32,1024]{1,0:T(8,128)S(1)} %get-tuple-element.85.odd), channel_id=1, source_target_pairs={{0,28},{4,8},{8,4},{12,16},{16,12},{20,24},{24,20},{28,0},{1,29},{... | collective-permute-start | bytes 393224 | tf_op jit(solution)/shard_map/ppermute | solution.py:322
  100.4 2.4 %collective-permute-done.26.came = f32[64,128]{1,0:T(8,128)S(1)} collective-permute-done((f32[64,128]{1,0:T(8,128)S(1)}, f32[64,128]{1,0:T(8,128)S(1)}, u32[]{:S(2)}, u32[]{:S(2)}) %collective-permute-start.26) | collective-permute-done | bytes 32800 | tf_op jit(solution)/shard_map/ppermute | solution.py:319
  106.5 3.5 %collective-permute-done.29.came = bf16[64,1024]{1,0:T(8,128)(2,1)S(1)} collective-permute-done((bf16[64,1024]{1,0:T(8,128)(2,1)S(1)}, bf16[64,1024]{1,0:T(8,128)(2,1)S(1)}, u32[]{:S(2)}, u32[]{:S(2)}) %collective-permute-start.29) | collective-permute-done | bytes 131104 | tf_op jit(solution)/shard_map/ppermute | solution.py:319
  112.8 2.4 %collective-permute-start.34 = (f32[32,1024]{1,0:T(8,128)S(1)}, f32[32,1024]{1,0:T(8,128)S(1)}, u32[]{:S(2)}, u32[]{:S(2)}) collective-permute-start(f32[32,1024]{1,0:T(8,128)S(1)} %get-tuple-element.89.refs_1_), channel_id=1, source_target_pairs={{0,28},{4,8},{8,4},{12,16},{16,12},{20,24},{24,20},{28,0},{1,29},{... | collective-permute-start | bytes 393224 | tf_op jit(solution)/shard_map/ppermute | solution.py:322
  116.4 2.4 %collective-permute-start.32 = (f32[32,1024]{1,0:T(8,128)S(1)}, f32[32,1024]{1,0:T(8,128)S(1)}, u32[]{:S(2)}, u32[]{:S(2)}) collective-permute-start(f32[32,1024]{1,0:T(8,128)S(1)} %get-tuple-element.87.refs_1_), channel_id=1, source_target_pairs={{0,28},{4,8},{8,4},{12,16},{16,12},{20,24},{24,20},{28,0},{1,29},{... | collective-permute-start | bytes 393224 | tf_op jit(solution)/shard_map/ppermute | solution.py:322
  119.2 2.1 %collective-permute-done.34.refs_3_ = f32[32,1024]{1,0:T(8,128)S(1)} collective-permute-done((f32[32,1024]{1,0:T(8,128)S(1)}, f32[32,1024]{1,0:T(8,128)S(1)}, u32[]{:S(2)}, u32[]{:S(2)}) %collective-permute-start.34) | collective-permute-done | bytes 131104 | tf_op jit(solution)/shard_map/ppermute | solution.py:322
  122.3 4.6 %collective-permute-done.31.refs_2_ = f32[32,1024]{1,0:T(8,128)S(1)} collective-permute-done((f32[32,1024]{1,0:T(8,128)S(1)}, f32[32,1024]{1,0:T(8,128)S(1)}, u32[]{:S(2)}, u32[]{:S(2)}) %collective-permute-start.31) | collective-permute-done | bytes 131104 | tf_op jit(solution)/shard_map/ppermute | solution.py:322
  130.1 2.4 %collective-permute-start.38 = (f32[32,1024]{1,0:T(8,128)S(1)}, f32[32,1024]{1,0:T(8,128)S(1)}, u32[]{:S(2)}, u32[]{:S(2)}) collective-permute-start(f32[32,1024]{1,0:T(8,128)S(1)} %get-tuple-element.97.odd), channel_id=1, source_target_pairs={{0,28},{4,8},{8,4},{12,16},{16,12},{20,24},{24,20},{28,0},{1,29},{... | collective-permute-start | bytes 393224 | tf_op jit(solution)/shard_map/ppermute | solution.py:322
  134.0 2.4 %collective-permute-done.36.came = f32[64,128]{1,0:T(8,128)S(1)} collective-permute-done((f32[64,128]{1,0:T(8,128)S(1)}, f32[64,128]{1,0:T(8,128)S(1)}, u32[]{:S(2)}, u32[]{:S(2)}) %collective-permute-start.36) | collective-permute-done | bytes 32800 | tf_op jit(solution)/shard_map/ppermute | solution.py:319
  141.5 2.1 %collective-permute-done.39.came.refs_3_ = bf16[64,1024]{1,0:T(8,128)(2,1)S(1)} collective-permute-done((bf16[64,1024]{1,0:T(8,128)(2,1)S(1)}, bf16[64,1024]{1,0:T(8,128)(2,1)S(1)}, u32[]{:S(2)}, u32[]{:S(2)}) %collective-permute-start.39) | collective-permute-done | bytes 131104 | tf_op jit(solution)/shard_map/ppermute | solution.py:319
  143.7 1.8 %update_own.1.refs_1_ = bf16[2,2048,512]{2,1,0:T(8,128)(2,1)S(1)} custom-call(s32[2]{0:T(128)S(1)} %pad_add_fusion.place, bf16[2048,64]{1,0:T(8,128)(2,1)S(1)} %basis.1.refs_0_.columns, bf16[64,1024]{1,0:T(8,128)(2,1)S(1)} %blend.7.piece, bf16[2048,2048]{1,0:T(8,128)(2,1)S(1)} %get-tuple-element.56.refs_4_.refs_6_.weight), custom_call_target="tpu_custom_call" | custom-call | flops 268435456 | bytes 6291456 | tf_op jit(solution)/shard_map/update_own/pallas_call | solution.py:29
  145.5 3.9 %update.1 = (bf16[2048,2048]{1,0:T(8,128)(2,1)}, f32[32,512]{1,0:T(8,128)}) custom-call(s32[2]{0:T(128)S(1)} %pad_add_fusion.place, bf16[2048,64]{1,0:T(8,128)(2,1)S(1)} %basis.1.refs_0_.columns, bf16[64,1024]{1,0:T(8,128)(2,1)S(1)} %collective-permute-done.40.refs_0_, bf16[2,2048,512]{2,1,0:T(8,128)(2,1)S(1)} %update_own.1.refs_1_, ...), custom_call_target="tpu_custom_call" | custom-call | flops 536870912 | bytes 8388608 | tf_op jit(solution)/shard_map/update/pallas_call | solution.py:430
  (96 shorter events, 57.1 us)
Async XLA Ops:
  1.6 9.6 %collective-permute-start = (bf16[32,2048]{1,0:T(8,128)(2,1)S(1)}, bf16[32,2048]{1,0:T(8,128)(2,1)S(1)}, u32[]{:S(2)}, u32[]{:S(2)}) collective-permute-start(bf16[32,2048]{1,0:T(8,128)(2,1)S(1)} %convert_bitcast_fusion.own), channel_id=1, source_target_pairs={{0,4},{4,8},{8,12},{12,16},{16,20},{20,24},{24,28},{28,0},{1,5},{5... | collective-permute-start | bytes 393224 | tf_op jit(solution)/shard_map/ppermute | solution.py:326
  12.5 8.0 %collective-permute-start.3 = (f32[32,1024]{1,0:T(8,128)S(1)}, f32[32,1024]{1,0:T(8,128)S(1)}, u32[]{:S(2)}, u32[]{:S(2)}) collective-permute-start(f32[32,1024]{1,0:T(8,128)S(1)} %get-tuple-element.54.refs_0_), channel_id=1, source_target_pairs={{0,4},{4,0},{8,12},{12,8},{16,20},{20,16},{24,28},{28,24},{1,5},{5... | collective-permute-start | bytes 393224 | tf_op jit(solution)/shard_map/ppermute | solution.py:322
  12.6 7.9 %collective-permute-start.4 = (f32[32,1024]{1,0:T(8,128)S(1)}, f32[32,1024]{1,0:T(8,128)S(1)}, u32[]{:S(2)}, u32[]{:S(2)}) collective-permute-start(f32[32,1024]{1,0:T(8,128)S(1)} %get-tuple-element.55.refs_1_), channel_id=1, source_target_pairs={{0,28},{4,8},{8,4},{12,16},{16,12},{20,24},{24,20},{28,0},{1,29},{... | collective-permute-start | bytes 393224 | tf_op jit(solution)/shard_map/ppermute | solution.py:322
  17.1 8.9 %collective-permute-start.1 = (f32[32,1024]{1,0:T(8,128)S(1)}, f32[32,1024]{1,0:T(8,128)S(1)}, u32[]{:S(2)}, u32[]{:S(2)}) collective-permute-start(f32[32,1024]{1,0:T(8,128)S(1)} %get-tuple-element.52.refs_0_), channel_id=1, source_target_pairs={{0,4},{4,0},{8,12},{12,8},{16,20},{20,16},{24,28},{28,24},{1,5},{5... | collective-permute-start | bytes 393224 | tf_op jit(solution)/shard_map/ppermute | solution.py:322
  17.2 8.8 %collective-permute-start.2 = (f32[32,1024]{1,0:T(8,128)S(1)}, f32[32,1024]{1,0:T(8,128)S(1)}, u32[]{:S(2)}, u32[]{:S(2)}) collective-permute-start(f32[32,1024]{1,0:T(8,128)S(1)} %get-tuple-element.53.refs_1_), channel_id=1, source_target_pairs={{0,28},{4,8},{8,4},{12,16},{16,12},{20,24},{24,20},{28,0},{1,29},{... | collective-permute-start | bytes 393224 | tf_op jit(solution)/shard_map/ppermute | solution.py:322
  28.9 7.8 %collective-permute-start.7 = (f32[32,1024]{1,0:T(8,128)S(1)}, f32[32,1024]{1,0:T(8,128)S(1)}, u32[]{:S(2)}, u32[]{:S(2)}) collective-permute-start(f32[32,1024]{1,0:T(8,128)S(1)} %get-tuple-element.62.even), channel_id=1, source_target_pairs={{0,4},{4,0},{8,12},{12,8},{16,20},{20,16},{24,28},{28,24},{1,5},{5... | collective-permute-start | bytes 393224 | tf_op jit(solution)/shard_map/ppermute | solution.py:322
  29.0 8.3 %collective-permute-start.8 = (f32[32,1024]{1,0:T(8,128)S(1)}, f32[32,1024]{1,0:T(8,128)S(1)}, u32[]{:S(2)}, u32[]{:S(2)}) collective-permute-start(f32[32,1024]{1,0:T(8,128)S(1)} %get-tuple-element.63.odd), channel_id=1, source_target_pairs={{0,28},{4,8},{8,4},{12,16},{16,12},{20,24},{24,20},{28,0},{1,29},{... | collective-permute-start | bytes 393224 | tf_op jit(solution)/shard_map/ppermute | solution.py:322
  31.7 3.9 %collective-permute-start.6 = (f32[64,128]{1,0:T(8,128)S(1)}, f32[64,128]{1,0:T(8,128)S(1)}, u32[]{:S(2)}, u32[]{:S(2)}) collective-permute-start(f32[64,128]{1,0:T(8,128)S(1)} %get-tuple-element.61.gram), channel_id=1, source_target_pairs={{0,2},{1,3},{2,0},{3,1},{4,6},{5,7},{6,4},{7,5},{8,10},{9,11},{10,... | collective-permute-start | bytes 98312 | tf_op jit(solution)/shard_map/ppermute | solution.py:319
  37.6 5.0 %collective-permute-start.9 = (bf16[64,1024]{1,0:T(8,128)(2,1)S(1)}, bf16[64,1024]{1,0:T(8,128)(2,1)S(1)}, u32[]{:S(2)}, u32[]{:S(2)}) collective-permute-start(bf16[64,1024]{1,0:T(8,128)(2,1)S(1)} %share.4), channel_id=1, source_target_pairs={{0,2},{1,3},{2,0},{3,1},{4,6},{5,7},{6,4},{7,5},{8,10},{9,11},{10,... | collective-permute-start | bytes 393224 | tf_op jit(solution)/shard_map/ppermute | solution.py:319
  45.2 6.7 %collective-permute-start.13 = (f32[32,1024]{1,0:T(8,128)S(1)}, f32[32,1024]{1,0:T(8,128)S(1)}, u32[]{:S(2)}, u32[]{:S(2)}) collective-permute-start(f32[32,1024]{1,0:T(8,128)S(1)} %get-tuple-element.66.refs_0_), channel_id=1, source_target_pairs={{0,4},{4,0},{8,12},{12,8},{16,20},{20,16},{24,28},{28,24},{1,5},{5... | collective-permute-start | bytes 393224 | tf_op jit(solution)/shard_map/ppermute | solution.py:322
  45.6 8.5 %collective-permute-start.14 = (f32[32,1024]{1,0:T(8,128)S(1)}, f32[32,1024]{1,0:T(8,128)S(1)}, u32[]{:S(2)}, u32[]{:S(2)}) collective-permute-start(f32[32,1024]{1,0:T(8,128)S(1)} %get-tuple-element.67.refs_1_), channel_id=1, source_target_pairs={{0,28},{4,8},{8,4},{12,16},{16,12},{20,24},{24,20},{28,0},{1,29},{... | collective-permute-start | bytes 393224 | tf_op jit(solution)/shard_map/ppermute | solution.py:322
  49.1 10.6 %collective-permute-start.11 = (f32[32,1024]{1,0:T(8,128)S(1)}, f32[32,1024]{1,0:T(8,128)S(1)}, u32[]{:S(2)}, u32[]{:S(2)}) collective-permute-start(f32[32,1024]{1,0:T(8,128)S(1)} %get-tuple-element.64.refs_0_), channel_id=1, source_target_pairs={{0,4},{4,0},{8,12},{12,8},{16,20},{20,16},{24,28},{28,24},{1,5},{5... | collective-permute-start | bytes 393224 | tf_op jit(solution)/shard_map/ppermute | solution.py:322
  49.1 10.5 %collective-permute-start.12 = (f32[32,1024]{1,0:T(8,128)S(1)}, f32[32,1024]{1,0:T(8,128)S(1)}, u32[]{:S(2)}, u32[]{:S(2)}) collective-permute-start(f32[32,1024]{1,0:T(8,128)S(1)} %get-tuple-element.65.refs_1_), channel_id=1, source_target_pairs={{0,28},{4,8},{8,4},{12,16},{16,12},{20,24},{24,20},{28,0},{1,29},{... | collective-permute-start | bytes 393224 | tf_op jit(solution)/shard_map/ppermute | solution.py:322
  62.5 7.8 %collective-permute-start.17 = (f32[32,1024]{1,0:T(8,128)S(1)}, f32[32,1024]{1,0:T(8,128)S(1)}, u32[]{:S(2)}, u32[]{:S(2)}) collective-permute-start(f32[32,1024]{1,0:T(8,128)S(1)} %get-tuple-element.73.even), channel_id=1, source_target_pairs={{0,4},{4,0},{8,12},{12,8},{16,20},{20,16},{24,28},{28,24},{1,5},{5... | collective-permute-start | bytes 393224 | tf_op jit(solution)/shard_map/ppermute | solution.py:322
  62.9 8.1 %collective-permute-start.18 = (f32[32,1024]{1,0:T(8,128)S(1)}, f32[32,1024]{1,0:T(8,128)S(1)}, u32[]{:S(2)}, u32[]{:S(2)}) collective-permute-start(f32[32,1024]{1,0:T(8,128)S(1)} %get-tuple-element.74.odd), channel_id=1, source_target_pairs={{0,28},{4,8},{8,4},{12,16},{16,12},{20,24},{24,20},{28,0},{1,29},{... | collective-permute-start | bytes 393224 | tf_op jit(solution)/shard_map/ppermute | solution.py:322
  65.3 3.9 %collective-permute-start.16 = (f32[64,128]{1,0:T(8,128)S(1)}, f32[64,128]{1,0:T(8,128)S(1)}, u32[]{:S(2)}, u32[]{:S(2)}) collective-permute-start(f32[64,128]{1,0:T(8,128)S(1)} %get-tuple-element.72.gram), channel_id=1, source_target_pairs={{0,2},{1,3},{2,0},{3,1},{4,6},{5,7},{6,4},{7,5},{8,10},{9,11},{10,... | collective-permute-start | bytes 98312 | tf_op jit(solution)/shard_map/ppermute | solution.py:319
  71.3 5.0 %collective-permute-start.19 = (bf16[64,1024]{1,0:T(8,128)(2,1)S(1)}, bf16[64,1024]{1,0:T(8,128)(2,1)S(1)}, u32[]{:S(2)}, u32[]{:S(2)}) collective-permute-start(bf16[64,1024]{1,0:T(8,128)(2,1)S(1)} %share.5), channel_id=1, source_target_pairs={{0,2},{1,3},{2,0},{3,1},{4,6},{5,7},{6,4},{7,5},{8,10},{9,11},{10,... | collective-permute-start | bytes 393224 | tf_op jit(solution)/shard_map/ppermute | solution.py:319
  78.9 6.7 %collective-permute-start.23 = (f32[32,1024]{1,0:T(8,128)S(1)}, f32[32,1024]{1,0:T(8,128)S(1)}, u32[]{:S(2)}, u32[]{:S(2)}) collective-permute-start(f32[32,1024]{1,0:T(8,128)S(1)} %get-tuple-element.77.refs_0_), channel_id=1, source_target_pairs={{0,4},{4,0},{8,12},{12,8},{16,20},{20,16},{24,28},{28,24},{1,5},{5... | collective-permute-start | bytes 393224 | tf_op jit(solution)/shard_map/ppermute | solution.py:322
  79.2 8.5 %collective-permute-start.24 = (f32[32,1024]{1,0:T(8,128)S(1)}, f32[32,1024]{1,0:T(8,128)S(1)}, u32[]{:S(2)}, u32[]{:S(2)}) collective-permute-start(f32[32,1024]{1,0:T(8,128)S(1)} %get-tuple-element.78.refs_1_), channel_id=1, source_target_pairs={{0,28},{4,8},{8,4},{12,16},{16,12},{20,24},{24,20},{28,0},{1,29},{... | collective-permute-start | bytes 393224 | tf_op jit(solution)/shard_map/ppermute | solution.py:322
  82.7 10.6 %collective-permute-start.21 = (f32[32,1024]{1,0:T(8,128)S(1)}, f32[32,1024]{1,0:T(8,128)S(1)}, u32[]{:S(2)}, u32[]{:S(2)}) collective-permute-start(f32[32,1024]{1,0:T(8,128)S(1)} %get-tuple-element.75.refs_0_), channel_id=1, source_target_pairs={{0,4},{4,0},{8,12},{12,8},{16,20},{20,16},{24,28},{28,24},{1,5},{5... | collective-permute-start | bytes 393224 | tf_op jit(solution)/shard_map/ppermute | solution.py:322
  82.9 10.3 %collective-permute-start.22 = (f32[32,1024]{1,0:T(8,128)S(1)}, f32[32,1024]{1,0:T(8,128)S(1)}, u32[]{:S(2)}, u32[]{:S(2)}) collective-permute-start(f32[32,1024]{1,0:T(8,128)S(1)} %get-tuple-element.76.refs_1_), channel_id=1, source_target_pairs={{0,28},{4,8},{8,4},{12,16},{16,12},{20,24},{24,20},{28,0},{1,29},{... | collective-permute-start | bytes 393224 | tf_op jit(solution)/shard_map/ppermute | solution.py:322
  96.1 7.8 %collective-permute-start.27 = (f32[32,1024]{1,0:T(8,128)S(1)}, f32[32,1024]{1,0:T(8,128)S(1)}, u32[]{:S(2)}, u32[]{:S(2)}) collective-permute-start(f32[32,1024]{1,0:T(8,128)S(1)} %get-tuple-element.84.even), channel_id=1, source_target_pairs={{0,4},{4,0},{8,12},{12,8},{16,20},{20,16},{24,28},{28,24},{1,5},{5... | collective-permute-start | bytes 393224 | tf_op jit(solution)/shard_map/ppermute | solution.py:322
  96.5 8.0 %collective-permute-start.28 = (f32[32,1024]{1,0:T(8,128)S(1)}, f32[32,1024]{1,0:T(8,128)S(1)}, u32[]{:S(2)}, u32[]{:S(2)}) collective-permute-start(f32[32,1024]{1,0:T(8,128)S(1)} %get-tuple-element.85.odd), channel_id=1, source_target_pairs={{0,28},{4,8},{8,4},{12,16},{16,12},{20,24},{24,20},{28,0},{1,29},{... | collective-permute-start | bytes 393224 | tf_op jit(solution)/shard_map/ppermute | solution.py:322
  98.9 3.9 %collective-permute-start.26 = (f32[64,128]{1,0:T(8,128)S(1)}, f32[64,128]{1,0:T(8,128)S(1)}, u32[]{:S(2)}, u32[]{:S(2)}) collective-permute-start(f32[64,128]{1,0:T(8,128)S(1)} %get-tuple-element.83.gram), channel_id=1, source_target_pairs={{0,2},{1,3},{2,0},{3,1},{4,6},{5,7},{6,4},{7,5},{8,10},{9,11},{10,... | collective-permute-start | bytes 98312 | tf_op jit(solution)/shard_map/ppermute | solution.py:319
  104.9 5.0 %collective-permute-start.29 = (bf16[64,1024]{1,0:T(8,128)(2,1)S(1)}, bf16[64,1024]{1,0:T(8,128)(2,1)S(1)}, u32[]{:S(2)}, u32[]{:S(2)}) collective-permute-start(bf16[64,1024]{1,0:T(8,128)(2,1)S(1)} %share.6), channel_id=1, source_target_pairs={{0,2},{1,3},{2,0},{3,1},{4,6},{5,7},{6,4},{7,5},{8,10},{9,11},{10,... | collective-permute-start | bytes 393224 | tf_op jit(solution)/shard_map/ppermute | solution.py:319
  112.5 6.7 %collective-permute-start.33 = (f32[32,1024]{1,0:T(8,128)S(1)}, f32[32,1024]{1,0:T(8,128)S(1)}, u32[]{:S(2)}, u32[]{:S(2)}) collective-permute-start(f32[32,1024]{1,0:T(8,128)S(1)} %get-tuple-element.88.refs_0_), channel_id=1, source_target_pairs={{0,4},{4,0},{8,12},{12,8},{16,20},{20,16},{24,28},{28,24},{1,5},{5... | collective-permute-start | bytes 393224 | tf_op jit(solution)/shard_map/ppermute | solution.py:322
  112.8 8.5 %collective-permute-start.34 = (f32[32,1024]{1,0:T(8,128)S(1)}, f32[32,1024]{1,0:T(8,128)S(1)}, u32[]{:S(2)}, u32[]{:S(2)}) collective-permute-start(f32[32,1024]{1,0:T(8,128)S(1)} %get-tuple-element.89.refs_1_), channel_id=1, source_target_pairs={{0,28},{4,8},{8,4},{12,16},{16,12},{20,24},{24,20},{28,0},{1,29},{... | collective-permute-start | bytes 393224 | tf_op jit(solution)/shard_map/ppermute | solution.py:322
  116.3 10.6 %collective-permute-start.31 = (f32[32,1024]{1,0:T(8,128)S(1)}, f32[32,1024]{1,0:T(8,128)S(1)}, u32[]{:S(2)}, u32[]{:S(2)}) collective-permute-start(f32[32,1024]{1,0:T(8,128)S(1)} %get-tuple-element.86.refs_0_), channel_id=1, source_target_pairs={{0,4},{4,0},{8,12},{12,8},{16,20},{20,16},{24,28},{28,24},{1,5},{5... | collective-permute-start | bytes 393224 | tf_op jit(solution)/shard_map/ppermute | solution.py:322
  116.4 10.5 %collective-permute-start.32 = (f32[32,1024]{1,0:T(8,128)S(1)}, f32[32,1024]{1,0:T(8,128)S(1)}, u32[]{:S(2)}, u32[]{:S(2)}) collective-permute-start(f32[32,1024]{1,0:T(8,128)S(1)} %get-tuple-element.87.refs_1_), channel_id=1, source_target_pairs={{0,28},{4,8},{8,4},{12,16},{16,12},{20,24},{24,20},{28,0},{1,29},{... | collective-permute-start | bytes 393224 | tf_op jit(solution)/shard_map/ppermute | solution.py:322
  129.7 7.8 %collective-permute-start.37 = (f32[32,1024]{1,0:T(8,128)S(1)}, f32[32,1024]{1,0:T(8,128)S(1)}, u32[]{:S(2)}, u32[]{:S(2)}) collective-permute-start(f32[32,1024]{1,0:T(8,128)S(1)} %get-tuple-element.96.even), channel_id=1, source_target_pairs={{0,4},{4,0},{8,12},{12,8},{16,20},{20,16},{24,28},{28,24},{1,5},{5... | collective-permute-start | bytes 393224 | tf_op jit(solution)/shard_map/ppermute | solution.py:322
  130.1 8.0 %collective-permute-start.38 = (f32[32,1024]{1,0:T(8,128)S(1)}, f32[32,1024]{1,0:T(8,128)S(1)}, u32[]{:S(2)}, u32[]{:S(2)}) collective-permute-start(f32[32,1024]{1,0:T(8,128)S(1)} %get-tuple-element.97.odd), channel_id=1, source_target_pairs={{0,28},{4,8},{8,4},{12,16},{16,12},{20,24},{24,20},{28,0},{1,29},{... | collective-permute-start | bytes 393224 | tf_op jit(solution)/shard_map/ppermute | solution.py:322
  138.5 5.0 %collective-permute-start.39 = (bf16[64,1024]{1,0:T(8,128)(2,1)S(1)}, bf16[64,1024]{1,0:T(8,128)(2,1)S(1)}, u32[]{:S(2)}, u32[]{:S(2)}) collective-permute-start(bf16[64,1024]{1,0:T(8,128)(2,1)S(1)} %share.7), channel_id=1, source_target_pairs={{0,2},{1,3},{2,0},{3,1},{4,6},{5,7},{6,4},{7,5},{8,10},{9,11},{10,... | collective-permute-start | bytes 393224 | tf_op jit(solution)/shard_map/ppermute | solution.py:319
  (9 other events, 16.6 us)

commit v6 on v5

--- a/solution.py
+++ b/solution.py
@@ -10,6 +10,7 @@
 POWER = 4
 MIXING = 1.0 / 3.0
 CHUNKS = 2
+FIRST_EIGHTHS = 5
 LANES = 128
 PIVOTS = 4
 TILE = 512
@@ -70,13 +71,17 @@
     )(weight)
 
 
+def chunk_span(chunk, rows, whole):
+    return slice(0, rows) if chunk == 0 else slice(whole - rows, whole)
+
+
 def first_kernel(chunk, place, own, prior, turned, even, odd, factor):
     rank, rows = even.shape
     parity = place[1]
     factor[pl.ds(pl.multiple_of(parity * rank, rank), rank), :] = own[...]
     factor[pl.ds(pl.multiple_of((1 - parity) * rank, rank), rank), :] = prior[...]
     product = jnp.dot(
-        factor[...], turned[:, chunk * rows : (chunk + 1) * rows], preferred_element_type=F32
+        factor[...], turned[:, chunk_span(chunk, rows, turned.shape[1])], preferred_element_type=F32
     )
     even[...] = product[:rank]
     odd[...] = product[rank:]
@@ -102,7 +107,7 @@
 def next_kernel(chunk, place, *refs):
     *pieces, partial, turned, even, odd = refs
     rank, rows = even.shape
-    columns = slice(chunk * rows, (chunk + 1) * rows)
+    columns = chunk_span(chunk, rows, turned.shape[1])
     product = partial[:, columns]
     for offset, piece in enumerate(pieces, 1):
         product += piece_product(place, offset, len(pieces) + 1, piece, turned, columns)
@@ -145,7 +150,7 @@
     split_raw(*products, both)
     total[...] = folded(
         jnp.dot(
-            both[...], weight[chunk * rows : (chunk + 1) * rows, :], preferred_element_type=F32
+            both[...], weight[chunk_span(chunk, rows, weight.shape[0]), :], preferred_element_type=F32
         )
     )
     gram[...] = gram_of(both)
@@ -245,12 +250,14 @@
 
 def basis_kernel(inverse, *refs):
     *chunks, columns = refs
-    for i, both in enumerate(chunks):
+    start = 0
+    for both in chunks:
         rank2 = both.shape[0] // 2
         rows = both.shape[1]
         raw = both[:rank2, :].astype(F32) + both[rank2:, :].astype(F32)
         basis = normalised(inverse[...], raw[: rank2 // 2], raw[rank2 // 2 :])
-        columns[i * rows : (i + 1) * rows, :] = basis.T.astype(BF16)
+        columns[start : start + rows, :] = basis.T.astype(BF16)
+        start += rows
 
 
 def updated(columns, piece, weight, rows, there, held):
@@ -327,17 +334,18 @@
     weight, turned = hold(weights[0])
     rows = weight.shape[0]
     width = wid // shards
-    chunk_rows = rows // CHUNKS
-    cost = dict(flops=4 * rank * chunk_rows * wid, moved=chunk_rows * wid * 2)
-    product_outs = (out((rank, chunk_rows), F32), out((rank, chunk_rows), F32))
+    first_rows = rows * FIRST_EIGHTHS // 8 // LANES * LANES
+    chunks = (first_rows, rows - first_rows)
+    cost = dict(flops=2 * rank * rows * wid, moved=rows * wid)
+    product_outs = [(out((rank, chunk), F32),) * 2 for chunk in chunks]
     factor_scratch = [pltpu.VMEM((2 * rank, wid), BF16)]
     gram_out = out((2 * rank, LANES), F32)
-    both_out = out((4 * rank, chunk_rows), BF16)
+    both_outs = [out((4 * rank, chunk), BF16) for chunk in chunks]
     part_out = out((rank, 2 * width), F32)
 
     products = [
         kernel_call(
-            functools.partial(first_kernel, chunk), product_outs, "first",
+            functools.partial(first_kernel, chunk), product_outs[chunk], "first",
             place, own, prior, turned, scratch=factor_scratch, mib=8, **cost,
         )
         for chunk in range(CHUNKS)
@@ -352,12 +360,12 @@
         slices = shards
         half = slices // 2 * width
         both, total, gram = kernel_call(
-            functools.partial(back_kernel, 0), (both_out, out((2 * rank, wid), F32), gram_out),
+            functools.partial(back_kernel, 0), (both_outs[0], out((2 * rank, wid), F32), gram_out),
             "back", *exchanged[0], weight, mib=8, **cost,
         )
         both_last, send = kernel_call(
             functools.partial(back_send_kernel, slices),
-            (both_out, out((2 * rank, half + LANES), F32)), "back_send",
+            (both_outs[1], out((2 * rank, half + LANES), F32)), "back_send",
             place, *exchanged[1], total, gram, weight, mib=8, **cost,
         )
         keep = kernel_call(
@@ -417,7 +425,7 @@
             )
             products = [
                 kernel_call(
-                    functools.partial(next_kernel, chunk), product_outs, "next",
+                    functools.partial(next_kernel, chunk), product_outs[chunk], "next",
                     place, *pieces[1:], partial, turned, mib=8, **cost,
                 )
                 for chunk in range(CHUNKS)

time: 150 us -> 150 us (level)
    ppermute x24, waiting for transfers between devices: 29.5 us -> 27.5 us  [paired(): return lax.ppermute(value, 'blk', list(enumerate(partner[slot])))]
  transfers between devices with their start and end apart: 41 -> 41, of which waited for: 28 -> 25; matrix products, arithmetic and copies ran while one was open for 0% -> 0% of each run, Pallas kernels for 19% -> 19%
where the time goes in v6:
time: 150 us; the launch traced here: 149 us
  waiting for transfers between devices  54.8 us (37%)
  starting transfers between devices  48.8 us (33%)
  Pallas kernels  43.5 us (29%)
    pallas_call x42, Pallas kernels, kernel_call(): pl.pallas_call(body, out_shape=outs, in_specs=specs, out_specs=jax.tree.m...  35.5 us
    ppermute x24, starting transfers between devices, paired(): return lax.ppermute(value, 'blk', list(enumerate(partner[slot])))  33.5 us
    ppermute x24, waiting for transfers between devices, paired(): return lax.ppermute(value, 'blk', list(enumerate(partner[slot])))  27.5 us
    ppermute x16, waiting for transfers between devices, across(): return lax.ppermute(value, 'shard', [(i, i ^ bit) for i in range(shards)])  24.9 us
    ppermute x16, starting transfers between devices, across(): return lax.ppermute(value, 'shard', [(i, i ^ bit) for i in range(shards)])  12.3 us
    pallas_call x1, Pallas kernels, hold(): pl.pallas_call(hold_kernel, out_shape=(pltpu.VMEM((rows, wid), weight.dty...  4.11 us
    pallas_call x1, Pallas kernels, on_device(): pl.pallas_call(functools.partial(update_kernel, last, last), out_shape=(o...  3.95 us
    ppermute x1, starting transfers between devices, on_device(): lax.ppermute(own, 'blk', [(i, (i + 1) % peers) for i in range(peers)])  3.02 us
  transfers between devices with their start and end apart: 41, of which 25 were waited for; matrix products, arithmetic and copies ran while one was open for 0% of the time, Pallas kernels for 19%

profile of v6, /device:TPU:0, one launch (start us, length us, event | category | flops | bytes accessed | tf_op | source)
XLA Modules:
  0.0 149.3 jit_solution(15515781231871893522)
XLA Ops:
  1.6 3.0 %collective-permute-start = (bf16[32,2048]{1,0:T(8,128)(2,1)S(1)}, bf16[32,2048]{1,0:T(8,128)(2,1)S(1)}, u32[]{:S(2)}, u32[]{:S(2)}) collective-permute-start(bf16[32,2048]{1,0:T(8,128)(2,1)S(1)} %convert_bitcast_fusion.own), channel_id=1, source_target_pairs={{0,4},{4,8},{8,12},{12,16},{16,20},{20,24},{24,28},{28,0},{1,5},{5... | collective-permute-start | bytes 393224 | tf_op jit(solution)/shard_map/ppermute | solution.py:333
  4.6 4.1 %hold.1 = (bf16[2048,2048]{1,0:T(8,128)(2,1)S(1)}, bf16[2048,2048]{1,0:T(8,128)(2,1)S(1)}) custom-call(bf16[2048,2048]{1,0:T(8,128)(2,1)} %bitcast.7), custom_call_target="tpu_custom_call" | custom-call | bytes 8388608 | tf_op jit(solution)/shard_map/hold/pallas_call | solution.py:62
  8.8 2.3 %collective-permute-done.prior = bf16[32,2048]{1,0:T(8,128)(2,1)S(1)} collective-permute-done((bf16[32,2048]{1,0:T(8,128)(2,1)S(1)}, bf16[32,2048]{1,0:T(8,128)(2,1)S(1)}, u32[]{:S(2)}, u32[]{:S(2)}) %collective-permute-start) | collective-permute-done | bytes 131104 | tf_op jit(solution)/shard_map/ppermute | solution.py:333
  11.2 1.6 %first.3 = (f32[32,1280]{1,0:T(8,128)S(1)}, f32[32,1280]{1,0:T(8,128)S(1)}) custom-call(s32[2]{0:T(128)S(1)} %pad_add_fusion.place, bf16[32,2048]{1,0:T(8,128)(2,1)S(1)} %convert_bitcast_fusion.own, bf16[32,2048]{1,0:T(8,128)(2,1)S(1)} %collective-permute-done.prior, bf16[2048,2048]{1,0:T(8,128)(2,1)S(1)} %get-tuple-element.51.turned.refs_2_), custom_call_target="tpu_custom_call" | custom-call | flops 268435456 | bytes 4194304 | tf_op jit(solution)/shard_map/first/pallas_call | solution.py:30
  12.8 3.1 %collective-permute-start.4 = (f32[32,1280]{1,0:T(8,128)S(1)}, f32[32,1280]{1,0:T(8,128)S(1)}, u32[]{:S(2)}, u32[]{:S(2)}) collective-permute-start(f32[32,1280]{1,0:T(8,128)S(1)} %get-tuple-element.55.refs_1_), channel_id=1, source_target_pairs={{0,28},{4,8},{8,4},{12,16},{16,12},{20,24},{24,20},{28,0},{1,29},{... | collective-permute-start | bytes 491528 | tf_op jit(solution)/shard_map/ppermute | solution.py:329
  17.2 1.9 %collective-permute-start.2 = (f32[32,768]{1,0:T(8,128)S(1)}, f32[32,768]{1,0:T(8,128)S(1)}, u32[]{:S(2)}, u32[]{:S(2)}) collective-permute-start(f32[32,768]{1,0:T(8,128)S(1)} %get-tuple-element.53.refs_1_), channel_id=1, source_target_pairs={{0,28},{4,8},{8,4},{12,16},{16,12},{20,24},{24,20},{28,0},{1,29},{... | collective-permute-start | bytes 294920 | tf_op jit(solution)/shard_map/ppermute | solution.py:329
  19.1 4.2 %collective-permute-done.3.refs_2_ = f32[32,1280]{1,0:T(8,128)S(1)} collective-permute-done((f32[32,1280]{1,0:T(8,128)S(1)}, f32[32,1280]{1,0:T(8,128)S(1)}, u32[]{:S(2)}, u32[]{:S(2)}) %collective-permute-start.3) | collective-permute-done | bytes 163872 | tf_op jit(solution)/shard_map/ppermute | solution.py:329
  29.1 2.8 %collective-permute-start.8 = (f32[32,1024]{1,0:T(8,128)S(1)}, f32[32,1024]{1,0:T(8,128)S(1)}, u32[]{:S(2)}, u32[]{:S(2)}) collective-permute-start(f32[32,1024]{1,0:T(8,128)S(1)} %get-tuple-element.63.odd), channel_id=1, source_target_pairs={{0,28},{4,8},{8,4},{12,16},{16,12},{20,24},{24,20},{28,0},{1,29},{... | collective-permute-start | bytes 393224 | tf_op jit(solution)/shard_map/ppermute | solution.py:329
  33.3 2.4 %collective-permute-done.6.came = f32[64,128]{1,0:T(8,128)S(1)} collective-permute-done((f32[64,128]{1,0:T(8,128)S(1)}, f32[64,128]{1,0:T(8,128)S(1)}, u32[]{:S(2)}, u32[]{:S(2)}) %collective-permute-start.6) | collective-permute-done | bytes 32800 | tf_op jit(solution)/shard_map/ppermute | solution.py:326
  38.9 3.5 %collective-permute-done.9.came = bf16[64,1024]{1,0:T(8,128)(2,1)S(1)} collective-permute-done((bf16[64,1024]{1,0:T(8,128)(2,1)S(1)}, bf16[64,1024]{1,0:T(8,128)(2,1)S(1)}, u32[]{:S(2)}, u32[]{:S(2)}) %collective-permute-start.9) | collective-permute-done | bytes 131104 | tf_op jit(solution)/shard_map/ppermute | solution.py:326
  45.5 2.8 %collective-permute-start.14 = (f32[32,1280]{1,0:T(8,128)S(1)}, f32[32,1280]{1,0:T(8,128)S(1)}, u32[]{:S(2)}, u32[]{:S(2)}) collective-permute-start(f32[32,1280]{1,0:T(8,128)S(1)} %get-tuple-element.67.refs_1_), channel_id=1, source_target_pairs={{0,28},{4,8},{8,4},{12,16},{16,12},{20,24},{24,20},{28,0},{1,29},{... | collective-permute-start | bytes 491528 | tf_op jit(solution)/shard_map/ppermute | solution.py:329
  49.3 2.0 %collective-permute-start.12 = (f32[32,768]{1,0:T(8,128)S(1)}, f32[32,768]{1,0:T(8,128)S(1)}, u32[]{:S(2)}, u32[]{:S(2)}) collective-permute-start(f32[32,768]{1,0:T(8,128)S(1)} %get-tuple-element.65.refs_1_), channel_id=1, source_target_pairs={{0,28},{4,8},{8,4},{12,16},{16,12},{20,24},{24,20},{28,0},{1,29},{... | collective-permute-start | bytes 294920 | tf_op jit(solution)/shard_map/ppermute | solution.py:329
  51.3 6.5 %collective-permute-done.13.refs_2_ = f32[32,1280]{1,0:T(8,128)S(1)} collective-permute-done((f32[32,1280]{1,0:T(8,128)S(1)}, f32[32,1280]{1,0:T(8,128)S(1)}, u32[]{:S(2)}, u32[]{:S(2)}) %collective-permute-start.13) | collective-permute-done | bytes 163872 | tf_op jit(solution)/shard_map/ppermute | solution.py:329
  62.7 2.8 %collective-permute-start.18 = (f32[32,1024]{1,0:T(8,128)S(1)}, f32[32,1024]{1,0:T(8,128)S(1)}, u32[]{:S(2)}, u32[]{:S(2)}) collective-permute-start(f32[32,1024]{1,0:T(8,128)S(1)} %get-tuple-element.74.odd), channel_id=1, source_target_pairs={{0,28},{4,8},{8,4},{12,16},{16,12},{20,24},{24,20},{28,0},{1,29},{... | collective-permute-start | bytes 393224 | tf_op jit(solution)/shard_map/ppermute | solution.py:329
  67.0 2.4 %collective-permute-done.16.came = f32[64,128]{1,0:T(8,128)S(1)} collective-permute-done((f32[64,128]{1,0:T(8,128)S(1)}, f32[64,128]{1,0:T(8,128)S(1)}, u32[]{:S(2)}, u32[]{:S(2)}) %collective-permute-start.16) | collective-permute-done | bytes 32800 | tf_op jit(solution)/shard_map/ppermute | solution.py:326
  72.6 3.5 %collective-permute-done.19.came = bf16[64,1024]{1,0:T(8,128)(2,1)S(1)} collective-permute-done((bf16[64,1024]{1,0:T(8,128)(2,1)S(1)}, bf16[64,1024]{1,0:T(8,128)(2,1)S(1)}, u32[]{:S(2)}, u32[]{:S(2)}) %collective-permute-start.19) | collective-permute-done | bytes 131104 | tf_op jit(solution)/shard_map/ppermute | solution.py:326
  79.1 2.8 %collective-permute-start.24 = (f32[32,1280]{1,0:T(8,128)S(1)}, f32[32,1280]{1,0:T(8,128)S(1)}, u32[]{:S(2)}, u32[]{:S(2)}) collective-permute-start(f32[32,1280]{1,0:T(8,128)S(1)} %get-tuple-element.78.refs_1_), channel_id=1, source_target_pairs={{0,28},{4,8},{8,4},{12,16},{16,12},{20,24},{24,20},{28,0},{1,29},{... | collective-permute-start | bytes 491528 | tf_op jit(solution)/shard_map/ppermute | solution.py:329
  83.1 2.0 %collective-permute-start.22 = (f32[32,768]{1,0:T(8,128)S(1)}, f32[32,768]{1,0:T(8,128)S(1)}, u32[]{:S(2)}, u32[]{:S(2)}) collective-permute-start(f32[32,768]{1,0:T(8,128)S(1)} %get-tuple-element.76.refs_1_), channel_id=1, source_target_pairs={{0,28},{4,8},{8,4},{12,16},{16,12},{20,24},{24,20},{28,0},{1,29},{... | collective-permute-start | bytes 294920 | tf_op jit(solution)/shard_map/ppermute | solution.py:329
  85.1 6.3 %collective-permute-done.23.refs_2_ = f32[32,1280]{1,0:T(8,128)S(1)} collective-permute-done((f32[32,1280]{1,0:T(8,128)S(1)}, f32[32,1280]{1,0:T(8,128)S(1)}, u32[]{:S(2)}, u32[]{:S(2)}) %collective-permute-start.23) | collective-permute-done | bytes 163872 | tf_op jit(solution)/shard_map/ppermute | solution.py:329
  96.3 2.8 %collective-permute-start.28 = (f32[32,1024]{1,0:T(8,128)S(1)}, f32[32,1024]{1,0:T(8,128)S(1)}, u32[]{:S(2)}, u32[]{:S(2)}) collective-permute-start(f32[32,1024]{1,0:T(8,128)S(1)} %get-tuple-element.85.odd), channel_id=1, source_target_pairs={{0,28},{4,8},{8,4},{12,16},{16,12},{20,24},{24,20},{28,0},{1,29},{... | collective-permute-start | bytes 393224 | tf_op jit(solution)/shard_map/ppermute | solution.py:329
  99.1 1.5 %collective-permute-start.26 = (f32[64,128]{1,0:T(8,128)S(1)}, f32[64,128]{1,0:T(8,128)S(1)}, u32[]{:S(2)}, u32[]{:S(2)}) collective-permute-start(f32[64,128]{1,0:T(8,128)S(1)} %get-tuple-element.83.gram), channel_id=1, source_target_pairs={{0,2},{1,3},{2,0},{3,1},{4,6},{5,7},{6,4},{7,5},{8,10},{9,11},{10,... | collective-permute-start | bytes 98312 | tf_op jit(solution)/shard_map/ppermute | solution.py:326
  100.6 2.4 %collective-permute-done.26.came = f32[64,128]{1,0:T(8,128)S(1)} collective-permute-done((f32[64,128]{1,0:T(8,128)S(1)}, f32[64,128]{1,0:T(8,128)S(1)}, u32[]{:S(2)}, u32[]{:S(2)}) %collective-permute-start.26) | collective-permute-done | bytes 32800 | tf_op jit(solution)/shard_map/ppermute | solution.py:326
  106.2 3.5 %collective-permute-done.29.came = bf16[64,1024]{1,0:T(8,128)(2,1)S(1)} collective-permute-done((bf16[64,1024]{1,0:T(8,128)(2,1)S(1)}, bf16[64,1024]{1,0:T(8,128)(2,1)S(1)}, u32[]{:S(2)}, u32[]{:S(2)}) %collective-permute-start.29) | collective-permute-done | bytes 131104 | tf_op jit(solution)/shard_map/ppermute | solution.py:326
  112.7 2.8 %collective-permute-start.34 = (f32[32,1280]{1,0:T(8,128)S(1)}, f32[32,1280]{1,0:T(8,128)S(1)}, u32[]{:S(2)}, u32[]{:S(2)}) collective-permute-start(f32[32,1280]{1,0:T(8,128)S(1)} %get-tuple-element.89.refs_1_), channel_id=1, source_target_pairs={{0,28},{4,8},{8,4},{12,16},{16,12},{20,24},{24,20},{28,0},{1,29},{... | collective-permute-start | bytes 491528 | tf_op jit(solution)/shard_map/ppermute | solution.py:329
  116.6 2.0 %collective-permute-start.32 = (f32[32,768]{1,0:T(8,128)S(1)}, f32[32,768]{1,0:T(8,128)S(1)}, u32[]{:S(2)}, u32[]{:S(2)}) collective-permute-start(f32[32,768]{1,0:T(8,128)S(1)} %get-tuple-element.87.refs_1_), channel_id=1, source_target_pairs={{0,28},{4,8},{8,4},{12,16},{16,12},{20,24},{24,20},{28,0},{1,29},{... | collective-permute-start | bytes 294920 | tf_op jit(solution)/shard_map/ppermute | solution.py:329
  118.6 6.5 %collective-permute-done.33.refs_2_ = f32[32,1280]{1,0:T(8,128)S(1)} collective-permute-done((f32[32,1280]{1,0:T(8,128)S(1)}, f32[32,1280]{1,0:T(8,128)S(1)}, u32[]{:S(2)}, u32[]{:S(2)}) %collective-permute-start.33) | collective-permute-done | bytes 163872 | tf_op jit(solution)/shard_map/ppermute | solution.py:329
  129.9 2.8 %collective-permute-start.38 = (f32[32,1024]{1,0:T(8,128)S(1)}, f32[32,1024]{1,0:T(8,128)S(1)}, u32[]{:S(2)}, u32[]{:S(2)}) collective-permute-start(f32[32,1024]{1,0:T(8,128)S(1)} %get-tuple-element.97.odd), channel_id=1, source_target_pairs={{0,28},{4,8},{8,4},{12,16},{16,12},{20,24},{24,20},{28,0},{1,29},{... | collective-permute-start | bytes 393224 | tf_op jit(solution)/shard_map/ppermute | solution.py:329
  132.7 1.5 %collective-permute-start.36 = (f32[64,128]{1,0:T(8,128)S(1)}, f32[64,128]{1,0:T(8,128)S(1)}, u32[]{:S(2)}, u32[]{:S(2)}) collective-permute-start(f32[64,128]{1,0:T(8,128)S(1)} %get-tuple-element.94.gram), channel_id=1, source_target_pairs={{0,2},{1,3},{2,0},{3,1},{4,6},{5,7},{6,4},{7,5},{8,10},{9,11},{10,... | collective-permute-start | bytes 98312 | tf_op jit(solution)/shard_map/ppermute | solution.py:326
  134.2 2.4 %collective-permute-done.36.came = f32[64,128]{1,0:T(8,128)S(1)} collective-permute-done((f32[64,128]{1,0:T(8,128)S(1)}, f32[64,128]{1,0:T(8,128)S(1)}, u32[]{:S(2)}, u32[]{:S(2)}) %collective-permute-start.36) | collective-permute-done | bytes 32800 | tf_op jit(solution)/shard_map/ppermute | solution.py:326
  141.2 2.1 %collective-permute-done.39.came.refs_3_ = bf16[64,1024]{1,0:T(8,128)(2,1)S(1)} collective-permute-done((bf16[64,1024]{1,0:T(8,128)(2,1)S(1)}, bf16[64,1024]{1,0:T(8,128)(2,1)S(1)}, u32[]{:S(2)}, u32[]{:S(2)}) %collective-permute-start.39) | collective-permute-done | bytes 131104 | tf_op jit(solution)/shard_map/ppermute | solution.py:326
  143.4 1.8 %update_own.1.refs_1_ = bf16[2,2048,512]{2,1,0:T(8,128)(2,1)S(1)} custom-call(s32[2]{0:T(128)S(1)} %pad_add_fusion.place, bf16[2048,64]{1,0:T(8,128)(2,1)S(1)} %basis.1.refs_0_.columns, bf16[64,1024]{1,0:T(8,128)(2,1)S(1)} %blend.7.piece, bf16[2048,2048]{1,0:T(8,128)(2,1)S(1)} %get-tuple-element.56.refs_4_.refs_6_.weight), custom_call_target="tpu_custom_call" | custom-call | flops 268435456 | bytes 6291456 | tf_op jit(solution)/shard_map/update_own/pallas_call | solution.py:30
  145.2 3.9 %update.1 = (bf16[2048,2048]{1,0:T(8,128)(2,1)}, f32[32,512]{1,0:T(8,128)}) custom-call(s32[2]{0:T(128)S(1)} %pad_add_fusion.place, bf16[2048,64]{1,0:T(8,128)(2,1)S(1)} %basis.1.refs_0_.columns, bf16[64,1024]{1,0:T(8,128)(2,1)S(1)} %collective-permute-done.40.refs_0_, bf16[2,2048,512]{2,1,0:T(8,128)(2,1)S(1)} %update_own.1.refs_1_, ...), custom_call_target="tpu_custom_call" | custom-call | flops 536870912 | bytes 8388608 | tf_op jit(solution)/shard_map/update/pallas_call | solution.py:438
  (96 shorter events, 52.0 us)
Async XLA Ops:
  1.6 9.6 %collective-permute-start = (bf16[32,2048]{1,0:T(8,128)(2,1)S(1)}, bf16[32,2048]{1,0:T(8,128)(2,1)S(1)}, u32[]{:S(2)}, u32[]{:S(2)}) collective-permute-start(bf16[32,2048]{1,0:T(8,128)(2,1)S(1)} %convert_bitcast_fusion.own), channel_id=1, source_target_pairs={{0,4},{4,8},{8,12},{12,16},{16,20},{20,24},{24,28},{28,0},{1,5},{5... | collective-permute-start | bytes 393224 | tf_op jit(solution)/shard_map/ppermute | solution.py:333
  12.7 10.6 %collective-permute-start.3 = (f32[32,1280]{1,0:T(8,128)S(1)}, f32[32,1280]{1,0:T(8,128)S(1)}, u32[]{:S(2)}, u32[]{:S(2)}) collective-permute-start(f32[32,1280]{1,0:T(8,128)S(1)} %get-tuple-element.54.refs_0_), channel_id=1, source_target_pairs={{0,4},{4,0},{8,12},{12,8},{16,20},{20,16},{24,28},{28,24},{1,5},{5... | collective-permute-start | bytes 491528 | tf_op jit(solution)/shard_map/ppermute | solution.py:329
  12.8 10.5 %collective-permute-start.4 = (f32[32,1280]{1,0:T(8,128)S(1)}, f32[32,1280]{1,0:T(8,128)S(1)}, u32[]{:S(2)}, u32[]{:S(2)}) collective-permute-start(f32[32,1280]{1,0:T(8,128)S(1)} %get-tuple-element.55.refs_1_), channel_id=1, source_target_pairs={{0,28},{4,8},{8,4},{12,16},{16,12},{20,24},{24,20},{28,0},{1,29},{... | collective-permute-start | bytes 491528 | tf_op jit(solution)/shard_map/ppermute | solution.py:329
  17.2 8.7 %collective-permute-start.1 = (f32[32,768]{1,0:T(8,128)S(1)}, f32[32,768]{1,0:T(8,128)S(1)}, u32[]{:S(2)}, u32[]{:S(2)}) collective-permute-start(f32[32,768]{1,0:T(8,128)S(1)} %get-tuple-element.52.refs_0_), channel_id=1, source_target_pairs={{0,4},{4,0},{8,12},{12,8},{16,20},{20,16},{24,28},{28,24},{1,5},{5... | collective-permute-start | bytes 294920 | tf_op jit(solution)/shard_map/ppermute | solution.py:329
  17.2 8.7 %collective-permute-start.2 = (f32[32,768]{1,0:T(8,128)S(1)}, f32[32,768]{1,0:T(8,128)S(1)}, u32[]{:S(2)}, u32[]{:S(2)}) collective-permute-start(f32[32,768]{1,0:T(8,128)S(1)} %get-tuple-element.53.refs_1_), channel_id=1, source_target_pairs={{0,28},{4,8},{8,4},{12,16},{16,12},{20,24},{24,20},{28,0},{1,29},{... | collective-permute-start | bytes 294920 | tf_op jit(solution)/shard_map/ppermute | solution.py:329
  28.7 8.2 %collective-permute-start.7 = (f32[32,1024]{1,0:T(8,128)S(1)}, f32[32,1024]{1,0:T(8,128)S(1)}, u32[]{:S(2)}, u32[]{:S(2)}) collective-permute-start(f32[32,1024]{1,0:T(8,128)S(1)} %get-tuple-element.62.even), channel_id=1, source_target_pairs={{0,4},{4,0},{8,12},{12,8},{16,20},{20,16},{24,28},{28,24},{1,5},{5... | collective-permute-start | bytes 393224 | tf_op jit(solution)/shard_map/ppermute | solution.py:329
  29.1 8.0 %collective-permute-start.8 = (f32[32,1024]{1,0:T(8,128)S(1)}, f32[32,1024]{1,0:T(8,128)S(1)}, u32[]{:S(2)}, u32[]{:S(2)}) collective-permute-start(f32[32,1024]{1,0:T(8,128)S(1)} %get-tuple-element.63.odd), channel_id=1, source_target_pairs={{0,28},{4,8},{8,4},{12,16},{16,12},{20,24},{24,20},{28,0},{1,29},{... | collective-permute-start | bytes 393224 | tf_op jit(solution)/shard_map/ppermute | solution.py:329
  31.8 3.9 %collective-permute-start.6 = (f32[64,128]{1,0:T(8,128)S(1)}, f32[64,128]{1,0:T(8,128)S(1)}, u32[]{:S(2)}, u32[]{:S(2)}) collective-permute-start(f32[64,128]{1,0:T(8,128)S(1)} %get-tuple-element.61.gram), channel_id=1, source_target_pairs={{0,2},{1,3},{2,0},{3,1},{4,6},{5,7},{6,4},{7,5},{8,10},{9,11},{10,... | collective-permute-start | bytes 98312 | tf_op jit(solution)/shard_map/ppermute | solution.py:326
  37.5 5.0 %collective-permute-start.9 = (bf16[64,1024]{1,0:T(8,128)(2,1)S(1)}, bf16[64,1024]{1,0:T(8,128)(2,1)S(1)}, u32[]{:S(2)}, u32[]{:S(2)}) collective-permute-start(bf16[64,1024]{1,0:T(8,128)(2,1)S(1)} %share.4), channel_id=1, source_target_pairs={{0,2},{1,3},{2,0},{3,1},{4,6},{5,7},{6,4},{7,5},{8,10},{9,11},{10,... | collective-permute-start | bytes 393224 | tf_op jit(solution)/shard_map/ppermute | solution.py:326
  45.1 12.7 %collective-permute-start.13 = (f32[32,1280]{1,0:T(8,128)S(1)}, f32[32,1280]{1,0:T(8,128)S(1)}, u32[]{:S(2)}, u32[]{:S(2)}) collective-permute-start(f32[32,1280]{1,0:T(8,128)S(1)} %get-tuple-element.66.refs_0_), channel_id=1, source_target_pairs={{0,4},{4,0},{8,12},{12,8},{16,20},{20,16},{24,28},{28,24},{1,5},{5... | collective-permute-start | bytes 491528 | tf_op jit(solution)/shard_map/ppermute | solution.py:329
  45.5 12.3 %collective-permute-start.14 = (f32[32,1280]{1,0:T(8,128)S(1)}, f32[32,1280]{1,0:T(8,128)S(1)}, u32[]{:S(2)}, u32[]{:S(2)}) collective-permute-start(f32[32,1280]{1,0:T(8,128)S(1)} %get-tuple-element.67.refs_1_), channel_id=1, source_target_pairs={{0,28},{4,8},{8,4},{12,16},{16,12},{20,24},{24,20},{28,0},{1,29},{... | collective-permute-start | bytes 491528 | tf_op jit(solution)/shard_map/ppermute | solution.py:329
  49.2 10.3 %collective-permute-start.11 = (f32[32,768]{1,0:T(8,128)S(1)}, f32[32,768]{1,0:T(8,128)S(1)}, u32[]{:S(2)}, u32[]{:S(2)}) collective-permute-start(f32[32,768]{1,0:T(8,128)S(1)} %get-tuple-element.64.refs_0_), channel_id=1, source_target_pairs={{0,4},{4,0},{8,12},{12,8},{16,20},{20,16},{24,28},{28,24},{1,5},{5... | collective-permute-start | bytes 294920 | tf_op jit(solution)/shard_map/ppermute | solution.py:329
  49.3 10.2 %collective-permute-start.12 = (f32[32,768]{1,0:T(8,128)S(1)}, f32[32,768]{1,0:T(8,128)S(1)}, u32[]{:S(2)}, u32[]{:S(2)}) collective-permute-start(f32[32,768]{1,0:T(8,128)S(1)} %get-tuple-element.65.refs_1_), channel_id=1, source_target_pairs={{0,28},{4,8},{8,4},{12,16},{16,12},{20,24},{24,20},{28,0},{1,29},{... | collective-permute-start | bytes 294920 | tf_op jit(solution)/shard_map/ppermute | solution.py:329
  62.3 8.2 %collective-permute-start.17 = (f32[32,1024]{1,0:T(8,128)S(1)}, f32[32,1024]{1,0:T(8,128)S(1)}, u32[]{:S(2)}, u32[]{:S(2)}) collective-permute-start(f32[32,1024]{1,0:T(8,128)S(1)} %get-tuple-element.73.even), channel_id=1, source_target_pairs={{0,4},{4,0},{8,12},{12,8},{16,20},{20,16},{24,28},{28,24},{1,5},{5... | collective-permute-start | bytes 393224 | tf_op jit(solution)/shard_map/ppermute | solution.py:329
  62.7 8.0 %collective-permute-start.18 = (f32[32,1024]{1,0:T(8,128)S(1)}, f32[32,1024]{1,0:T(8,128)S(1)}, u32[]{:S(2)}, u32[]{:S(2)}) collective-permute-start(f32[32,1024]{1,0:T(8,128)S(1)} %get-tuple-element.74.odd), channel_id=1, source_target_pairs={{0,28},{4,8},{8,4},{12,16},{16,12},{20,24},{24,20},{28,0},{1,29},{... | collective-permute-start | bytes 393224 | tf_op jit(solution)/shard_map/ppermute | solution.py:329
  65.5 3.9 %collective-permute-start.16 = (f32[64,128]{1,0:T(8,128)S(1)}, f32[64,128]{1,0:T(8,128)S(1)}, u32[]{:S(2)}, u32[]{:S(2)}) collective-permute-start(f32[64,128]{1,0:T(8,128)S(1)} %get-tuple-element.72.gram), channel_id=1, source_target_pairs={{0,2},{1,3},{2,0},{3,1},{4,6},{5,7},{6,4},{7,5},{8,10},{9,11},{10,... | collective-permute-start | bytes 98312 | tf_op jit(solution)/shard_map/ppermute | solution.py:326
  71.1 5.0 %collective-permute-start.19 = (bf16[64,1024]{1,0:T(8,128)(2,1)S(1)}, bf16[64,1024]{1,0:T(8,128)(2,1)S(1)}, u32[]{:S(2)}, u32[]{:S(2)}) collective-permute-start(bf16[64,1024]{1,0:T(8,128)(2,1)S(1)} %share.5), channel_id=1, source_target_pairs={{0,2},{1,3},{2,0},{3,1},{4,6},{5,7},{6,4},{7,5},{8,10},{9,11},{10,... | collective-permute-start | bytes 393224 | tf_op jit(solution)/shard_map/ppermute | solution.py:326
  78.8 12.7 %collective-permute-start.23 = (f32[32,1280]{1,0:T(8,128)S(1)}, f32[32,1280]{1,0:T(8,128)S(1)}, u32[]{:S(2)}, u32[]{:S(2)}) collective-permute-start(f32[32,1280]{1,0:T(8,128)S(1)} %get-tuple-element.77.refs_0_), channel_id=1, source_target_pairs={{0,4},{4,0},{8,12},{12,8},{16,20},{20,16},{24,28},{28,24},{1,5},{5... | collective-permute-start | bytes 491528 | tf_op jit(solution)/shard_map/ppermute | solution.py:329
  79.1 12.3 %collective-permute-start.24 = (f32[32,1280]{1,0:T(8,128)S(1)}, f32[32,1280]{1,0:T(8,128)S(1)}, u32[]{:S(2)}, u32[]{:S(2)}) collective-permute-start(f32[32,1280]{1,0:T(8,128)S(1)} %get-tuple-element.78.refs_1_), channel_id=1, source_target_pairs={{0,28},{4,8},{8,4},{12,16},{16,12},{20,24},{24,20},{28,0},{1,29},{... | collective-permute-start | bytes 491528 | tf_op jit(solution)/shard_map/ppermute | solution.py:329
  83.0 10.1 %collective-permute-start.21 = (f32[32,768]{1,0:T(8,128)S(1)}, f32[32,768]{1,0:T(8,128)S(1)}, u32[]{:S(2)}, u32[]{:S(2)}) collective-permute-start(f32[32,768]{1,0:T(8,128)S(1)} %get-tuple-element.75.refs_0_), channel_id=1, source_target_pairs={{0,4},{4,0},{8,12},{12,8},{16,20},{20,16},{24,28},{28,24},{1,5},{5... | collective-permute-start | bytes 294920 | tf_op jit(solution)/shard_map/ppermute | solution.py:329
  83.1 10.0 %collective-permute-start.22 = (f32[32,768]{1,0:T(8,128)S(1)}, f32[32,768]{1,0:T(8,128)S(1)}, u32[]{:S(2)}, u32[]{:S(2)}) collective-permute-start(f32[32,768]{1,0:T(8,128)S(1)} %get-tuple-element.76.refs_1_), channel_id=1, source_target_pairs={{0,28},{4,8},{8,4},{12,16},{16,12},{20,24},{24,20},{28,0},{1,29},{... | collective-permute-start | bytes 294920 | tf_op jit(solution)/shard_map/ppermute | solution.py:329
  95.9 8.2 %collective-permute-start.27 = (f32[32,1024]{1,0:T(8,128)S(1)}, f32[32,1024]{1,0:T(8,128)S(1)}, u32[]{:S(2)}, u32[]{:S(2)}) collective-permute-start(f32[32,1024]{1,0:T(8,128)S(1)} %get-tuple-element.84.even), channel_id=1, source_target_pairs={{0,4},{4,0},{8,12},{12,8},{16,20},{20,16},{24,28},{28,24},{1,5},{5... | collective-permute-start | bytes 393224 | tf_op jit(solution)/shard_map/ppermute | solution.py:329
  96.3 8.0 %collective-permute-start.28 = (f32[32,1024]{1,0:T(8,128)S(1)}, f32[32,1024]{1,0:T(8,128)S(1)}, u32[]{:S(2)}, u32[]{:S(2)}) collective-permute-start(f32[32,1024]{1,0:T(8,128)S(1)} %get-tuple-element.85.odd), channel_id=1, source_target_pairs={{0,28},{4,8},{8,4},{12,16},{16,12},{20,24},{24,20},{28,0},{1,29},{... | collective-permute-start | bytes 393224 | tf_op jit(solution)/shard_map/ppermute | solution.py:329
  99.1 3.9 %collective-permute-start.26 = (f32[64,128]{1,0:T(8,128)S(1)}, f32[64,128]{1,0:T(8,128)S(1)}, u32[]{:S(2)}, u32[]{:S(2)}) collective-permute-start(f32[64,128]{1,0:T(8,128)S(1)} %get-tuple-element.83.gram), channel_id=1, source_target_pairs={{0,2},{1,3},{2,0},{3,1},{4,6},{5,7},{6,4},{7,5},{8,10},{9,11},{10,... | collective-permute-start | bytes 98312 | tf_op jit(solution)/shard_map/ppermute | solution.py:326
  104.7 5.0 %collective-permute-start.29 = (bf16[64,1024]{1,0:T(8,128)(2,1)S(1)}, bf16[64,1024]{1,0:T(8,128)(2,1)S(1)}, u32[]{:S(2)}, u32[]{:S(2)}) collective-permute-start(bf16[64,1024]{1,0:T(8,128)(2,1)S(1)} %share.6), channel_id=1, source_target_pairs={{0,2},{1,3},{2,0},{3,1},{4,6},{5,7},{6,4},{7,5},{8,10},{9,11},{10,... | collective-permute-start | bytes 393224 | tf_op jit(solution)/shard_map/ppermute | solution.py:326
  112.4 12.7 %collective-permute-start.33 = (f32[32,1280]{1,0:T(8,128)S(1)}, f32[32,1280]{1,0:T(8,128)S(1)}, u32[]{:S(2)}, u32[]{:S(2)}) collective-permute-start(f32[32,1280]{1,0:T(8,128)S(1)} %get-tuple-element.88.refs_0_), channel_id=1, source_target_pairs={{0,4},{4,0},{8,12},{12,8},{16,20},{20,16},{24,28},{28,24},{1,5},{5... | collective-permute-start | bytes 491528 | tf_op jit(solution)/shard_map/ppermute | solution.py:329
  112.7 12.3 %collective-permute-start.34 = (f32[32,1280]{1,0:T(8,128)S(1)}, f32[32,1280]{1,0:T(8,128)S(1)}, u32[]{:S(2)}, u32[]{:S(2)}) collective-permute-start(f32[32,1280]{1,0:T(8,128)S(1)} %get-tuple-element.89.refs_1_), channel_id=1, source_target_pairs={{0,28},{4,8},{8,4},{12,16},{16,12},{20,24},{24,20},{28,0},{1,29},{... | collective-permute-start | bytes 491528 | tf_op jit(solution)/shard_map/ppermute | solution.py:329
  116.5 10.3 %collective-permute-start.31 = (f32[32,768]{1,0:T(8,128)S(1)}, f32[32,768]{1,0:T(8,128)S(1)}, u32[]{:S(2)}, u32[]{:S(2)}) collective-permute-start(f32[32,768]{1,0:T(8,128)S(1)} %get-tuple-element.86.refs_0_), channel_id=1, source_target_pairs={{0,4},{4,0},{8,12},{12,8},{16,20},{20,16},{24,28},{28,24},{1,5},{5... | collective-permute-start | bytes 294920 | tf_op jit(solution)/shard_map/ppermute | solution.py:329
  116.6 10.2 %collective-permute-start.32 = (f32[32,768]{1,0:T(8,128)S(1)}, f32[32,768]{1,0:T(8,128)S(1)}, u32[]{:S(2)}, u32[]{:S(2)}) collective-permute-start(f32[32,768]{1,0:T(8,128)S(1)} %get-tuple-element.87.refs_1_), channel_id=1, source_target_pairs={{0,28},{4,8},{8,4},{12,16},{16,12},{20,24},{24,20},{28,0},{1,29},{... | collective-permute-start | bytes 294920 | tf_op jit(solution)/shard_map/ppermute | solution.py:329
  129.5 8.2 %collective-permute-start.37 = (f32[32,1024]{1,0:T(8,128)S(1)}, f32[32,1024]{1,0:T(8,128)S(1)}, u32[]{:S(2)}, u32[]{:S(2)}) collective-permute-start(f32[32,1024]{1,0:T(8,128)S(1)} %get-tuple-element.96.even), channel_id=1, source_target_pairs={{0,4},{4,0},{8,12},{12,8},{16,20},{20,16},{24,28},{28,24},{1,5},{5... | collective-permute-start | bytes 393224 | tf_op jit(solution)/shard_map/ppermute | solution.py:329
  129.9 8.0 %collective-permute-start.38 = (f32[32,1024]{1,0:T(8,128)S(1)}, f32[32,1024]{1,0:T(8,128)S(1)}, u32[]{:S(2)}, u32[]{:S(2)}) collective-permute-start(f32[32,1024]{1,0:T(8,128)S(1)} %get-tuple-element.97.odd), channel_id=1, source_target_pairs={{0,28},{4,8},{8,4},{12,16},{16,12},{20,24},{24,20},{28,0},{1,29},{... | collective-permute-start | bytes 393224 | tf_op jit(solution)/shard_map/ppermute | solution.py:329
  138.3 5.0 %collective-permute-start.39 = (bf16[64,1024]{1,0:T(8,128)(2,1)S(1)}, bf16[64,1024]{1,0:T(8,128)(2,1)S(1)}, u32[]{:S(2)}, u32[]{:S(2)}) collective-permute-start(bf16[64,1024]{1,0:T(8,128)(2,1)S(1)} %share.7), channel_id=1, source_target_pairs={{0,2},{1,3},{2,0},{3,1},{4,6},{5,7},{6,4},{7,5},{8,10},{9,11},{10,... | collective-permute-start | bytes 393224 | tf_op jit(solution)/shard_map/ppermute | solution.py:326
  (9 other events, 16.6 us)
